TPU v7x, 512 devices: a whole 4x8x8 slice. The times are simulated.
512 devices in a mesh: tower: 16 (over y, core), shard: 32 (over z, x).
Axes of the slice: x: 4, y: 8, z: 8, core: 2. Of those that a mesh axis runs over, the one named last changes fastest.
Arguments:
- out_grad: bfloat16 [4096, 16, 256], P(('tower', 'shard')), may hold values from -6 to 6
- hidden_pre: bfloat16 [16, 4096, 1024], P('tower', 'shard'), may hold values from -6 to 6
- down_proj: bfloat16 [16, 1024, 256], P('tower'), may hold values from -0.1875 to 0.1875
- up_proj: bfloat16 [16, 4096, 1024], P('tower'), may hold values from -0.09375 to 0.09375
- feature_slot: int32 [16, 32], P('tower'), may hold values from 0 to 31, each once within a row
- element_segment: int32 [16, 32, 5120], P('tower', 'shard'), may hold values from 0 to 4095, never falling along the last dimension, each value on 1 to 4 neighbouring positions
- element_weight: float32 [16, 32, 5120], P('tower', 'shard'), may hold values from 0.25 to 1.75
- row_owner: int32 [16, 32, 5120, 1], P('tower', 'shard'), may hold values from 0 to 31; in each aligned block of 5120 rows (0 to 5119, 5120 to 10239, ..., all dimensions but the last counted through in order) at most 320 rows name the same one
- row_local: int32 [16, 32, 5120], P('tower', 'shard'), may hold values from 0 to 511
Outputs:
- table_grad: float32 [16, 16384, 128], P('tower', 'shard')
Inputs may be any that keep to these rules, and one draw needn't show every extreme that they name: `element_segment`: segment c of a device is the jagged sequence of its sample c // 32 and feature c % 32; numbers never fall along a device's elements, each of the 4096 segments holds 1 to 4 elements and some holds 4. `row_owner`: among the 5120 elements of one device no shard is named more than 320 times, a bound that some block reaches. `feature_slot`: each tower's slots name every block once.
All inputs are finite; a program needn't handle non-finite values.
Results may differ from a plain program's by a relative error of at most 0.005.
Values may be sent and summed in bfloat16 or wider, within the bound.
No kernel may reach another device: no remote copies, remote signals or barrier semaphores. Data moves between devices by JAX's collectives and lax.ppermute only.
A program may use at most 64 MiB of HBM per device.

v0:
```python
import jax
import jax.numpy as jnp
from jax import lax
from jax.sharding import PartitionSpec as P

E = 128
FEAT = 32
ROW_DEV = 512


def element_gradients(pooled_flat, element_segment, element_weight, feature_slot):
    segment = element_segment.reshape(-1)
    local_row = segment // FEAT
    feature = segment % FEAT
    matches = feature[:, None] == jnp.arange(FEAT, dtype=jnp.int32)[None, :]
    slot_index = jnp.sum(jnp.where(matches, feature_slot, 0), axis=1)
    gathered = jnp.take(pooled_flat, local_row * FEAT + slot_index, axis=0)
    weights = element_weight.reshape(-1, 1)
    return (gathered.astype(jnp.float32) * weights).astype(jnp.bfloat16)


def owner_counts(owner_shard, shards):
    count = owner_shard.shape[0]
    owner_cols = (owner_shard[:, None] == jnp.arange(shards, dtype=jnp.int32)[None, :]).astype(
        jnp.bfloat16
    )
    block = 128
    blocks = count // block
    lower = (
        jnp.arange(block, dtype=jnp.int32)[:, None] >= jnp.arange(block, dtype=jnp.int32)[None, :]
    ).astype(jnp.bfloat16)
    within = jnp.einsum(
        "ij,kjo->kio",
        lower,
        owner_cols.reshape(blocks, block, shards),
        preferred_element_type=jnp.float32,
    )
    totals = within[:, block - 1, :]
    before = (
        jnp.arange(blocks, dtype=jnp.int32)[:, None] > jnp.arange(blocks, dtype=jnp.int32)[None, :]
    ).astype(jnp.float32)
    offsets = jnp.dot(
        before, totals, precision=lax.Precision.HIGHEST, preferred_element_type=jnp.float32
    )
    inclusive = (within + offsets[:, None, :]).reshape(count, shards)
    return inclusive.astype(jnp.int32)


def bucket_rows(elem_grads, owner_shard, local_rows, shards):
    count = owner_shard.shape[0]
    capacity = 2 * count // shards
    inclusive = owner_counts(owner_shard, shards)
    span = 512
    places = jnp.arange(capacity, dtype=jnp.int32)

    def count_step(total, piece):
        below = (piece[:, :, None] <= places[None, None, :]).astype(jnp.int32)
        return (total + jnp.sum(below, axis=0), None)

    source_index, unused = lax.scan(
        count_step,
        jnp.zeros((shards, capacity), jnp.int32),
        inclusive.reshape(count // span, span, shards),
    )
    source_index = source_index.reshape(-1)
    filled = source_index < count
    safe_index = jnp.minimum(source_index, count - 1)
    outgoing = jnp.where(
        filled[:, None], jnp.take(elem_grads, safe_index, axis=0), jnp.zeros((), jnp.bfloat16)
    )
    out_rows = jnp.where(filled, jnp.take(local_rows, safe_index, axis=0), ROW_DEV)
    return (outgoing.reshape(shards, capacity, -1), out_rows.reshape(shards, capacity))


def rows_total(grads, rows):
    row_ids = jnp.arange(ROW_DEV, dtype=jnp.int32)
    selector = (row_ids[:, None] == rows[None, :]).astype(jnp.bfloat16)
    return jnp.dot(selector, grads, preferred_element_type=jnp.float32)


def local(
    out_grad,
    hidden_pre,
    down_proj,
    up_proj,
    feature_slot,
    element_segment,
    element_weight,
    row_owner,
    row_local,
):
    arrived = lax.all_to_all(out_grad, "tower", split_axis=1, concat_axis=0, tiled=True)
    grad_rows = arrived.reshape(arrived.shape[0], arrived.shape[2])
    contract = (((1,), (1,)), ((), ()))
    backward = lax.dot_general(
        grad_rows, down_proj[0], contract, preferred_element_type=jnp.float32
    )
    hid_grad = jnp.where(hidden_pre[0] > 0, backward, 0.0).astype(jnp.bfloat16)
    pooled = lax.dot_general(
        hid_grad, up_proj[0], contract, preferred_element_type=jnp.float32
    ).astype(jnp.bfloat16)
    pooled_flat = pooled.reshape(-1, E)
    elem_grads = element_gradients(pooled_flat, element_segment, element_weight, feature_slot)
    owner_shard = row_owner.reshape(-1)
    local_rows = row_local.reshape(-1)
    shards = lax.axis_size("shard")
    outgoing, out_rows = bucket_rows(elem_grads, owner_shard, local_rows, shards)
    capacity = outgoing.shape[1]
    incoming, in_rows = (
        lax.all_to_all(outgoing, "shard", split_axis=0, concat_axis=0, tiled=True),
        lax.all_to_all(out_rows, "shard", split_axis=0, concat_axis=0, tiled=True),
    )
    turns = 8
    group_rows = shards * capacity // turns
    grad_blocks = incoming.reshape(turns, group_rows, E)
    row_blocks = in_rows.reshape(turns, group_rows)

    def add_block(total, pieces):
        return (total + rows_total(pieces[0], pieces[1]), None)

    table_grad, unused = lax.scan(
        add_block, jnp.zeros((ROW_DEV, E), jnp.float32), (grad_blocks, row_blocks)
    )
    return table_grad.reshape(1, ROW_DEV, E)


def solution(mesh):
    in_specs = (
        P(("tower", "shard"), None, None),
        P("tower", "shard", None),
        P("tower", None, None),
        P("tower", None, None),
        P("tower", None),
        P("tower", "shard", None),
        P("tower", "shard", None),
        P("tower", "shard", None, None),
        P("tower", "shard", None),
    )
    out_specs = P("tower", "shard", None)
    return jax.shard_map(local, mesh=mesh, in_specs=in_specs, out_specs=out_specs, check_vma=False)
```

profile of v0, /device:TPU:1, one launch (start us, length us, event | category | flops | bytes accessed | tf_op | source)
XLA Modules:
  0.0 253.6 jit_solution(14572083956906975009)
XLA Ops:
  0.0 1.5 copy.25
  1.6 10.2 %all-to-all-start.1 = ((bf16[8,16,256]{2,0,1:T(8,128)(2,1)}), bf16[8,16,256]{2,0,1:T(8,128)(2,1)S(1)}, u32[]{:S(2)}, u32[]{:S(2)}) async-start(bf16[8,16,256]{2,0,1:T(8,128)(2,1)} %copy.25), calls=%async_computation.1 | async-start | bytes 131072 | tf_op jit(solution)/shard_map/all_to_all | solution.py:92
  11.7 0.7 add_select_fusion
  12.5 0.8 select_reduce_fusion
  13.3 0.8 compare_and_fusion.1
  14.1 0.9 compare_select_fusion.2
  14.9 1.0 convolution_bitcast_fusion
  17.5 25.4 %while.22 = (s32[]{:T(128)}, s32[32,320]{1,0:T(8,128)S(1)}, s32[10,512,32]{1,0,2:T(8,128)S(1)}, s32[]{:T(128)}, s32[]{:T(128)}) while((s32[]{:T(128)}, s32[32,320]{1,0:T(8,128)S(1)}, s32[10,512,32]{1,0,2:T(8,128)S(1)}, s32[]{:T(128)}, s32[]{:T(128)}) %tuple.44), condition=%wide.region_2.3_spmd.clone, body=%wide.region_0.2_spmd.clone.sunk | while | flops 15738883 | bytes 491595 | solution.py:60
  17.6 2.4 convert_reduce_fusion.2
  20.1 2.4 convert_reduce_fusion.2
  22.6 2.4 convert_reduce_fusion.2
  25.2 2.4 convert_reduce_fusion.2
  27.7 2.4 convert_reduce_fusion.2
  30.3 2.4 convert_reduce_fusion.2
  32.8 2.4 convert_reduce_fusion.2
  35.4 2.4 convert_reduce_fusion.2
  37.9 2.4 convert_reduce_fusion.2
  40.5 2.4 convert_reduce_fusion.2
  43.1 56.8 %gather_fusion = s32[10240]{0:T(1024)S(1)} fusion(s32[5120]{0:T(1024)S(1)} %bitcast.63, s32[10240]{0:T(1024)S(1)} %broadcast_clamp_fusion), kind=kCustom, calls=%fused_computation | custom fusion | bytes 122880 | tf_op jit(solution)/shard_map/jit(_take)/gather | solution.py:71
  100.0 0.7 all_to_all.20
  100.7 11.4 %all-to-all-start = ((s32[32,1,320]{2,1,0:T(1,128)}), s32[32,1,320]{2,1,0:T(1,128)S(1)}, u32[]{:S(2)}, u32[]{:S(2)}) async-start(s32[32,1,320]{2,1,0:T(1,128)} %all_to_all.20), calls=%async_computation | async-start | bytes 98304 | tf_op jit(solution)/shard_map/all_to_all | solution.py:111
  112.1 6.4 %fusion.10 = bf16[128,4096]{1,0:T(8,128)(2,1)S(1)} fusion(bf16[1,4096,1024]{2,1,0:T(8,128)(2,1)} %param.16, bf16[1,1024,256]{2,1,0:T(8,128)(2,1)S(1)} %copy-done, bf16[1,128,1024]{2,1,0:T(8,128)(2,1)S(1)} %copy-done.2, bf16[8,16,256]{2,0,1:T(8,128)(2,1)S(1)} %all-to-all-done.1), kind=kOutput, calls=%fused_computation.19 | convolution fusion | flops 1141768192 | bytes 10289152 | tf_op jit(solution)/shard_map/dot_general | solution.py:99
  119.1 15.1 %gather_fusion.1 = bf16[5120,128]{1,0:T(8,128)(2,1)S(1)} fusion(bf16[4096,128]{1,0:T(8,128)(2,1)S(1)} %reshape.215, s32[5120]{0:T(1024)S(1)} %broadcast_clamp_fusion.1), kind=kCustom, calls=%fused_computation.1 | custom fusion | bytes 2641920 | tf_op jit(solution)/shard_map/jit(_take)/gather | solution.py:17
  134.2 1.7 multiply_convert_fusion
  136.0 36.4 %gather_fusion.2 = bf16[10240,128]{1,0:T(8,128)(2,1)} fusion(bf16[5120,128]{1,0:T(8,128)(2,1)S(1)} %multiply_convert_fusion, s32[10240]{0:T(1024)S(1)} %broadcast_clamp_fusion), kind=kCustom, calls=%fused_computation.2 | custom fusion | bytes 5283840 | tf_op jit(solution)/shard_map/jit(_take)/gather | solution.py:69
  172.4 6.2 %select_select_fusion = bf16[32,320,128]{2,1,0:T(8,128)(2,1)} fusion(bf16[32,320,128]{2,1,0:T(8,128)(2,1)} %bitcast.64, pred[32,320]{1,0:T(8,128)(4,1)S(1)} %get-tuple-element.104, pred[32,320]{1,0:T(8,128)(4,1)S(1)} %get-tuple-element.105), kind=kLoop, calls=%fused_computation.20 | loop fusion | flops 2621440 | bytes 5263360 | tf_op jit(solution)/shard_map/jit(_where)/select_n | solution.py:68
  178.6 9.2 %all-to-all-start.2 = ((bf16[32,320,128]{2,1,0:T(8,128)(2,1)}), bf16[32,320,128]{2,1,0:T(8,128)(2,1)S(1)}, u32[]{:S(2)}, u32[]{:S(2)}) async-start(bf16[32,320,128]{2,1,0:T(8,128)(2,1)} %select_select_fusion), calls=%async_computation.2 | async-start | bytes 5242880 | tf_op jit(solution)/shard_map/all_to_all | solution.py:110
  188.1 59.5 %all-to-all-done.2 = bf16[32,320,128]{2,1,0:T(8,128)(2,1)S(1)} async-done(((bf16[32,320,128]{2,1,0:T(8,128)(2,1)}), bf16[32,320,128]{2,1,0:T(8,128)(2,1)S(1)}, u32[]{:S(2)}, u32[]{:S(2)}) %all-to-all-start.2) | async-done | bytes 2621472 | tf_op jit(solution)/shard_map/all_to_all | solution.py:110
  247.6 5.4 %while.23 = (s32[]{:T(128)}, f32[512,128]{1,0:T(8,128)S(1)}, s32[8,1280]{1,0:T(8,128)S(1)}, bf16[8,1280,128]{2,1,0:T(8,128)(2,1)S(1)}, s32[]{:T(128)}, /*index=5*/s32[]{:T(128)}) while((s32[]{:T(128)}, f32[512,128]{1,0:T(8,128)S(1)}, s32[8,1280]{1,0:T(8,128)S(1)}, bf16[8,1280,128]{2,1,0:T(8,128)(2,1)S(1)}, s32[]{:T(128)}, ...), condition=%wide.region_5.6_spmd.clone, body=%wide.region_4.5_spmd.clone.sunk | while | flops 168558592 | bytes 870487 | solution.py:121
  248.3 0.6 fusion.36
  249.6 0.6 fusion.36
  252.9 0.7 copy-done.4
  (73 shorter events, 7.2 us)
Async XLA Ops:
  0.0 112.1 %copy-start = (bf16[1,1024,256]{2,1,0:T(8,128)(2,1)S(1)}, bf16[1,1024,256]{2,1,0:T(8,128)(2,1)}, u32[]{:S(2)}) copy-start(bf16[1,1024,256]{2,1,0:T(8,128)(2,1)} %param.15) | copy-start | bytes 1572868
  1.6 99.1 %all-to-all-start.1 = ((bf16[8,16,256]{2,0,1:T(8,128)(2,1)}), bf16[8,16,256]{2,0,1:T(8,128)(2,1)S(1)}, u32[]{:S(2)}, u32[]{:S(2)}) async-start(bf16[8,16,256]{2,0,1:T(8,128)(2,1)} %copy.25), calls=%async_computation.1 | async-start | bytes 131072 | tf_op jit(solution)/shard_map/all_to_all | solution.py:92
  17.3 25.8 %copy-start.1 = (s32[1,1,5120]{2,1,0:T(1,128)S(1)}, s32[1,1,5120]{2,1,0:T(1,128)}, u32[]{:S(2)}) copy-start(s32[1,1,5120]{2,1,0:T(1,128)} %param.21) | copy-start | bytes 61444
  43.1 69.0 %copy-start.2 = (bf16[1,128,1024]{2,1,0:T(8,128)(2,1)S(1)}, bf16[1,128,1024]{2,1,0:T(8,128)(2,1)}, u32[]{:S(2)}) copy-start(bf16[1,128,1024]{2,1,0:T(8,128)(2,1)} %param.14) | copy-start | bytes 786436
  100.7 77.9 %all-to-all-start = ((s32[32,1,320]{2,1,0:T(1,128)}), s32[32,1,320]{2,1,0:T(1,128)S(1)}, u32[]{:S(2)}, u32[]{:S(2)}) async-start(s32[32,1,320]{2,1,0:T(1,128)} %all_to_all.20), calls=%async_computation | async-start | bytes 98304 | tf_op jit(solution)/shard_map/all_to_all | solution.py:111
  119.1 15.1 %copy-start.3 = (f32[1,1,5120]{2,1,0:T(1,128)S(1)}, f32[1,1,5120]{2,1,0:T(1,128)}, u32[]{:S(2)}) copy-start(f32[1,1,5120]{2,1,0:T(1,128)} %param.19) | copy-start | bytes 61444
  178.6 69.0 %all-to-all-start.2 = ((bf16[32,320,128]{2,1,0:T(8,128)(2,1)}), bf16[32,320,128]{2,1,0:T(8,128)(2,1)S(1)}, u32[]{:S(2)}, u32[]{:S(2)}) async-start(bf16[32,320,128]{2,1,0:T(8,128)(2,1)} %select_select_fusion), calls=%async_computation.2 | async-start | bytes 5242880 | tf_op jit(solution)/shard_map/all_to_all | solution.py:110
  252.9 0.7 copy-start.4
where the time goes:
time: 255 us; the launch traced here: 254 us
  local copies, waits for them, and re-layouts  114 us (45%)
  waiting for transfers between devices  59.5 us (23%)
  other arithmetic  35.9 us (14%)
  starting transfers between devices  30.8 us (12%)
  matrix products  12.5 us (5%)
    all_to_all x1, waiting for transfers between devices, local(): lax.all_to_all(outgoing, 'shard', split_axis=0, concat_axis=0, tiled=True)  59.5 us
    gather x2, local copies, waits for them, and re-layouts, bucket_rows(): jnp.take(local_rows, safe_index, axis=0)  56.9 us
    gather x1, local copies, waits for them, and re-layouts, bucket_rows(): jnp.take(elem_grads, safe_index, axis=0)  36.4 us
    reduce_sum x10, other arithmetic, count_step(): return (total + jnp.sum(below, axis=0), None)  24.2 us
    gather x1, local copies, waits for them, and re-layouts, element_gradients(): gathered = jnp.take(pooled_flat, local_row * FEAT + slot_index, axis=0)  15.1 us
    all_to_all x1, starting transfers between devices, local(): lax.all_to_all(out_rows, 'shard', split_axis=0, concat_axis=0, tiled=True)  11.4 us
    all_to_all x1, starting transfers between devices, local(): lax.all_to_all(out_grad, 'tower', split_axis=1, concat_axis=0, tiled=True)  10.2 us
    all_to_all x1, starting transfers between devices, local(): lax.all_to_all(outgoing, 'shard', split_axis=0, concat_axis=0, tiled=True)  9.23 us
  transfers between devices with their start and end apart: 3, of which 1 were waited for; matrix products, arithmetic and copies ran while one was open for 61% of the time, Pallas kernels for 0%

commit v1 on v0

v1 whole, which is shorter than its diff:
```python
import functools

import jax
import jax.numpy as jnp
from jax import lax
from jax.experimental import pallas as pl
from jax.experimental.pallas import tpu as pltpu
from jax.sharding import Mesh
from jax.sharding import PartitionSpec as P

E = 128
FEAT = 32
SAMP = 128
HID = 1024
TOUT = 256
TIN = 4096
ROW_DEV = 512
ELEMS = 5120
CAP = 320
NX = 4
NZ = 8
HALVES = 2
HALF = ROW_DEV // HALVES
BUCKETS = NZ * HALVES
SUBS = NX * BUCKETS
PIECES = 6
SLOTS = 384
LANES = 128
CHUNKS = SLOTS // LANES
STEP = 512
UNROLL = 16
BF = jnp.bfloat16
F32 = jnp.float32
I32 = jnp.int32
NT = (((1,), (1,)), ((), ()))


def bucket_kernel(seg_ref, weight_ref, owner_ref, row_ref, slot_ref, out_ref, acc_ref):
    upper = (
        lax.broadcasted_iota(I32, (STEP, STEP), 0) <= lax.broadcasted_iota(I32, (STEP, STEP), 1)
    ).astype(F32).astype(BF)
    sub_ids = lax.broadcasted_iota(I32, (SUBS, STEP), 0)
    feat_ids = lax.broadcasted_iota(I32, (FEAT, STEP), 0)
    slot_ids = lax.broadcasted_iota(I32, (SLOTS, STEP), 0).astype(F32)
    acc_ref[...] = jnp.zeros_like(acc_ref)

    def step(k, carry):
        cols = pl.ds(pl.multiple_of(k * STEP, STEP), STEP)
        seg = seg_ref[:, cols]
        weight = weight_ref[:, cols]
        owner = owner_ref[:, cols]
        row = row_ref[:, cols]
        sub = (owner & 3) * BUCKETS + (row >> 8) * NZ + (owner >> 2)
        mine = sub_ids == sub
        ones = jnp.where(mine, 1.0, 0.0)
        inclusive = jnp.dot(ones.astype(BF), upper, preferred_element_type=F32) + carry
        rank = jnp.sum(ones * inclusive, axis=0, keepdims=True) - 1.0
        block = jnp.sum(
            jnp.where(feat_ids == (seg & 31), slot_ref[...], 0.0), axis=0, keepdims=True
        )
        sample = (seg >> 5).astype(F32)
        row_next = ((row & 255) + 1).astype(F32)
        high = weight.astype(BF).astype(F32)
        rest = weight - high
        middle = rest.astype(BF).astype(F32)
        low = rest - middle
        pieces = (block, sample, row_next, high, middle, low)
        left = jnp.concatenate([(ones * piece).astype(BF) for piece in pieces], axis=0)
        right = jnp.where(slot_ids == rank, 1.0, 0.0).astype(BF)
        acc_ref[...] += lax.dot_general(left, right, NT, preferred_element_type=F32)
        return inclusive[:, STEP - 1 : STEP]

    count = lax.fori_loop(0, ELEMS // STEP, step, jnp.zeros((SUBS, 1), F32))
    count = jnp.broadcast_to(count.astype(I32), (SUBS, LANES))
    count_parts = ((count >> 7).astype(F32), (count & 127).astype(F32))
    spare = lax.broadcasted_iota(I32, (SUBS, LANES), 1) >= CAP - (CHUNKS - 1) * LANES
    for p in range(PIECES):
        for c in range(CHUNKS):
            part = acc_ref[p * SUBS : (p + 1) * SUBS, c * LANES : (c + 1) * LANES]
            if p < 2 and c == CHUNKS - 1:
                part = jnp.where(spare, count_parts[p], part)
            part = part.astype(BF)
            for x in range(NX):
                out_ref[x, p, c] = part[x * BUCKETS : (x + 1) * BUCKETS]


def bucket_elements(segment, weight, owner, row, slots):
    return pl.pallas_call(
        bucket_kernel,
        out_shape=jax.ShapeDtypeStruct((NX, PIECES, CHUNKS, BUCKETS, LANES), BF),
        in_specs=[pl.BlockSpec(memory_space=pltpu.VMEM)] * 5,
        out_specs=pl.BlockSpec(memory_space=pltpu.VMEM),
        scratch_shapes=[pltpu.VMEM((PIECES * SUBS, SLOTS), F32)],
        compiler_params=pltpu.CompilerParams(vmem_limit_bytes=32 << 20),
        cost_estimate=pl.CostEstimate(flops=3 << 30, bytes_accessed=1 << 20, transcendentals=0),
    )(segment, weight, owner, row, slots)


def add_elements(half, index_ref, weight_ref, row_ref, pooled_ref, group_ref, total_ref, out_ref):
    group_ref[...] = jnp.zeros_like(group_ref)

    def fetch(x, place, count):
        def some(i, unused):
            base = pl.multiple_of(i * UNROLL, UNROLL)
            for u in range(UNROLL):
                source = index_ref[place, base + u] + x * (FEAT * SAMP)
                scale = weight_ref[place, base + u]
                value = pooled_ref[pl.ds(source, 1), :] * scale
                group_ref[pl.ds(x * LANES + base + u, 1), :] = value
            return unused

        lax.fori_loop(0, (count + (UNROLL - 1)) // UNROLL, some, 0)

    def owner_step(o, unused):
        bucket = half * NZ + o
        places = [x * CHUNKS * BUCKETS + bucket for x in range(NX)]
        counts = [
            index_ref[places[x] + (CHUNKS - 1) * BUCKETS, CAP - (CHUNKS - 1) * LANES]
            for x in range(NX)
        ]
        for x in range(NX):
            fetch(x, places[x], jnp.minimum(counts[x], LANES))
        rows = jnp.concatenate([row_ref[pl.ds(places[x], 1), :] for x in range(NX)], axis=1)
        row_ids = lax.broadcasted_iota(I32, (HALF, NX * LANES), 0) + 1
        chosen = jnp.where(row_ids == rows, 1.0, 0.0).astype(BF)
        total_ref[...] = jnp.dot(
            chosen, group_ref[...].astype(BF), preferred_element_type=F32
        )
        for x in range(NX):
            for c in range(1, CHUNKS):

                @pl.when(counts[x] > c * LANES)
                def _():
                    place = places[x] + c * BUCKETS
                    fetch(x, place, jnp.minimum(counts[x] - c * LANES, LANES))
                    ids = lax.broadcasted_iota(I32, (HALF, LANES), 0) + 1
                    more = jnp.where(ids == row_ref[pl.ds(place, 1), :], 1.0, 0.0).astype(BF)
                    total_ref[...] += jnp.dot(
                        more,
                        group_ref[x * LANES : (x + 1) * LANES, :].astype(BF),
                        preferred_element_type=F32,
                    )

        out_ref[o] = total_ref[...].astype(BF)
        return unused

    lax.fori_loop(0, NZ, owner_step, 0)


UP_STEP = 512
UP_STEPS = TIN // UP_STEP


def first_kernel(
    index_ref,
    weight_ref,
    row_ref,
    grad_ref,
    hidden_ref,
    down_ref,
    up_ref,
    out_ref,
    pooled_out_ref,
    hid_ref,
    pooled_ref,
    group_ref,
    total_ref,
    sem,
):
    k = pl.program_id(0)

    @pl.when(k == 0)
    def _():
        for x in range(NX):
            left = jnp.concatenate([grad_ref[x, 0], grad_ref[x, 1]], axis=1)
            backward = lax.dot_general(left, down_ref[...], NT, preferred_element_type=F32)
            keep = hidden_ref[x * SAMP : (x + 1) * SAMP, :].astype(F32) > 0
            hid_ref[x * SAMP : (x + 1) * SAMP, :] = jnp.where(keep, backward, 0.0).astype(BF)

    result = lax.dot_general(hid_ref[...], up_ref[...], NT, preferred_element_type=F32)
    result = result.astype(BF).astype(F32)
    for x in range(NX):
        for j in range(UP_STEP // E):
            start = pl.multiple_of(x * FEAT * SAMP + (k * (UP_STEP // E) + j) * SAMP, SAMP)
            pooled_ref[pl.ds(start, SAMP), :] = result[
                x * SAMP : (x + 1) * SAMP, j * E : (j + 1) * E
            ]

    @pl.when(k == UP_STEPS - 1)
    def _():
        copy = pltpu.make_async_copy(pooled_ref, pooled_out_ref, sem)
        copy.start()
        add_elements(
            0, index_ref, weight_ref, row_ref, pooled_ref, group_ref, total_ref, out_ref
        )
        copy.wait()


def first_half(index, weight, rows, grads, hidden, down, up):
    whole = lambda shape: pl.BlockSpec(shape, lambda k: (0,) * len(shape))
    smem = pl.BlockSpec(memory_space=pltpu.SMEM)
    return pl.pallas_call(
        first_kernel,
        grid=(UP_STEPS,),
        out_shape=(
            jax.ShapeDtypeStruct((NZ, HALF, E), BF),
            jax.ShapeDtypeStruct((NX * FEAT * SAMP, E), F32),
        ),
        in_specs=[
            smem,
            smem,
            whole(rows.shape),
            whole(grads.shape),
            whole(hidden.shape),
            whole(down.shape),
            pl.BlockSpec((UP_STEP, HID), lambda k: (k, 0)),
        ],
        out_specs=(whole((NZ, HALF, E)), pl.BlockSpec(memory_space=pl.ANY)),
        scratch_shapes=[
            pltpu.VMEM((NX * SAMP, HID), BF),
            pltpu.VMEM((NX * FEAT * SAMP, E), F32),
            pltpu.VMEM((NX * LANES, E), F32),
            pltpu.VMEM((HALF, E), F32),
            pltpu.SemaphoreType.DMA,
        ],
        compiler_params=pltpu.CompilerParams(vmem_limit_bytes=40 << 20),
        cost_estimate=pl.CostEstimate(flops=5 << 30, bytes_accessed=20 << 20, transcendentals=0),
    )(index, weight, rows, grads, hidden, down, up)


def second_kernel(index_ref, weight_ref, row_ref, pooled_ref, out_ref, group_ref, total_ref):
    add_elements(1, index_ref, weight_ref, row_ref, pooled_ref, group_ref, total_ref, out_ref)


def second_half(index, weight, rows, pooled):
    smem = pl.BlockSpec(memory_space=pltpu.SMEM)
    vmem = pl.BlockSpec(memory_space=pltpu.VMEM)
    return pl.pallas_call(
        second_kernel,
        out_shape=jax.ShapeDtypeStruct((NZ, HALF, E), BF),
        in_specs=[smem, smem, vmem, vmem],
        out_specs=vmem,
        scratch_shapes=[pltpu.VMEM((NX * LANES, E), F32), pltpu.VMEM((HALF, E), F32)],
        compiler_params=pltpu.CompilerParams(vmem_limit_bytes=32 << 20),
        cost_estimate=pl.CostEstimate(flops=5 << 30, bytes_accessed=10 << 20, transcendentals=0),
    )(index, weight, rows, pooled)


def local(
    out_grad,
    hidden_pre,
    down_proj,
    up_proj,
    feature_slot,
    element_segment,
    element_weight,
    row_owner,
    row_local,
):
    hidden = lax.all_gather(hidden_pre[0], "x", tiled=True)
    arrived = lax.all_to_all(out_grad, "tower", split_axis=1, concat_axis=0, tiled=True)
    grad_rows = arrived.reshape(SAMP, TOUT)
    flat = (1, ELEMS)
    meta = bucket_elements(
        element_segment.reshape(flat),
        element_weight.reshape(flat),
        row_owner.reshape(flat),
        row_local.reshape(flat),
        feature_slot.reshape(FEAT, 1).astype(F32),
    )
    halves = jnp.stack([grad_rows[:, :LANES], grad_rows[:, LANES:]]).reshape(1, 2 * SAMP, LANES)
    outgoing = jnp.concatenate(
        [
            jnp.broadcast_to(halves, (NX, 2 * SAMP, LANES)),
            meta.reshape(NX, PIECES * CHUNKS * BUCKETS, LANES),
        ],
        axis=1,
    )
    incoming = lax.all_to_all(outgoing, "x", split_axis=0, concat_axis=0, tiled=True)
    grads = incoming[:, : 2 * SAMP].reshape(NX, 2, SAMP, LANES)
    parts = incoming[:, 2 * SAMP :].reshape(NX, PIECES, CHUNKS * BUCKETS, LANES).astype(F32)
    table = (NX * CHUNKS * BUCKETS, LANES)
    index = (parts[:, 0] * SAMP + parts[:, 1]).astype(I32).reshape(table)
    rows = parts[:, 2].astype(I32).reshape(table)
    weight = (parts[:, 3] + parts[:, 4] + parts[:, 5]).reshape(table)
    sums, pooled = first_half(index, weight, rows, grads, hidden, down_proj[0], up_proj[0])
    swap = functools.partial(
        lax.all_to_all, axis_name="z", split_axis=0, concat_axis=0, tiled=True
    )
    first = swap(sums)
    second = swap(second_half(index, weight, rows, pooled))
    table_grad = jnp.concatenate(
        [jnp.sum(first.astype(F32), axis=0), jnp.sum(second.astype(F32), axis=0)], axis=0
    )
    return table_grad.reshape(1, ROW_DEV, E)


def solution(mesh):
    towers = mesh.shape["tower"]
    grid = Mesh(mesh.devices.reshape(towers, NZ, NX), ("tower", "z", "x"))
    shard = ("z", "x")
    in_specs = (
        P(("tower", "z", "x"), None, None),
        P("tower", shard, None),
        P("tower", None, None),
        P("tower", None, None),
        P("tower", None),
        P("tower", shard, None),
        P("tower", shard, None),
        P("tower", shard, None, None),
        P("tower", shard, None),
    )
    out_specs = P("tower", shard, None)
    return jax.shard_map(local, mesh=grid, in_specs=in_specs, out_specs=out_specs, check_vma=False)
```

time: 255 us -> 142 us (0.56)
  local copies, waits for them, and re-layouts: 114 us -> 12.4 us
  Pallas kernels: 0 us -> 50.4 us
  waiting for transfers between devices: 59.5 us -> 20.1 us
  other arithmetic: 35.9 us -> 1.64 us
  blocking collectives: 0 us -> 18.1 us
  between operations: 0.24 us -> 13.5 us
  matrix products: 12.5 us -> 0 us
  starting transfers between devices: 30.8 us -> 25.2 us
    gather x4 -> x0, local copies, waits for them, and re-layouts: 108 us -> none  [the longest x2 56.9 us: bucket_rows(): jnp.take(local_rows, safe_index, axis=0)]
    pallas_call x0 -> x3, Pallas kernels: none -> 50.4 us  [the longest x1 27.2 us: first_half(): pl.pallas_call(first_kernel, grid=(UP_STEPS,), out_shape=(jax.ShapeDtypeS...]
    all_to_all x2, waiting for transfers between devices: 59.5 us -> 17.9 us  [the longest x1 17.9 us: local(): second = swap(second_half(index, weight, rows, pooled))]
    reduce_sum x11 -> x2, other arithmetic: 25 us -> 0.14 us  [the longest x1 0.07 us: local(): jnp.sum(first.astype(F32), axis=0)]
    all_to_all x0 -> x1, blocking collectives: none -> 18.1 us  [local(): lax.all_to_all(outgoing, 'x', split_axis=0, concat_axis=0, tiled=True)]
    dot_general x11 -> x0, matrix products: 12.5 us -> none  [the longest x1 6.44 us: local(): lax.dot_general(hid_grad, up_proj[0], contract, preferred_element_type=jn...]
    unnamed x11 -> x17, local copies, waits for them, and re-layouts: 2.27 us -> 12.2 us
    select_n x5 -> x0, other arithmetic: 7.9 us -> none  [the longest x1 6.23 us: bucket_rows(): jnp.where(filled[:, None], jnp.take(elem_grads, safe_index, axis=0), jnp....]
  transfers between devices with their start and end apart: 3 -> 4, of which waited for: 1 -> 2; matrix products, arithmetic and copies ran while one was open for 61% -> 2% of each run, Pallas kernels for 0% -> 16%
where the time goes in v1:
time: 142 us; the launch traced here: 141 us
  Pallas kernels  50.4 us (35%)
  starting transfers between devices  25.2 us (18%)
  waiting for transfers between devices  20.1 us (14%)
  blocking collectives  18.1 us (13%)
  between operations  13.5 us (10%)
  local copies, waits for them, and re-layouts  12.4 us (9%)
  other arithmetic  1.64 us (1%)
    pallas_call x1, Pallas kernels, first_half(): pl.pallas_call(first_kernel, grid=(UP_STEPS,), out_shape=(jax.ShapeDtypeS...  27.2 us
    all_to_all x1, blocking collectives, local(): lax.all_to_all(outgoing, 'x', split_axis=0, concat_axis=0, tiled=True)  18.1 us
    all_to_all x1, waiting for transfers between devices, local(): second = swap(second_half(index, weight, rows, pooled))  17.9 us
    pallas_call x1, Pallas kernels, second_half(): pl.pallas_call(second_kernel, out_shape=jax.ShapeDtypeStruct((NZ, HALF, E...  17.3 us
    unnamed x17, local copies, waits for them, and re-layouts  12.2 us
    all_to_all x1, starting transfers between devices, local(): lax.all_to_all(out_grad, 'tower', split_axis=1, concat_axis=0, tiled=True)  10.2 us
    all_to_all x1, starting transfers between devices, local(): first = swap(sums)  8.07 us
    all_to_all x1, starting transfers between devices, local(): second = swap(second_half(index, weight, rows, pooled))  6.94 us
  transfers between devices with their start and end apart: 4, of which 2 were waited for; matrix products, arithmetic and copies ran while one was open for 2% of the time, Pallas kernels for 16%

profile of v1, /device:TPU:1, one launch (start us, length us, event | category | flops | bytes accessed | tf_op | source)
XLA Modules:
  0.0 141.4 jit_solution(10866799111961424681)
XLA Ops:
  6.5 0.0 all-gather.3.cloned.1.call-start
  6.5 0.7 all-gather.3.cloned.1.call-update
  7.3 1.5 %copy.11 = bf16[8,16,256]{2,0,1:T(8,128)(2,1)} copy(bf16[8,16,256]{2,1,0:T(8,128)(2,1)} %param.9) | data formatting | bytes 131072 | tf_op args[0]
  8.7 10.2 %all-to-all-start = ((bf16[8,16,256]{2,0,1:T(8,128)(2,1)}), bf16[8,16,256]{2,0,1:T(8,128)(2,1)S(1)}, u32[]{:S(2)}, u32[]{:S(2)}) async-start(bf16[8,16,256]{2,0,1:T(8,128)(2,1)} %copy.11), calls=%async_computation | async-start | bytes 131072 | tf_op jit(solution)/shard_map/all_to_all | solution.py:261
  18.9 0.7 convert_bitcast_fusion
  19.6 0.1 copy.12.slot_ref
  19.7 0.0 copy-start.2
  19.7 0.7 copy-done.2
  20.4 0.0 copy-start.3
  20.4 0.7 copy-done.3
  21.1 0.0 copy-start.4
  21.1 0.7 copy-done.4
  21.9 0.7 copy-done.5
  22.6 6.0 %shard_map.91 = bf16[4,6,3,16,128]{4,3,2,1,0:T(8,128)(2,1)S(1)} custom-call(s32[1,5120]{1,0:T(1,128)S(1)} %bitcast.38, f32[1,5120]{1,0:T(1,128)S(1)} %bitcast.39, s32[1,5120]{1,0:T(1,128)S(1)} %bitcast.40, s32[1,5120]{1,0:T(1,128)S(1)} %bitcast.41, f32[32,1]{1,0:T(8,128)S(1)} %copy.12.slot_ref), custom_call_target="tpu_custom_call" | custom-call | flops 3221225472 | bytes 1048576 | tf_op jit(solution)/shard_map/pallas_call | solution.py:88
  28.6 0.0 all-to-all-done
  28.7 18.1 %all_to_all.30 = bf16[4,544,128]{2,1,0:T(8,128)(2,1)S(1)} all-to-all(bf16[4,544,128]{2,1,0:T(8,128)(2,1)S(1)} %pad_maximum_fusion), channel_id=1, replica_groups=mesh['tower'=16,'z'=8,'x'=4] {'x'}, dimensions={0} | all-to-all | bytes 1114112 | tf_op jit(solution)/shard_map/all_to_all | solution.py:279
  46.8 0.0 copy-start.1
  47.0 1.5 %all-gather.3.cloned.1.call-done = bf16[1,512,1024]{2,1,0:T(8,128)(2,1)} async-done(((bf16[1,128,1024]{2,1,0:T(8,128)(2,1)}), bf16[1,512,1024]{2,1,0:T(8,128)(2,1)}) %all-gather.3.cloned.1.call-update) | async-done | bytes 1048592 | tf_op jit(solution)/shard_map/all_gather | solution.py:260
  48.5 0.0 copy-done.1
  48.5 1.2 copy-done
  49.7 27.2 %shard_map.92 = (bf16[8,256,128]{2,1,0:T(8,128)(2,1)}, f32[16384,128]{1,0:T(8,128)S(1)}) custom-call(s32[192,128]{1,0:T(8,128)S(1)} %bitcast.34, f32[192,128]{1,0:T(8,128)S(1)} %bitcast.32, s32[192,128]{1,0:T(8,128)S(1)} %bitcast.30, bf16[4,2,128,128]{3,2,1,0:T(8,128)(2,1)S(1)} %bitcast.29, bf16[512,1024]{1,0:T(8,128)(2,1)S(1)} %bitcast.36, ...), custom_call_target="tpu_custom_call" | custom-call | flops 5368709120 | bytes 20971520 | tf_op jit(solution)/shard_map/pallas_call | solution.py:202
  76.9 0.0 copy-start.6
  76.9 3.2 %copy-done.6 = f32[16384,128]{1,0:T(8,128)} copy-done((f32[16384,128]{1,0:T(8,128)}, f32[16384,128]{1,0:T(8,128)S(1)}, u32[]{:S(2)}) %copy-start.6) | copy-done | bytes 8388632
  80.1 8.1 %all-to-all-start.2 = ((bf16[8,256,128]{2,1,0:T(8,128)(2,1)}), bf16[8,256,128]{2,1,0:T(8,128)(2,1)S(1)}, u32[]{:S(2)}, u32[]{:S(2)}) async-start(bf16[8,256,128]{2,1,0:T(8,128)(2,1)} %get-tuple-element.7), calls=%async_computation.2 | async-start | bytes 1048576 | tf_op jit(solution)/shard_map/all_to_all | solution.py:290
  88.2 3.4 %copy-done.7 = f32[16384,128]{1,0:T(8,128)S(1)} copy-done((f32[16384,128]{1,0:T(8,128)S(1)}, f32[16384,128]{1,0:T(8,128)}, u32[]{:S(2)}) %copy-start.7) | copy-done | bytes 8388632
  91.5 17.3 %shard_map.93 = bf16[8,256,128]{2,1,0:T(8,128)(2,1)} custom-call(s32[192,128]{1,0:T(8,128)S(1)} %bitcast.35, f32[192,128]{1,0:T(8,128)S(1)} %bitcast.33, s32[192,128]{1,0:T(8,128)S(1)} %bitcast.31, f32[16384,128]{1,0:T(8,128)S(1)} %copy-done.7), custom_call_target="tpu_custom_call" | custom-call | flops 5368709120 | bytes 10485760 | tf_op jit(solution)/shard_map/pallas_call | solution.py:238
  108.8 0.0 all-to-all-done.2
  108.8 6.9 %all-to-all-start.3 = ((bf16[8,256,128]{2,1,0:T(8,128)(2,1)}), bf16[8,256,128]{2,1,0:T(8,128)(2,1)S(1)}, u32[]{:S(2)}, u32[]{:S(2)}) async-start(bf16[8,256,128]{2,1,0:T(8,128)(2,1)} %shard_map.93), calls=%async_computation.3 | async-start | bytes 1048576 | tf_op jit(solution)/shard_map/all_to_all | solution.py:291
  115.8 0.1 convert_reduce_fusion.1
  115.9 17.9 %all-to-all-done.3 = bf16[8,256,128]{2,1,0:T(8,128)(2,1)S(1)} async-done(((bf16[8,256,128]{2,1,0:T(8,128)(2,1)}), bf16[8,256,128]{2,1,0:T(8,128)(2,1)S(1)}, u32[]{:S(2)}, u32[]{:S(2)}) %all-to-all-start.3) | async-done | bytes 524320 | tf_op jit(solution)/shard_map/all_to_all | solution.py:291
  133.7 0.1 convert_reduce_fusion
  133.8 0.7 maximum_bitcast_fusion
  (11 shorter events, 0.2 us)
Async XLA Ops:
  6.5 41.9 %all-gather.3.cloned.1.call-start = ((), (), s32[]{:S(2)}) async-start(), calls=%async_computation.4 | async-start | bytes 1310720 | tf_op jit(solution)/shard_map/all_gather | solution.py:260
  8.7 19.8 %all-to-all-start = ((bf16[8,16,256]{2,0,1:T(8,128)(2,1)}), bf16[8,16,256]{2,0,1:T(8,128)(2,1)S(1)}, u32[]{:S(2)}, u32[]{:S(2)}) async-start(bf16[8,16,256]{2,0,1:T(8,128)(2,1)} %copy.11), calls=%async_computation | async-start | bytes 131072 | tf_op jit(solution)/shard_map/all_to_all | solution.py:261
  19.7 0.7 copy-start.2
  20.4 0.7 copy-start.3
  21.1 0.7 copy-start.4
  21.8 0.7 copy-start.5
  46.8 1.6 %copy-start.1 = (bf16[1,1024,256]{2,1,0:T(8,128)(2,1)S(1)}, bf16[1,1024,256]{2,1,0:T(8,128)(2,1)}, u32[]{:S(2)}) copy-start(bf16[1,1024,256]{2,1,0:T(8,128)(2,1)} %param.11) | copy-start | bytes 1572868
  48.5 1.2 copy-start
  76.9 3.2 %copy-start.6 = (f32[16384,128]{1,0:T(8,128)}, f32[16384,128]{1,0:T(8,128)S(1)}, u32[]{:S(2)}) copy-start(f32[16384,128]{1,0:T(8,128)S(1)} %get-tuple-element.8.pooled_ref) | copy-start | bytes 25165828
  80.1 28.7 %all-to-all-start.2 = ((bf16[8,256,128]{2,1,0:T(8,128)(2,1)}), bf16[8,256,128]{2,1,0:T(8,128)(2,1)S(1)}, u32[]{:S(2)}, u32[]{:S(2)}) async-start(bf16[8,256,128]{2,1,0:T(8,128)(2,1)} %get-tuple-element.7), calls=%async_computation.2 | async-start | bytes 1048576 | tf_op jit(solution)/shard_map/all_to_all | solution.py:290
  88.2 3.4 %copy-start.7 = (f32[16384,128]{1,0:T(8,128)S(1)}, f32[16384,128]{1,0:T(8,128)}, u32[]{:S(2)}) copy-start(f32[16384,128]{1,0:T(8,128)} %copy-done.6) | copy-start | bytes 25165828
  108.8 24.9 %all-to-all-start.3 = ((bf16[8,256,128]{2,1,0:T(8,128)(2,1)}), bf16[8,256,128]{2,1,0:T(8,128)(2,1)S(1)}, u32[]{:S(2)}, u32[]{:S(2)}) async-start(bf16[8,256,128]{2,1,0:T(8,128)(2,1)} %shard_map.93), calls=%async_computation.3 | async-start | bytes 1048576 | tf_op jit(solution)/shard_map/all_to_all | solution.py:291
Sparse Core Ops, SparseCore 0:
  9.5 38.9 all-gather.2

commit v2 on v1

--- a/solution.py
+++ b/solution.py
@@ -23,7 +23,7 @@
 HALF = ROW_DEV // HALVES
 BUCKETS = NZ * HALVES
 SUBS = NX * BUCKETS
-PIECES = 6
+PIECES = 5
 SLOTS = 384
 LANES = 128
 CHUNKS = SLOTS // LANES
@@ -63,8 +63,7 @@
         high = weight.astype(BF).astype(F32)
         rest = weight - high
         middle = rest.astype(BF).astype(F32)
-        low = rest - middle
-        pieces = (block, sample, row_next, high, middle, low)
+        pieces = (block, sample, row_next, high, middle)
         left = jnp.concatenate([(ones * piece).astype(BF) for piece in pieces], axis=0)
         right = jnp.where(slot_ids == rank, 1.0, 0.0).astype(BF)
         acc_ref[...] += lax.dot_general(left, right, NT, preferred_element_type=F32)
@@ -96,67 +95,92 @@
     )(segment, weight, owner, row, slots)
 
 
-def add_elements(half, index_ref, weight_ref, row_ref, pooled_ref, group_ref, total_ref, out_ref):
+def add_elements(
+    half, index_ref, weight_ref, row_ref, pooled_ref, group_ref, spill_ref, total_ref, out_ref
+):
     group_ref[...] = jnp.zeros_like(group_ref)
-
-    def fetch(x, place, count):
-        def some(i, unused):
-            base = pl.multiple_of(i * UNROLL, UNROLL)
+    spill_ref[...] = jnp.zeros_like(spill_ref)
+
+    def place_of(i):
+        return (i & (NX - 1)) * (CHUNKS * BUCKETS) + half * NZ + (i >> 2)
+
+    def count_of(place):
+        return index_ref[
+            (place + (CHUNKS - 1) * BUCKETS) * LANES + CAP - (CHUNKS - 1) * LANES
+        ]
+
+    def fetch(place, count, target_ref, start):
+        def some(j, unused):
+            source = place * LANES + j * UNROLL
+            target = pl.multiple_of(start + j * UNROLL, UNROLL)
             for u in range(UNROLL):
-                source = index_ref[place, base + u] + x * (FEAT * SAMP)
-                scale = weight_ref[place, base + u]
-                value = pooled_ref[pl.ds(source, 1), :] * scale
-                group_ref[pl.ds(x * LANES + base + u, 1), :] = value
+                value = pooled_ref[pl.ds(index_ref[source + u], 1), :] * weight_ref[source + u]
+                target_ref[pl.ds(target + u, 1), :] = value
             return unused
 
         lax.fori_loop(0, (count + (UNROLL - 1)) // UNROLL, some, 0)
 
-    def owner_step(o, unused):
-        bucket = half * NZ + o
-        places = [x * CHUNKS * BUCKETS + bucket for x in range(NX)]
-        counts = [
-            index_ref[places[x] + (CHUNKS - 1) * BUCKETS, CAP - (CHUNKS - 1) * LANES]
-            for x in range(NX)
-        ]
-        for x in range(NX):
-            fetch(x, places[x], jnp.minimum(counts[x], LANES))
-        rows = jnp.concatenate([row_ref[pl.ds(places[x], 1), :] for x in range(NX)], axis=1)
-        row_ids = lax.broadcasted_iota(I32, (HALF, NX * LANES), 0) + 1
-        chosen = jnp.where(row_ids == rows, 1.0, 0.0).astype(BF)
-        total_ref[...] = jnp.dot(
-            chosen, group_ref[...].astype(BF), preferred_element_type=F32
+    def bucket_step(i, unused):
+        place = place_of(i)
+        fetch(place, jnp.minimum(count_of(place), LANES), group_ref, i * LANES)
+        return unused
+
+    lax.fori_loop(0, NZ * NX, bucket_step, 0)
+
+    def chosen(rows):
+        row_ids = lax.broadcasted_iota(I32, (HALF, rows.shape[1]), 0) + 1
+        return jnp.where(row_ids == rows, 1.0, 0.0).astype(BF)
+
+    for o in range(NZ):
+        rows = jnp.concatenate(
+            [
+                row_ref[pl.ds(x * CHUNKS * BUCKETS + half * NZ + o, 1), :]
+                for x in range(NX)
+            ],
+            axis=1,
         )
-        for x in range(NX):
-            for c in range(1, CHUNKS):
-
-                @pl.when(counts[x] > c * LANES)
-                def _():
-                    place = places[x] + c * BUCKETS
-                    fetch(x, place, jnp.minimum(counts[x] - c * LANES, LANES))
-                    ids = lax.broadcasted_iota(I32, (HALF, LANES), 0) + 1
-                    more = jnp.where(ids == row_ref[pl.ds(place, 1), :], 1.0, 0.0).astype(BF)
-                    total_ref[...] += jnp.dot(
-                        more,
-                        group_ref[x * LANES : (x + 1) * LANES, :].astype(BF),
-                        preferred_element_type=F32,
-                    )
-
-        out_ref[o] = total_ref[...].astype(BF)
-        return unused
-
-    lax.fori_loop(0, NZ, owner_step, 0)
-
-
+        values = group_ref[o * NX * LANES : (o + 1) * NX * LANES, :].astype(BF)
+        total_ref[o] = jnp.dot(chosen(rows), values, preferred_element_type=F32)
+
+    def spill_step(i, unused):
+        place = place_of(i)
+        count = count_of(place)
+
+        def chunk_step(c, unused):
+            there = place + c * BUCKETS
+            fetch(there, jnp.minimum(count - c * LANES, LANES), spill_ref, 0)
+            total_ref[i >> 2] += jnp.dot(
+                chosen(row_ref[pl.ds(there, 1), :]),
+                spill_ref[...].astype(BF),
+                preferred_element_type=F32,
+            )
+            return unused
+
+        return lax.fori_loop(1, (count + (LANES - 1)) // LANES, chunk_step, unused)
+
+    lax.fori_loop(0, NZ * NX, spill_step, 0)
+    out_ref[...] = total_ref[...].astype(BF)
+
+
+SCRATCH = (
+    pltpu.VMEM((NZ * NX * LANES, E), F32),
+    pltpu.VMEM((LANES, E), F32),
+    pltpu.VMEM((NZ, HALF, E), F32),
+)
 UP_STEP = 512
 UP_STEPS = TIN // UP_STEP
 
 
 def first_kernel(
+    me_ref,
     index_ref,
     weight_ref,
     row_ref,
     grad_ref,
-    hidden_ref,
+    hidden0_ref,
+    hidden1_ref,
+    hidden2_ref,
+    hidden3_ref,
     down_ref,
     up_ref,
     out_ref,
@@ -164,6 +188,7 @@
     hid_ref,
     pooled_ref,
     group_ref,
+    spill_ref,
     total_ref,
     sem,
 ):
@@ -171,11 +196,13 @@
 
     @pl.when(k == 0)
     def _():
-        for x in range(NX):
+        for r, hidden_ref in enumerate((hidden0_ref, hidden1_ref, hidden2_ref, hidden3_ref)):
+            x = (me_ref[0] + (NX - r)) & (NX - 1)
             left = jnp.concatenate([grad_ref[x, 0], grad_ref[x, 1]], axis=1)
             backward = lax.dot_general(left, down_ref[...], NT, preferred_element_type=F32)
-            keep = hidden_ref[x * SAMP : (x + 1) * SAMP, :].astype(F32) > 0
-            hid_ref[x * SAMP : (x + 1) * SAMP, :] = jnp.where(keep, backward, 0.0).astype(BF)
+            keep = hidden_ref[...].astype(F32) > 0
+            there = pl.ds(pl.multiple_of(x * SAMP, SAMP), SAMP)
+            hid_ref[there, :] = jnp.where(keep, backward, 0.0).astype(BF)
 
     result = lax.dot_general(hid_ref[...], up_ref[...], NT, preferred_element_type=F32)
     result = result.astype(BF).astype(F32)
@@ -191,12 +218,20 @@
         copy = pltpu.make_async_copy(pooled_ref, pooled_out_ref, sem)
         copy.start()
         add_elements(
-            0, index_ref, weight_ref, row_ref, pooled_ref, group_ref, total_ref, out_ref
+            0,
+            index_ref,
+            weight_ref,
+            row_ref,
+            pooled_ref,
+            group_ref,
+            spill_ref,
+            total_ref,
+            out_ref,
         )
         copy.wait()
 
 
-def first_half(index, weight, rows, grads, hidden, down, up):
+def first_half(me, index, weight, rows, grads, hiddens, down, up):
     whole = lambda shape: pl.BlockSpec(shape, lambda k: (0,) * len(shape))
     smem = pl.BlockSpec(memory_space=pltpu.SMEM)
     return pl.pallas_call(
@@ -204,32 +239,40 @@
         grid=(UP_STEPS,),
         out_shape=(
             jax.ShapeDtypeStruct((NZ, HALF, E), BF),
-            jax.ShapeDtypeStruct((NX * FEAT * SAMP, E), F32),
+            pltpu.HBM((NX * FEAT * SAMP, E), F32),
         ),
         in_specs=[
             smem,
             smem,
+            smem,
             whole(rows.shape),
             whole(grads.shape),
-            whole(hidden.shape),
+            *[whole((SAMP, HID))] * NX,
             whole(down.shape),
             pl.BlockSpec((UP_STEP, HID), lambda k: (k, 0)),
         ],
-        out_specs=(whole((NZ, HALF, E)), pl.BlockSpec(memory_space=pl.ANY)),
+        out_specs=(whole((NZ, HALF, E)), pl.BlockSpec(memory_space=pltpu.HBM)),
         scratch_shapes=[
             pltpu.VMEM((NX * SAMP, HID), BF),
             pltpu.VMEM((NX * FEAT * SAMP, E), F32),
-            pltpu.VMEM((NX * LANES, E), F32),
-            pltpu.VMEM((HALF, E), F32),
+            *SCRATCH,
             pltpu.SemaphoreType.DMA,
         ],
         compiler_params=pltpu.CompilerParams(vmem_limit_bytes=40 << 20),
         cost_estimate=pl.CostEstimate(flops=5 << 30, bytes_accessed=20 << 20, transcendentals=0),
-    )(index, weight, rows, grads, hidden, down, up)
-
-
-def second_kernel(index_ref, weight_ref, row_ref, pooled_ref, out_ref, group_ref, total_ref):
-    add_elements(1, index_ref, weight_ref, row_ref, pooled_ref, group_ref, total_ref, out_ref)
+    )(me, index, weight, rows, grads, *hiddens, down, up)
+
+
+def second_kernel(
+    index_ref, weight_ref, row_ref, pooled_hbm_ref, out_ref, pooled_ref, group_ref, spill_ref,
+    total_ref, sem,
+):
+    copy = pltpu.make_async_copy(pooled_hbm_ref, pooled_ref, sem)
+    copy.start()
+    copy.wait()
+    add_elements(
+        1, index_ref, weight_ref, row_ref, pooled_ref, group_ref, spill_ref, total_ref, out_ref
+    )
 
 
 def second_half(index, weight, rows, pooled):
@@ -238,12 +281,16 @@
     return pl.pallas_call(
         second_kernel,
         out_shape=jax.ShapeDtypeStruct((NZ, HALF, E), BF),
-        in_specs=[smem, smem, vmem, vmem],
+        in_specs=[smem, smem, vmem, pl.BlockSpec(memory_space=pltpu.HBM)],
         out_specs=vmem,
-        scratch_shapes=[pltpu.VMEM((NX * LANES, E), F32), pltpu.VMEM((HALF, E), F32)],
+        scratch_shapes=[
+            pltpu.VMEM((NX * FEAT * SAMP, E), F32),
+            *SCRATCH,
+            pltpu.SemaphoreType.DMA,
+        ],
         compiler_params=pltpu.CompilerParams(vmem_limit_bytes=32 << 20),
         cost_estimate=pl.CostEstimate(flops=5 << 30, bytes_accessed=10 << 20, transcendentals=0),
-    )(index, weight, rows, pooled)
+    )(index, weight, rows, pltpu.with_memory_space_constraint(pooled, pltpu.HBM))
 
 
 def local(
@@ -257,7 +304,11 @@
     row_owner,
     row_local,
 ):
-    hidden = lax.all_gather(hidden_pre[0], "x", tiled=True)
+    hidden = hidden_pre[0]
+    hiddens = [hidden] + [
+        lax.ppermute(hidden, "x", [(i, (i + shift) % NX) for i in range(NX)])
+        for shift in range(1, NX)
+    ]
     arrived = lax.all_to_all(out_grad, "tower", split_axis=1, concat_axis=0, tiled=True)
     grad_rows = arrived.reshape(SAMP, TOUT)
     flat = (1, ELEMS)
@@ -279,11 +330,18 @@
     incoming = lax.all_to_all(outgoing, "x", split_axis=0, concat_axis=0, tiled=True)
     grads = incoming[:, : 2 * SAMP].reshape(NX, 2, SAMP, LANES)
     parts = incoming[:, 2 * SAMP :].reshape(NX, PIECES, CHUNKS * BUCKETS, LANES).astype(F32)
-    table = (NX * CHUNKS * BUCKETS, LANES)
-    index = (parts[:, 0] * SAMP + parts[:, 1]).astype(I32).reshape(table)
-    rows = parts[:, 2].astype(I32).reshape(table)
-    weight = (parts[:, 3] + parts[:, 4] + parts[:, 5]).reshape(table)
-    sums, pooled = first_half(index, weight, rows, grads, hidden, down_proj[0], up_proj[0])
+    shape = (NX, CHUNKS * BUCKETS, LANES)
+    slot = lax.broadcasted_iota(I32, shape, 1) // BUCKETS * LANES + lax.broadcasted_iota(
+        I32, shape, 2
+    )
+    offset = jnp.where(slot < CAP, lax.broadcasted_iota(I32, shape, 0) * (FEAT * SAMP), 0)
+    index = ((parts[:, 0] * SAMP + parts[:, 1]).astype(I32) + offset).reshape(-1)
+    rows = parts[:, 2].astype(I32).reshape(NX * CHUNKS * BUCKETS, LANES)
+    weight = (parts[:, 3] + parts[:, 4]).reshape(-1)
+    me = lax.axis_index("x").astype(I32).reshape(1)
+    sums, pooled = first_half(
+        me, index, weight, rows, grads, hiddens, down_proj[0], up_proj[0]
+    )
     swap = functools.partial(
         lax.all_to_all, axis_name="z", split_axis=0, concat_axis=0, tiled=True
     )

time: 142 us -> 120 us (0.85)
  the two profiles are of different devices: /device:TPU:1 before, /device:TPU:9 now
where the time goes in v2:
time: 120 us; the launch traced here: 119 us
  Pallas kernels  42.8 us (36%)
  starting transfers between devices  39.1 us (33%)
  waiting for transfers between devices  26.5 us (22%)
  local copies, waits for them, and re-layouts  7.95 us (7%)
  other arithmetic  2.53 us (2%)
    pallas_call x1, Pallas kernels, first_half(): pl.pallas_call(first_kernel, grid=(UP_STEPS,), out_shape=(jax.ShapeDtypeS...  19.7 us
    all_to_all x1, waiting for transfers between devices, local(): second = swap(second_half(index, weight, rows, pooled))  17.9 us
    pallas_call x1, Pallas kernels, second_half(): pl.pallas_call(second_kernel, out_shape=jax.ShapeDtypeStruct((NZ, HALF, E...  17.5 us
    all_to_all x1, starting transfers between devices, local(): first = swap(sums)  9.88 us
    ppermute x3, starting transfers between devices, local(): lax.ppermute(hidden, 'x', [(i, (i + shift) % NX) for i in range(NX)])  9.32 us
    all_to_all x1, starting transfers between devices, local(): lax.all_to_all(out_grad, 'tower', split_axis=1, concat_axis=0, tiled=True)  8.72 us
    all_to_all x1, waiting for transfers between devices, local(): lax.all_to_all(outgoing, 'x', split_axis=0, concat_axis=0, tiled=True)  8.62 us
    unnamed x15, local copies, waits for them, and re-layouts  7.78 us
  transfers between devices with their start and end apart: 7, of which 2 were waited for; matrix products, arithmetic and copies ran while one was open for 3% of the time, Pallas kernels for 19%

profile of v2, /device:TPU:9, one launch (start us, length us, event | category | flops | bytes accessed | tf_op | source)
XLA Modules:
  0.0 119.1 jit_solution(6182778651310208744)
XLA Ops:
  0.0 4.4 %collective-permute-start.2 = (bf16[128,1024]{1,0:T(8,128)(2,1)}, bf16[128,1024]{1,0:T(8,128)(2,1)S(1)}, u32[]{:S(2)}, u32[]{:S(2)}) collective-permute-start(bf16[128,1024]{1,0:T(8,128)(2,1)} %bitcast.38), channel_id=1, source_target_pairs={{0,3},{1,0},{2,1},{3,2},{4,7},{5,4},{6,5},{7,6},{8,11},{9,8},{10,9... | collective-permute-start | bytes 786440 | tf_op jit(solution)/shard_map/ppermute | solution.py:309
  4.4 2.4 %collective-permute-start.1 = (bf16[128,1024]{1,0:T(8,128)(2,1)}, bf16[128,1024]{1,0:T(8,128)(2,1)S(1)}, u32[]{:S(2)}, u32[]{:S(2)}) collective-permute-start(bf16[128,1024]{1,0:T(8,128)(2,1)} %bitcast.39), channel_id=1, source_target_pairs={{0,2},{1,3},{2,0},{3,1},{4,6},{5,7},{6,4},{7,5},{8,10},{9,11},{10,... | collective-permute-start | bytes 786440 | tf_op jit(solution)/shard_map/ppermute | solution.py:309
  6.8 2.5 %collective-permute-start = (bf16[128,1024]{1,0:T(8,128)(2,1)}, bf16[128,1024]{1,0:T(8,128)(2,1)S(1)}, u32[]{:S(2)}, u32[]{:S(2)}) collective-permute-start(bf16[128,1024]{1,0:T(8,128)(2,1)} %bitcast.40), channel_id=1, source_target_pairs={{0,1},{1,2},{2,3},{3,0},{4,5},{5,6},{6,7},{7,4},{8,9},{9,10},{10,1... | collective-permute-start | bytes 786440 | tf_op jit(solution)/shard_map/ppermute | solution.py:309
  9.3 1.5 %copy.11 = bf16[8,16,256]{2,0,1:T(8,128)(2,1)} copy(bf16[8,16,256]{2,1,0:T(8,128)(2,1)} %param.9) | data formatting | bytes 131072 | tf_op args[0]
  10.8 8.7 %all-to-all-start = ((bf16[8,16,256]{2,0,1:T(8,128)(2,1)}), bf16[8,16,256]{2,0,1:T(8,128)(2,1)S(1)}, u32[]{:S(2)}, u32[]{:S(2)}) async-start(bf16[8,16,256]{2,0,1:T(8,128)(2,1)} %copy.11), calls=%async_computation | async-start | bytes 131072 | tf_op jit(solution)/shard_map/all_to_all | solution.py:312
  19.6 0.7 convert_bitcast_fusion
  20.2 0.1 copy.12.slot_ref
  20.3 0.7 copy-done.3
  21.0 0.7 copy-done.4
  21.8 0.7 copy-done.5
  22.5 0.7 copy-done.6
  23.2 5.6 %shard_map.91 = bf16[4,5,3,16,128]{4,3,2,1,0:T(8,128)(2,1)S(1)} custom-call(s32[1,5120]{1,0:T(1,128)S(1)} %bitcast.42, f32[1,5120]{1,0:T(1,128)S(1)} %bitcast.43, s32[1,5120]{1,0:T(1,128)S(1)} %bitcast.44, s32[1,5120]{1,0:T(1,128)S(1)} %bitcast.45, f32[32,1]{1,0:T(8,128)S(1)} %copy.12.slot_ref), custom_call_target="tpu_custom_call" | custom-call | flops 3221225472 | bytes 1048576 | tf_op jit(solution)/shard_map/pallas_call | solution.py:87
  28.9 0.0 all-to-all-done
  29.0 0.8 pad_maximum_fusion
  29.8 4.3 %all-to-all-start.1 = ((bf16[4,496,128]{2,1,0:T(8,128)(2,1)}), bf16[4,496,128]{2,1,0:T(8,128)(2,1)S(1)}, u32[]{:S(2)}, u32[]{:S(2)}) async-start(bf16[4,496,128]{2,1,0:T(8,128)(2,1)} %pad_maximum_fusion), calls=%async_computation.1 | async-start | bytes 1015808 | tf_op jit(solution)/shard_map/all_to_all | solution.py:330
  34.1 0.1 fusion.1
  34.2 8.6 %all-to-all-done.1 = bf16[4,496,128]{2,1,0:T(8,128)(2,1)S(1)} async-done(((bf16[4,496,128]{2,1,0:T(8,128)(2,1)}), bf16[4,496,128]{2,1,0:T(8,128)(2,1)S(1)}, u32[]{:S(2)}, u32[]{:S(2)}) %all-to-all-start.1) | async-done | bytes 507936 | tf_op jit(solution)/shard_map/all_to_all | solution.py:330
  43.0 0.0 collective-permute-done.2.hidden3_ref
  43.0 0.0 collective-permute-done.1.hidden2_ref
  43.0 0.0 collective-permute-done.hidden1_ref
  43.0 0.0 copy-done.1
  43.0 0.0 copy-start
  43.0 3.4 %copy-done = bf16[1,4096,1024]{2,1,0:T(8,128)(2,1)S(1)} copy-done((bf16[1,4096,1024]{2,1,0:T(8,128)(2,1)S(1)}, bf16[1,4096,1024]{2,1,0:T(8,128)(2,1)}, u32[]{:S(2)}) %copy-start) | copy-done | bytes 8388632
  46.4 19.7 %shard_map.92 = (bf16[8,256,128]{2,1,0:T(8,128)(2,1)}, f32[16384,128]{1,0:T(8,128)}) custom-call(s32[1]{0:T(128)} %bitcast.me_ref, s32[24576]{0:T(1024)S(1)} %add.24.index_ref, f32[24576]{0:T(1024)S(1)} %bitcast.34, s32[192,128]{1,0:T(8,128)S(1)} %bitcast.32, bf16[4,2,128,128]{3,2,1,0:T(8,128)(2,1)S(1)} %bitcast.30, bf16[128,1024]{1,0:T(8,128)(2,1)S(1)} %bitcast.41, ...), custom_call_target="tpu_custom_call" | custom-call | flops 5368709120 | bytes 20971520 | tf_op jit(solution)/shard_map/pallas_call | solution.py:237
  66.0 9.9 %all-to-all-start.2 = ((bf16[8,256,128]{2,1,0:T(8,128)(2,1)}), bf16[8,256,128]{2,1,0:T(8,128)(2,1)S(1)}, u32[]{:S(2)}, u32[]{:S(2)}) async-start(bf16[8,256,128]{2,1,0:T(8,128)(2,1)} %get-tuple-element.7), calls=%async_computation.2 | async-start | bytes 1048576 | tf_op jit(solution)/shard_map/all_to_all | solution.py:348
  75.9 17.5 %shard_map.93 = bf16[8,256,128]{2,1,0:T(8,128)(2,1)} custom-call(s32[24576]{0:T(1024)S(1)} %add.24.index_ref, f32[24576]{0:T(1024)S(1)} %bitcast.35, s32[192,128]{1,0:T(8,128)S(1)} %bitcast.33, f32[16384,128]{1,0:T(8,128)} %get-tuple-element.8.pooled_hbm_ref), custom_call_target="tpu_custom_call" | custom-call | flops 5368709120 | bytes 10485760 | tf_op jit(solution)/shard_map/pallas_call | solution.py:281
  93.4 0.0 all-to-all-done.2
  93.4 6.9 %all-to-all-start.3 = ((bf16[8,256,128]{2,1,0:T(8,128)(2,1)}), bf16[8,256,128]{2,1,0:T(8,128)(2,1)S(1)}, u32[]{:S(2)}, u32[]{:S(2)}) async-start(bf16[8,256,128]{2,1,0:T(8,128)(2,1)} %shard_map.93), calls=%async_computation.3 | async-start | bytes 1048576 | tf_op jit(solution)/shard_map/all_to_all | solution.py:349
  100.4 0.1 convert_reduce_fusion.1
  100.4 17.9 %all-to-all-done.3 = bf16[8,256,128]{2,1,0:T(8,128)(2,1)S(1)} async-done(((bf16[8,256,128]{2,1,0:T(8,128)(2,1)}), bf16[8,256,128]{2,1,0:T(8,128)(2,1)S(1)}, u32[]{:S(2)}, u32[]{:S(2)}) %all-to-all-start.3) | async-done | bytes 524320 | tf_op jit(solution)/shard_map/all_to_all | solution.py:349
  118.3 0.1 convert_reduce_fusion
  118.4 0.7 maximum_bitcast_fusion
  (18 shorter events, 0.2 us)
Async XLA Ops:
  0.0 43.0 %collective-permute-start.2 = (bf16[128,1024]{1,0:T(8,128)(2,1)}, bf16[128,1024]{1,0:T(8,128)(2,1)S(1)}, u32[]{:S(2)}, u32[]{:S(2)}) collective-permute-start(bf16[128,1024]{1,0:T(8,128)(2,1)} %bitcast.38), channel_id=1, source_target_pairs={{0,3},{1,0},{2,1},{3,2},{4,7},{5,4},{6,5},{7,6},{8,11},{9,8},{10,9... | collective-permute-start | bytes 786440 | tf_op jit(solution)/shard_map/ppermute | solution.py:309
  4.4 38.6 %collective-permute-start.1 = (bf16[128,1024]{1,0:T(8,128)(2,1)}, bf16[128,1024]{1,0:T(8,128)(2,1)S(1)}, u32[]{:S(2)}, u32[]{:S(2)}) collective-permute-start(bf16[128,1024]{1,0:T(8,128)(2,1)} %bitcast.39), channel_id=1, source_target_pairs={{0,2},{1,3},{2,0},{3,1},{4,6},{5,7},{6,4},{7,5},{8,10},{9,11},{10,... | collective-permute-start | bytes 786440 | tf_op jit(solution)/shard_map/ppermute | solution.py:309
  6.8 36.1 %collective-permute-start = (bf16[128,1024]{1,0:T(8,128)(2,1)}, bf16[128,1024]{1,0:T(8,128)(2,1)S(1)}, u32[]{:S(2)}, u32[]{:S(2)}) collective-permute-start(bf16[128,1024]{1,0:T(8,128)(2,1)} %bitcast.40), channel_id=1, source_target_pairs={{0,1},{1,2},{2,3},{3,0},{4,5},{5,6},{6,7},{7,4},{8,9},{9,10},{10,1... | collective-permute-start | bytes 786440 | tf_op jit(solution)/shard_map/ppermute | solution.py:309
  10.8 18.0 %all-to-all-start = ((bf16[8,16,256]{2,0,1:T(8,128)(2,1)}), bf16[8,16,256]{2,0,1:T(8,128)(2,1)S(1)}, u32[]{:S(2)}, u32[]{:S(2)}) async-start(bf16[8,16,256]{2,0,1:T(8,128)(2,1)} %copy.11), calls=%async_computation | async-start | bytes 131072 | tf_op jit(solution)/shard_map/all_to_all | solution.py:312
  20.3 0.7 copy-start.3
  21.0 0.7 copy-start.4
  21.8 0.7 copy-start.5
  22.5 0.7 copy-start.6
  23.2 19.8 %copy-start.1 = (bf16[1,1024,256]{2,1,0:T(8,128)(2,1)S(1)}, bf16[1,1024,256]{2,1,0:T(8,128)(2,1)}, u32[]{:S(2)}) copy-start(bf16[1,1024,256]{2,1,0:T(8,128)(2,1)} %param.11) | copy-start | bytes 1572868
  23.2 19.8 %copy-start.2 = (bf16[1,128,1024]{2,1,0:T(8,128)(2,1)S(1)}, bf16[1,128,1024]{2,1,0:T(8,128)(2,1)}, u32[]{:S(2)}) copy-start(bf16[1,128,1024]{2,1,0:T(8,128)(2,1)} %param.10) | copy-start | bytes 786436
  29.8 13.0 %all-to-all-start.1 = ((bf16[4,496,128]{2,1,0:T(8,128)(2,1)}), bf16[4,496,128]{2,1,0:T(8,128)(2,1)S(1)}, u32[]{:S(2)}, u32[]{:S(2)}) async-start(bf16[4,496,128]{2,1,0:T(8,128)(2,1)} %pad_maximum_fusion), calls=%async_computation.1 | async-start | bytes 1015808 | tf_op jit(solution)/shard_map/all_to_all | solution.py:330
  43.0 3.4 %copy-start = (bf16[1,4096,1024]{2,1,0:T(8,128)(2,1)S(1)}, bf16[1,4096,1024]{2,1,0:T(8,128)(2,1)}, u32[]{:S(2)}) copy-start(bf16[1,4096,1024]{2,1,0:T(8,128)(2,1)} %param.12) | copy-start | bytes 25165828
  66.0 27.4 %all-to-all-start.2 = ((bf16[8,256,128]{2,1,0:T(8,128)(2,1)}), bf16[8,256,128]{2,1,0:T(8,128)(2,1)S(1)}, u32[]{:S(2)}, u32[]{:S(2)}) async-start(bf16[8,256,128]{2,1,0:T(8,128)(2,1)} %get-tuple-element.7), calls=%async_computation.2 | async-start | bytes 1048576 | tf_op jit(solution)/shard_map/all_to_all | solution.py:348
  93.4 24.9 %all-to-all-start.3 = ((bf16[8,256,128]{2,1,0:T(8,128)(2,1)}), bf16[8,256,128]{2,1,0:T(8,128)(2,1)S(1)}, u32[]{:S(2)}, u32[]{:S(2)}) async-start(bf16[8,256,128]{2,1,0:T(8,128)(2,1)} %shard_map.93), calls=%async_computation.3 | async-start | bytes 1048576 | tf_op jit(solution)/shard_map/all_to_all | solution.py:349

commit v3 on v2

v3 whole, which is shorter than its diff:
```python
import functools

import jax
import jax.numpy as jnp
from jax import lax
from jax.experimental import pallas as pl
from jax.experimental.pallas import tpu as pltpu
from jax.sharding import Mesh
from jax.sharding import PartitionSpec as P

E = 128
FEAT = 32
SAMP = 128
HID = 1024
TOUT = 256
TIN = 4096
ROW_DEV = 512
ELEMS = 5120
CAP = 320
NX = 4
NZ = 8
HALVES = 2
HALF = ROW_DEV // HALVES
BUCKETS = NZ * HALVES
SUBS = NX * BUCKETS
PIECES = 5
SLOTS = 384
LANES = 128
CHUNKS = SLOTS // LANES
USED = 120
STEP = 512
UNROLL = 16
BF = jnp.bfloat16
F32 = jnp.float32
I32 = jnp.int32
NT = (((1,), (1,)), ((), ()))


def in_hbm(operand):
    return pltpu.with_memory_space_constraint(operand, pltpu.HBM)


def in_vmem(operand):
    return pltpu.with_memory_space_constraint(operand, pltpu.VMEM)


def bucket_kernel(
    seg_ref,
    weight_ref,
    owner_ref,
    row_ref,
    slot_ref,
    up_hbm_ref,
    after_ref,
    out_ref,
    up_ref,
    acc_ref,
    up_sem,
):
    del after_ref
    up_copy = pltpu.make_async_copy(up_hbm_ref, up_ref, up_sem)
    up_copy.start()
    square = (FEAT, FEAT)
    diagonal = lax.broadcasted_iota(I32, square, 0) == lax.broadcasted_iota(I32, square, 1)
    slots = jnp.sum(
        jnp.where(diagonal, slot_ref[...].astype(F32), 0.0), axis=1, keepdims=True
    )
    upper = (
        lax.broadcasted_iota(I32, (STEP, STEP), 0) <= lax.broadcasted_iota(I32, (STEP, STEP), 1)
    ).astype(F32).astype(BF)
    sub_ids = lax.broadcasted_iota(I32, (SUBS, STEP), 0)
    feat_ids = lax.broadcasted_iota(I32, (FEAT, STEP), 0)
    slot_ids = lax.broadcasted_iota(I32, (SLOTS, STEP), 0).astype(F32)
    acc_ref[...] = jnp.zeros_like(acc_ref)

    def step(k, carry):
        cols = pl.ds(pl.multiple_of(k * STEP, STEP), STEP)
        seg = seg_ref[:, cols]
        weight = weight_ref[:, cols]
        owner = owner_ref[:, cols]
        row = row_ref[:, cols]
        sub = (owner & 3) * BUCKETS + (row >> 8) * NZ + (owner >> 2)
        mine = sub_ids == sub
        ones = jnp.where(mine, 1.0, 0.0)
        inclusive = jnp.dot(ones.astype(BF), upper, preferred_element_type=F32) + carry
        rank = jnp.sum(ones * inclusive, axis=0, keepdims=True) - 1.0
        block = jnp.sum(
            jnp.where(feat_ids == (seg & 31), slots, 0.0), axis=0, keepdims=True
        )
        sample = (seg >> 5).astype(F32)
        row_next = ((row & 255) + 1).astype(F32)
        high = weight.astype(BF).astype(F32)
        rest = weight - high
        middle = rest.astype(BF).astype(F32)
        pieces = (block, sample, row_next, high, middle)
        left = jnp.concatenate([(ones * piece).astype(BF) for piece in pieces], axis=0)
        place = rank
        for c in range(1, CHUNKS):
            place = place + jnp.where(rank >= c * USED, float(LANES - USED), 0.0)
        right = jnp.where(slot_ids == place, 1.0, 0.0).astype(BF)
        acc_ref[...] += lax.dot_general(left, right, NT, preferred_element_type=F32)
        return inclusive[:, STEP - 1 : STEP]

    count = lax.fori_loop(0, ELEMS // STEP, step, jnp.zeros((SUBS, 1), F32), unroll=10)
    count = jnp.broadcast_to(count.astype(I32), (SUBS, LANES))
    count_parts = ((count >> 7).astype(F32), (count & 127).astype(F32))
    spare = lax.broadcasted_iota(I32, (SUBS, LANES), 1) >= USED
    for p in range(PIECES):
        for c in range(CHUNKS):
            part = acc_ref[p * SUBS : (p + 1) * SUBS, c * LANES : (c + 1) * LANES]
            if p < 2 and c == 0:
                part = jnp.where(spare, count_parts[p], part)
            part = part.astype(BF)
            for x in range(NX):
                out_ref[x, p, c] = part[x * BUCKETS : (x + 1) * BUCKETS]
    up_copy.wait()


def bucket_elements(segment, weight, owner, row, slots, up, after):
    vmem = pl.BlockSpec(memory_space=pltpu.VMEM)
    operands = (segment, weight, owner, row, slots, up)
    return pl.pallas_call(
        bucket_kernel,
        out_shape=(
            jax.ShapeDtypeStruct((NX, PIECES, CHUNKS, BUCKETS, LANES), BF),
            pltpu.VMEM((TIN, HID), BF),
        ),
        in_specs=[vmem] * 5
        + [pl.BlockSpec(memory_space=pltpu.HBM), pl.BlockSpec(memory_space=pl.ANY)],
        out_specs=(vmem, vmem),
        scratch_shapes=[pltpu.VMEM((PIECES * SUBS, SLOTS), F32), pltpu.SemaphoreType.DMA],
        compiler_params=pltpu.CompilerParams(vmem_limit_bytes=24 << 20),
        cost_estimate=pl.CostEstimate(flops=3 << 30, bytes_accessed=9 << 20, transcendentals=0),
    )(*[in_hbm(operand) for operand in operands], after)


def chosen(rows):
    row_ids = lax.broadcasted_iota(I32, (HALF, rows.shape[1]), 0) + 1
    return jnp.where(row_ids == rows, 1.0, 0.0).astype(BF)


def table_kernel(
    half,
    index_hbm_ref,
    weight_ref,
    row_ref,
    pooled_ref,
    out_ref,
    group_ref,
    spill_ref,
    total_ref,
    index_ref,
    index_sems,
):
    part = NZ * LANES

    def index_copy(c, x):
        start = ((x * CHUNKS + c) * BUCKETS + half * NZ) * LANES
        return pltpu.make_async_copy(
            index_hbm_ref.at[pl.ds(start, part)],
            index_ref.at[pl.ds((c * NX + x) * part, part)],
            index_sems.at[c, x],
        )

    for c in range(CHUNKS):
        for x in range(NX):
            index_copy(c, x).start()
    group_ref[...] = jnp.zeros_like(group_ref)
    spill_ref[...] = jnp.zeros_like(spill_ref)

    def vector_row(c, x, o):
        return pl.ds((x * CHUNKS + c) * BUCKETS + half * NZ + o, 1)

    def index_row(c, x, o):
        return ((c * NX + x) * NZ + o) * LANES

    def fetch(source_row, count, shift, target_ref, start):
        def some(j, unused):
            source = source_row + j * UNROLL
            target = pl.multiple_of(start + j * UNROLL, UNROLL)
            for u in range(UNROLL):
                target_ref[pl.ds(target + u, 1), :] = pooled_ref[
                    pl.ds(index_ref[source + u] + shift, 1), :
                ]
            return unused

        lax.fori_loop(0, (count + (UNROLL - 1)) // UNROLL, some, 0)

    for x in range(NX):
        index_copy(0, x).wait()

        def bucket_step(o, unused, x=x):
            row = index_row(0, x, o)
            count = jnp.minimum(index_ref[row + USED], USED)
            fetch(row, count, x * (FEAT * SAMP), group_ref, (o * NX + x) * LANES)
            return unused

        lax.fori_loop(0, NZ, bucket_step, 0)
    blank = jnp.zeros((8 - NX, LANES), F32)
    for o in range(NZ):
        rows = jnp.concatenate([row_ref[vector_row(0, x, o), :] for x in range(NX)], axis=1)
        weights = [weight_ref[vector_row(0, x, o), :] for x in range(NX)]
        columns = jnp.concatenate([*weights, blank], axis=0).T
        values = []
        for x in range(NX):
            start = (o * NX + x) * LANES
            values.append(group_ref[start : start + LANES, :] * columns[:, x : x + 1])
        values = jnp.concatenate(values, axis=0).astype(BF)
        total_ref[o] = jnp.dot(chosen(rows), values, preferred_element_type=F32)
    for c in range(1, CHUNKS):
        for x in range(NX):
            index_copy(c, x).wait()

    def spill_step(i, unused):
        x, o = i & (NX - 1), i >> 2
        count = index_ref[index_row(0, x, o) + USED]

        def chunk_step(c, unused):
            rest = jnp.minimum(count - c * USED, USED)
            fetch(index_row(c, x, o), rest, x * (FEAT * SAMP), spill_ref, 0)
            weight = weight_ref[vector_row(c, x, o), :]
            column = jnp.broadcast_to(weight, (8, LANES)).T[:, :1]
            total_ref[o] += jnp.dot(
                chosen(row_ref[vector_row(c, x, o), :]),
                (spill_ref[...] * column).astype(BF),
                preferred_element_type=F32,
            )
            return unused

        return lax.fori_loop(1, (count + (USED - 1)) // USED, chunk_step, unused)

    lax.fori_loop(0, NX * NZ, spill_step, 0)
    out_ref[...] = total_ref[...].astype(BF)


def half_tables(half, index, weight, rows, pooled):
    hbm = pl.BlockSpec(memory_space=pltpu.HBM)
    vmem = pl.BlockSpec(memory_space=pltpu.VMEM)
    return pl.pallas_call(
        functools.partial(table_kernel, half),
        out_shape=jax.ShapeDtypeStruct((NZ, HALF, E), BF),
        in_specs=[hbm, vmem, vmem, vmem],
        out_specs=vmem,
        scratch_shapes=[
            pltpu.VMEM((NZ * NX * LANES, E), F32),
            pltpu.VMEM((LANES, E), F32),
            pltpu.VMEM((NZ, HALF, E), F32),
            pltpu.SMEM((CHUNKS * NX * NZ * LANES,), I32),
            pltpu.SemaphoreType.DMA((CHUNKS, NX)),
        ],
        compiler_params=pltpu.CompilerParams(vmem_limit_bytes=24 << 20),
        cost_estimate=pl.CostEstimate(flops=5 << 30, bytes_accessed=10 << 20, transcendentals=0),
    )(in_hbm(index), weight, rows, in_vmem(pooled))


UP_STEP = 1024
UP_STEPS = TIN // UP_STEP
UP_PART = 512


def pooled_kernel(
    me_ref,
    grad_ref,
    hidden0_ref,
    hidden1_ref,
    hidden2_ref,
    hidden3_ref,
    down_ref,
    up_ref,
    pooled_ref,
    hid_ref,
):
    for r, hidden_ref in enumerate((hidden0_ref, hidden1_ref, hidden2_ref, hidden3_ref)):
        x = (me_ref[0] + (NX - r)) & (NX - 1)
        backward = lax.dot_general(grad_ref[x], down_ref[...], NT, preferred_element_type=F32)
        keep = hidden_ref[...].astype(F32) > 0
        there = pl.ds(pl.multiple_of(x * SAMP, SAMP), SAMP)
        hid_ref[there, :] = jnp.where(keep, backward, 0.0).astype(BF)

    def up_step(k, unused):
        for j in range(UP_STEP // UP_PART):
            rows = pl.ds(pl.multiple_of(k * UP_STEP + j * UP_PART, UP_PART), UP_PART)
            result = lax.dot_general(
                hid_ref[...], up_ref[rows, :], NT, preferred_element_type=F32
            )
            result = result.astype(BF).astype(F32)
            for x in range(NX):
                for i in range(UP_PART // E):
                    block = (k * UP_STEP + j * UP_PART) // E + i
                    start = pl.multiple_of((x * FEAT + block) * SAMP, SAMP)
                    pooled_ref[pl.ds(start, SAMP), :] = result[
                        x * SAMP : (x + 1) * SAMP, i * E : (i + 1) * E
                    ]
        return unused

    lax.fori_loop(0, UP_STEPS, up_step, 0)


def pooled_gradients(me, grads, hiddens, down, up):
    vmem = pl.BlockSpec(memory_space=pltpu.VMEM)
    smem = pl.BlockSpec(memory_space=pltpu.SMEM)
    return pl.pallas_call(
        pooled_kernel,
        out_shape=pltpu.VMEM((NX * FEAT * SAMP, E), F32),
        in_specs=[smem, vmem, *[vmem] * NX, vmem, vmem],
        out_specs=vmem,
        scratch_shapes=[pltpu.VMEM((NX * SAMP, HID), BF)],
        compiler_params=pltpu.CompilerParams(vmem_limit_bytes=24 << 20),
        cost_estimate=pl.CostEstimate(flops=5 << 30, bytes_accessed=20 << 20, transcendentals=0),
    )(me, grads, *hiddens, down, in_vmem(up))


def local(
    out_grad,
    hidden_pre,
    down_proj,
    up_proj,
    feature_slot,
    element_segment,
    element_weight,
    row_owner,
    row_local,
):
    hidden = hidden_pre[0]
    hiddens = [hidden] + [
        lax.ppermute(hidden, "x", [(i, (i + shift) % NX) for i in range(NX)])
        for shift in range(1, NX)
    ]
    arrived = lax.all_to_all(out_grad, "tower", split_axis=1, concat_axis=0, tiled=True)
    swap_x = functools.partial(
        lax.all_to_all, axis_name="x", split_axis=0, concat_axis=0, tiled=True
    )
    grads = swap_x(jnp.broadcast_to(arrived.reshape(1, SAMP, TOUT), (NX, SAMP, TOUT)))
    flat = (1, ELEMS)
    buckets, up = bucket_elements(
        element_segment.reshape(flat),
        element_weight.reshape(flat),
        row_owner.reshape(flat),
        row_local.reshape(flat),
        feature_slot,
        up_proj[0],
        arrived,
    )
    buckets = swap_x(buckets)
    parts = buckets.reshape(NX, PIECES, CHUNKS * BUCKETS, LANES).astype(F32)
    index = (parts[:, 0] * SAMP + parts[:, 1]).astype(I32).reshape(-1)
    rows = parts[:, 2].astype(I32).reshape(NX * CHUNKS * BUCKETS, LANES)
    weight = (parts[:, 3] + parts[:, 4]).reshape(NX * CHUNKS * BUCKETS, LANES)
    me = lax.axis_index("x").astype(I32).reshape(1)
    pooled = pooled_gradients(me, grads, hiddens, down_proj[0], up)
    swap = functools.partial(
        lax.all_to_all, axis_name="z", split_axis=0, concat_axis=0, tiled=True
    )
    first = swap(half_tables(0, index, weight, rows, pooled))
    second = swap(half_tables(1, index, weight, rows, pooled))
    table_grad = jnp.concatenate(
        [jnp.sum(first.astype(F32), axis=0), jnp.sum(second.astype(F32), axis=0)], axis=0
    )
    return table_grad.reshape(1, ROW_DEV, E)


def solution(mesh):
    towers = mesh.shape["tower"]
    grid = Mesh(mesh.devices.reshape(towers, NZ, NX), ("tower", "z", "x"))
    shard = ("z", "x")
    in_specs = (
        P(("tower", "z", "x"), None, None),
        P("tower", shard, None),
        P("tower", None, None),
        P("tower", None, None),
        P("tower", None),
        P("tower", shard, None),
        P("tower", shard, None),
        P("tower", shard, None, None),
        P("tower", shard, None),
    )
    out_specs = P("tower", shard, None)
    return jax.shard_map(local, mesh=grid, in_specs=in_specs, out_specs=out_specs, check_vma=False)
```

time: 120 us -> 124 us (1.033)
  the two profiles are of different devices: /device:TPU:9 before, /device:TPU:8 now
where the time goes in v3:
time: 124 us; the launch traced here: 123 us
  starting transfers between devices  37.4 us (30%)
  Pallas kernels  33.9 us (27%)
  waiting for transfers between devices  20.3 us (16%)
  local copies, waits for them, and re-layouts  15 us (12%)
  blocking collectives  14.8 us (12%)
  other arithmetic  1.59 us (1%)
    pallas_call x2, Pallas kernels, half_tables(): pl.pallas_call(functools.partial(table_kernel, half), out_shape=jax.Shape...  22.3 us
    all_to_all x1, blocking collectives, local(): lax.all_to_all(out_grad, 'tower', split_axis=1, concat_axis=0, tiled=True)  14.8 us
    unnamed x13, local copies, waits for them, and re-layouts  14.1 us
    all_to_all x1, waiting for transfers between devices, local(): second = swap(half_tables(1, index, weight, rows, pooled))  14.1 us
    ppermute x3, starting transfers between devices, local(): lax.ppermute(hidden, 'x', [(i, (i + shift) % NX) for i in range(NX)])  11.8 us
    all_to_all x1, starting transfers between devices, local(): first = swap(half_tables(0, index, weight, rows, pooled))  11 us
    all_to_all x1, starting transfers between devices, local(): second = swap(half_tables(1, index, weight, rows, pooled))  7.71 us
    pallas_call x1, Pallas kernels, pooled_gradients(): pl.pallas_call(pooled_kernel, out_shape=pltpu.VMEM((NX * FEAT * SAMP, E),...  6.01 us
  transfers between devices with their start and end apart: 7, of which 5 were waited for; matrix products, arithmetic and copies ran while one was open for 1% of the time, Pallas kernels for 9%

profile of v3, /device:TPU:8, one launch (start us, length us, event | category | flops | bytes accessed | tf_op | source)
XLA Modules:
  0.0 123.1 jit_solution(4159440635932573662)
XLA Ops:
  0.0 0.9 copy.14
  0.9 14.8 %all_to_all.38 = bf16[8,16,256]{2,0,1:T(8,128)(2,1)S(1)} all-to-all(bf16[8,16,256]{2,0,1:T(8,128)(2,1)S(1)} %copy.14), channel_id=1, replica_groups=mesh['tower'=16,'z'=8,'x'=4] {'tower'}, dimensions={1} | all-to-all | bytes 131072 | tf_op jit(solution)/shard_map/all_to_all | solution.py:329
  15.8 0.1 copy.15.after_ref
  15.9 5.7 %shard_map.91 = (bf16[4,5,3,16,128]{4,3,2,1,0:T(8,128)(2,1)}, bf16[4096,1024]{1,0:T(8,128)(2,1)S(1)}) custom-call(s32[1,5120]{1,0:T(1,128)} %bitcast.49, f32[1,5120]{1,0:T(1,128)} %bitcast.50, s32[1,5120]{1,0:T(1,128)} %bitcast.51, s32[1,5120]{1,0:T(1,128)} %bitcast.52, s32[1,32]{1,0:T(1,128)} %slot_ref.1, bf16[4096,1024]{1,0:T(8,128)(2,1)} %bitcast.48, ...), custom_call_target="tpu_custom_call" | custom-call | flops 3221225472 | bytes 9437184 | tf_op jit(solution)/shard_map/pallas_call | solution.py:122
  21.5 0.0 copy-start.2
  21.6 3.2 %copy-done.2 = bf16[4096,1024]{1,0:T(8,128)(2,1)} copy-done((bf16[4096,1024]{1,0:T(8,128)(2,1)}, bf16[4096,1024]{1,0:T(8,128)(2,1)S(1)}, u32[]{:S(2)}) %copy-start.2) | copy-done | bytes 8388632
  24.8 3.4 %all-to-all-start.1 = ((bf16[4,5,3,16,128]{4,3,2,1,0:T(8,128)(2,1)}), bf16[4,5,3,16,128]{4,3,2,1,0:T(8,128)(2,1)S(1)}, u32[]{:S(2)}, u32[]{:S(2)}) async-start(bf16[4,5,3,16,128]{4,3,2,1,0:T(8,128)(2,1)} %get-tuple-element.7), calls=%async_computation.1 | async-start | bytes 491520 | tf_op jit(solution)/shard_map/all_to_all | solution.py:344
  28.2 3.9 %collective-permute-start = (bf16[128,1024]{1,0:T(8,128)(2,1)S(1)}, bf16[128,1024]{1,0:T(8,128)(2,1)S(1)}, u32[]{:S(2)}, u32[]{:S(2)}) collective-permute-start(bf16[128,1024]{1,0:T(8,128)(2,1)S(1)} %bitcast.40), channel_id=1, source_target_pairs={{0,1},{1,2},{2,3},{3,0},{4,5},{5,6},{6,7},{7,4},{8,9},{9,10},{10,1... | collective-permute-start | bytes 786440 | tf_op jit(solution)/shard_map/ppermute | solution.py:326
  32.1 4.6 %collective-permute-start.1 = (bf16[128,1024]{1,0:T(8,128)(2,1)S(1)}, bf16[128,1024]{1,0:T(8,128)(2,1)S(1)}, u32[]{:S(2)}, u32[]{:S(2)}) collective-permute-start(bf16[128,1024]{1,0:T(8,128)(2,1)S(1)} %bitcast.41), channel_id=1, source_target_pairs={{0,2},{1,3},{2,0},{3,1},{4,6},{5,7},{6,4},{7,5},{8,10},{9,11},{10,... | collective-permute-start | bytes 786440 | tf_op jit(solution)/shard_map/ppermute | solution.py:326
  36.7 3.4 %collective-permute-start.2 = (bf16[128,1024]{1,0:T(8,128)(2,1)S(1)}, bf16[128,1024]{1,0:T(8,128)(2,1)S(1)}, u32[]{:S(2)}, u32[]{:S(2)}) collective-permute-start(bf16[128,1024]{1,0:T(8,128)(2,1)S(1)} %bitcast.42), channel_id=1, source_target_pairs={{0,3},{1,0},{2,1},{3,2},{4,7},{5,4},{6,5},{7,6},{8,11},{9,8},{10,9... | collective-permute-start | bytes 786440 | tf_op jit(solution)/shard_map/ppermute | solution.py:326
  40.0 0.0 all-to-all-done.1
  40.1 0.7 broadcast_in_dim.8
  40.8 3.4 %all-to-all-start.2 = ((bf16[4,128,256]{2,1,0:T(8,128)(2,1)}), bf16[4,128,256]{2,1,0:T(8,128)(2,1)S(1)}, u32[]{:S(2)}, u32[]{:S(2)}) async-start(bf16[4,128,256]{2,1,0:T(8,128)(2,1)} %broadcast_in_dim.8), calls=%async_computation.2 | async-start | bytes 524288 | tf_op jit(solution)/shard_map/all_to_all | solution.py:333
  44.2 0.1 bitcast_convert_fusion
  44.3 0.7 fusion
  44.9 0.0 collective-permute-done.hidden1_ref
  44.9 1.6 %collective-permute-done.1.hidden2_ref = bf16[128,1024]{1,0:T(8,128)(2,1)S(1)} collective-permute-done((bf16[128,1024]{1,0:T(8,128)(2,1)S(1)}, bf16[128,1024]{1,0:T(8,128)(2,1)S(1)}, u32[]{:S(2)}, u32[]{:S(2)}) %collective-permute-start.1) | collective-permute-done | bytes 262176 | tf_op jit(solution)/shard_map/ppermute | solution.py:326
  46.5 2.3 %collective-permute-done.2.hidden3_ref = bf16[128,1024]{1,0:T(8,128)(2,1)S(1)} collective-permute-done((bf16[128,1024]{1,0:T(8,128)(2,1)S(1)}, bf16[128,1024]{1,0:T(8,128)(2,1)S(1)}, u32[]{:S(2)}, u32[]{:S(2)}) %collective-permute-start.2) | collective-permute-done | bytes 262176 | tf_op jit(solution)/shard_map/ppermute | solution.py:326
  48.9 2.0 %all-to-all-done.2.grad_ref = bf16[4,128,256]{2,1,0:T(8,128)(2,1)S(1)} async-done(((bf16[4,128,256]{2,1,0:T(8,128)(2,1)}), bf16[4,128,256]{2,1,0:T(8,128)(2,1)S(1)}, u32[]{:S(2)}, u32[]{:S(2)}) %all-to-all-start.2) | async-done | bytes 262176 | tf_op jit(solution)/shard_map/all_to_all | solution.py:333
  50.8 3.4 %copy-done.3 = bf16[4096,1024]{1,0:T(8,128)(2,1)S(1)} copy-done((bf16[4096,1024]{1,0:T(8,128)(2,1)S(1)}, bf16[4096,1024]{1,0:T(8,128)(2,1)}, u32[]{:S(2)}) %copy-start.3) | copy-done | bytes 8388632
  54.2 6.0 %shard_map.92.pooled_ref = f32[16384,128]{1,0:T(8,128)S(1)} custom-call(s32[1]{0:T(128)} %bitcast.13.me_ref, bf16[4,128,256]{2,1,0:T(8,128)(2,1)S(1)} %all-to-all-done.2.grad_ref, bf16[128,1024]{1,0:T(8,128)(2,1)S(1)} %bitcast.43, bf16[128,1024]{1,0:T(8,128)(2,1)S(1)} %collective-permute-done.hidden1_ref, ...), custom_call_target="tpu_custom_call" | custom-call | flops 5368709120 | bytes 20971520 | tf_op jit(solution)/shard_map/pallas_call | solution.py:302
  60.2 11.0 %shard_map.93 = bf16[8,256,128]{2,1,0:T(8,128)(2,1)} custom-call(s32[24576]{0:T(1024)} %bitcast.46, f32[192,128]{1,0:T(8,128)S(1)} %bitcast.35, s32[192,128]{1,0:T(8,128)S(1)} %bitcast.37, f32[16384,128]{1,0:T(8,128)S(1)} %shard_map.92.pooled_ref), custom_call_target="tpu_custom_call" | custom-call | flops 5368709120 | bytes 10485760 | tf_op jit(solution)/shard_map/pallas_call | solution.py:239
  71.3 3.2 %copy-done.4 = f32[16384,128]{1,0:T(8,128)} copy-done((f32[16384,128]{1,0:T(8,128)}, f32[16384,128]{1,0:T(8,128)S(1)}, u32[]{:S(2)}) %copy-start.4) | copy-done | bytes 8388632
  74.5 11.0 %all-to-all-start.3 = ((bf16[8,256,128]{2,1,0:T(8,128)(2,1)}), bf16[8,256,128]{2,1,0:T(8,128)(2,1)S(1)}, u32[]{:S(2)}, u32[]{:S(2)}) async-start(bf16[8,256,128]{2,1,0:T(8,128)(2,1)} %shard_map.93), calls=%async_computation.3 | async-start | bytes 1048576 | tf_op jit(solution)/shard_map/all_to_all | solution.py:354
  85.5 3.4 %copy-done.5 = f32[16384,128]{1,0:T(8,128)S(1)} copy-done((f32[16384,128]{1,0:T(8,128)S(1)}, f32[16384,128]{1,0:T(8,128)}, u32[]{:S(2)}) %copy-start.5) | copy-done | bytes 8388632
  88.9 11.3 %shard_map.94 = bf16[8,256,128]{2,1,0:T(8,128)(2,1)} custom-call(s32[24576]{0:T(1024)} %bitcast.47, f32[192,128]{1,0:T(8,128)S(1)} %bitcast.36, s32[192,128]{1,0:T(8,128)S(1)} %bitcast.38, f32[16384,128]{1,0:T(8,128)S(1)} %copy-done.5), custom_call_target="tpu_custom_call" | custom-call | flops 5368709120 | bytes 10485760 | tf_op jit(solution)/shard_map/pallas_call | solution.py:239
  100.1 0.3 all-to-all-done.3
  100.4 7.7 %all-to-all-start.4 = ((bf16[8,256,128]{2,1,0:T(8,128)(2,1)}), bf16[8,256,128]{2,1,0:T(8,128)(2,1)S(1)}, u32[]{:S(2)}, u32[]{:S(2)}) async-start(bf16[8,256,128]{2,1,0:T(8,128)(2,1)} %shard_map.94), calls=%async_computation.4 | async-start | bytes 1048576 | tf_op jit(solution)/shard_map/all_to_all | solution.py:355
  108.1 0.1 convert_reduce_fusion.1
  108.2 14.1 %all-to-all-done.4 = bf16[8,256,128]{2,1,0:T(8,128)(2,1)S(1)} async-done(((bf16[8,256,128]{2,1,0:T(8,128)(2,1)}), bf16[8,256,128]{2,1,0:T(8,128)(2,1)S(1)}, u32[]{:S(2)}, u32[]{:S(2)}) %all-to-all-start.4) | async-done | bytes 524320 | tf_op jit(solution)/shard_map/all_to_all | solution.py:355
  122.3 0.1 convert_reduce_fusion
  122.4 0.7 maximum_bitcast_fusion
  (8 shorter events, 0.0 us)
Async XLA Ops:
  0.0 28.2 %copy-start.1 = (bf16[1,128,1024]{2,1,0:T(8,128)(2,1)S(1)}, bf16[1,128,1024]{2,1,0:T(8,128)(2,1)}, u32[]{:S(2)}) copy-start(bf16[1,128,1024]{2,1,0:T(8,128)(2,1)} %param.10) | copy-start | bytes 786436
  0.0 50.8 %copy-start = (bf16[1,1024,256]{2,1,0:T(8,128)(2,1)S(1)}, bf16[1,1024,256]{2,1,0:T(8,128)(2,1)}, u32[]{:S(2)}) copy-start(bf16[1,1024,256]{2,1,0:T(8,128)(2,1)} %param.11) | copy-start | bytes 1572868
  21.5 3.2 %copy-start.2 = (bf16[4096,1024]{1,0:T(8,128)(2,1)}, bf16[4096,1024]{1,0:T(8,128)(2,1)S(1)}, u32[]{:S(2)}) copy-start(bf16[4096,1024]{1,0:T(8,128)(2,1)S(1)} %get-tuple-element.8.up_ref) | copy-start | bytes 25165828
  24.8 15.3 %all-to-all-start.1 = ((bf16[4,5,3,16,128]{4,3,2,1,0:T(8,128)(2,1)}), bf16[4,5,3,16,128]{4,3,2,1,0:T(8,128)(2,1)S(1)}, u32[]{:S(2)}, u32[]{:S(2)}) async-start(bf16[4,5,3,16,128]{4,3,2,1,0:T(8,128)(2,1)} %get-tuple-element.7), calls=%async_computation.1 | async-start | bytes 491520 | tf_op jit(solution)/shard_map/all_to_all | solution.py:344
  28.2 16.7 %collective-permute-start = (bf16[128,1024]{1,0:T(8,128)(2,1)S(1)}, bf16[128,1024]{1,0:T(8,128)(2,1)S(1)}, u32[]{:S(2)}, u32[]{:S(2)}) collective-permute-start(bf16[128,1024]{1,0:T(8,128)(2,1)S(1)} %bitcast.40), channel_id=1, source_target_pairs={{0,1},{1,2},{2,3},{3,0},{4,5},{5,6},{6,7},{7,4},{8,9},{9,10},{10,1... | collective-permute-start | bytes 786440 | tf_op jit(solution)/shard_map/ppermute | solution.py:326
  32.1 14.5 %collective-permute-start.1 = (bf16[128,1024]{1,0:T(8,128)(2,1)S(1)}, bf16[128,1024]{1,0:T(8,128)(2,1)S(1)}, u32[]{:S(2)}, u32[]{:S(2)}) collective-permute-start(bf16[128,1024]{1,0:T(8,128)(2,1)S(1)} %bitcast.41), channel_id=1, source_target_pairs={{0,2},{1,3},{2,0},{3,1},{4,6},{5,7},{6,4},{7,5},{8,10},{9,11},{10,... | collective-permute-start | bytes 786440 | tf_op jit(solution)/shard_map/ppermute | solution.py:326
  36.7 12.2 %collective-permute-start.2 = (bf16[128,1024]{1,0:T(8,128)(2,1)S(1)}, bf16[128,1024]{1,0:T(8,128)(2,1)S(1)}, u32[]{:S(2)}, u32[]{:S(2)}) collective-permute-start(bf16[128,1024]{1,0:T(8,128)(2,1)S(1)} %bitcast.42), channel_id=1, source_target_pairs={{0,3},{1,0},{2,1},{3,2},{4,7},{5,4},{6,5},{7,6},{8,11},{9,8},{10,9... | collective-permute-start | bytes 786440 | tf_op jit(solution)/shard_map/ppermute | solution.py:326
  40.8 10.1 %all-to-all-start.2 = ((bf16[4,128,256]{2,1,0:T(8,128)(2,1)}), bf16[4,128,256]{2,1,0:T(8,128)(2,1)S(1)}, u32[]{:S(2)}, u32[]{:S(2)}) async-start(bf16[4,128,256]{2,1,0:T(8,128)(2,1)} %broadcast_in_dim.8), calls=%async_computation.2 | async-start | bytes 524288 | tf_op jit(solution)/shard_map/all_to_all | solution.py:333
  50.8 3.4 %copy-start.3 = (bf16[4096,1024]{1,0:T(8,128)(2,1)S(1)}, bf16[4096,1024]{1,0:T(8,128)(2,1)}, u32[]{:S(2)}) copy-start(bf16[4096,1024]{1,0:T(8,128)(2,1)} %copy-done.2) | copy-start | bytes 25165828
  71.2 3.2 %copy-start.4 = (f32[16384,128]{1,0:T(8,128)}, f32[16384,128]{1,0:T(8,128)S(1)}, u32[]{:S(2)}) copy-start(f32[16384,128]{1,0:T(8,128)S(1)} %shard_map.92.pooled_ref) | copy-start | bytes 25165828
  74.5 25.9 %all-to-all-start.3 = ((bf16[8,256,128]{2,1,0:T(8,128)(2,1)}), bf16[8,256,128]{2,1,0:T(8,128)(2,1)S(1)}, u32[]{:S(2)}, u32[]{:S(2)}) async-start(bf16[8,256,128]{2,1,0:T(8,128)(2,1)} %shard_map.93), calls=%async_computation.3 | async-start | bytes 1048576 | tf_op jit(solution)/shard_map/all_to_all | solution.py:354
  85.5 3.4 %copy-start.5 = (f32[16384,128]{1,0:T(8,128)S(1)}, f32[16384,128]{1,0:T(8,128)}, u32[]{:S(2)}) copy-start(f32[16384,128]{1,0:T(8,128)} %copy-done.4) | copy-start | bytes 25165828
  100.4 21.9 %all-to-all-start.4 = ((bf16[8,256,128]{2,1,0:T(8,128)(2,1)}), bf16[8,256,128]{2,1,0:T(8,128)(2,1)S(1)}, u32[]{:S(2)}, u32[]{:S(2)}) async-start(bf16[8,256,128]{2,1,0:T(8,128)(2,1)} %shard_map.94), calls=%async_computation.4 | async-start | bytes 1048576 | tf_op jit(solution)/shard_map/all_to_all | solution.py:355

commit v4 on v3

v4 whole, which is shorter than its diff:
```python
import functools

import jax
import jax.numpy as jnp
from jax import lax
from jax.experimental import pallas as pl
from jax.experimental.pallas import tpu as pltpu
from jax.sharding import Mesh
from jax.sharding import PartitionSpec as P

E = 128
FEAT = 32
SAMP = 128
HID = 1024
TOUT = 256
TIN = 4096
ROW_DEV = 512
ELEMS = 5120
CAP = 320
NX = 4
NZ = 8
HALVES = 2
HALF = ROW_DEV // HALVES
BUCKETS = NZ * HALVES
SUBS = NX * BUCKETS
PIECES = 5
SLOTS = 384
LANES = 128
CHUNKS = SLOTS // LANES
USED = 120
STEP = 512
UNROLL = 16
BF = jnp.bfloat16
F32 = jnp.float32
I32 = jnp.int32
NT = (((1,), (1,)), ((), ()))


def in_hbm(operand):
    return pltpu.with_memory_space_constraint(operand, pltpu.HBM)


def bucket_kernel(
    seg_ref,
    weight_ref,
    owner_ref,
    row_ref,
    slot_ref,
    after_ref,
    out_ref,
    acc_ref,
):
    del after_ref
    square = (FEAT, FEAT)
    diagonal = lax.broadcasted_iota(I32, square, 0) == lax.broadcasted_iota(I32, square, 1)
    slots = jnp.sum(
        jnp.where(diagonal, slot_ref[...].astype(F32), 0.0), axis=1, keepdims=True
    )
    upper = (
        lax.broadcasted_iota(I32, (STEP, STEP), 0) <= lax.broadcasted_iota(I32, (STEP, STEP), 1)
    ).astype(F32).astype(BF)
    sub_ids = lax.broadcasted_iota(I32, (SUBS, STEP), 0)
    feat_ids = lax.broadcasted_iota(I32, (FEAT, STEP), 0)
    slot_ids = lax.broadcasted_iota(I32, (SLOTS, STEP), 0).astype(F32)
    acc_ref[...] = jnp.zeros_like(acc_ref)

    def step(k, carry):
        cols = pl.ds(pl.multiple_of(k * STEP, STEP), STEP)
        seg = seg_ref[:, cols]
        weight = weight_ref[:, cols]
        owner = owner_ref[:, cols]
        row = row_ref[:, cols]
        sub = (owner & 3) * BUCKETS + (row >> 8) * NZ + (owner >> 2)
        mine = sub_ids == sub
        ones = jnp.where(mine, 1.0, 0.0)
        inclusive = jnp.dot(ones.astype(BF), upper, preferred_element_type=F32) + carry
        rank = jnp.sum(ones * inclusive, axis=0, keepdims=True) - 1.0
        block = jnp.sum(
            jnp.where(feat_ids == (seg & 31), slots, 0.0), axis=0, keepdims=True
        )
        sample = (seg >> 5).astype(F32)
        row_next = ((row & 255) + 1).astype(F32)
        high = weight.astype(BF).astype(F32)
        rest = weight - high
        middle = rest.astype(BF).astype(F32)
        pieces = (block, sample, row_next, high, middle)
        left = jnp.concatenate([(ones * piece).astype(BF) for piece in pieces], axis=0)
        place = rank
        for c in range(1, CHUNKS):
            place = place + jnp.where(rank >= c * USED, float(LANES - USED), 0.0)
        right = jnp.where(slot_ids == place, 1.0, 0.0).astype(BF)
        acc_ref[...] += lax.dot_general(left, right, NT, preferred_element_type=F32)
        return inclusive[:, STEP - 1 : STEP]

    count = lax.fori_loop(0, ELEMS // STEP, step, jnp.zeros((SUBS, 1), F32), unroll=10)
    count = jnp.broadcast_to(count.astype(I32), (SUBS, LANES))
    count_parts = ((count >> 7).astype(F32), (count & 127).astype(F32))
    spare = lax.broadcasted_iota(I32, (SUBS, LANES), 1) >= USED
    for p in range(PIECES):
        for c in range(CHUNKS):
            part = acc_ref[p * SUBS : (p + 1) * SUBS, c * LANES : (c + 1) * LANES]
            if p < 2 and c == 0:
                part = jnp.where(spare, count_parts[p], part)
            part = part.astype(BF)
            for x in range(NX):
                out_ref[x, p, c] = part[x * BUCKETS : (x + 1) * BUCKETS]


def bucket_elements(segment, weight, owner, row, slots, after):
    vmem = pl.BlockSpec(memory_space=pltpu.VMEM)
    operands = (segment, weight, owner, row, slots)
    return pl.pallas_call(
        bucket_kernel,
        out_shape=jax.ShapeDtypeStruct((NX, PIECES, CHUNKS, BUCKETS, LANES), BF),
        in_specs=[vmem] * 5 + [pl.BlockSpec(memory_space=pl.ANY)],
        out_specs=vmem,
        scratch_shapes=[pltpu.VMEM((PIECES * SUBS, SLOTS), F32)],
        compiler_params=pltpu.CompilerParams(vmem_limit_bytes=24 << 20),
        cost_estimate=pl.CostEstimate(flops=3 << 30, bytes_accessed=1 << 20, transcendentals=0),
    )(*[in_hbm(operand) for operand in operands], after)


def chosen(rows):
    row_ids = lax.broadcasted_iota(I32, (HALF, rows.shape[1]), 0) + 1
    return jnp.where(row_ids == rows, 1.0, 0.0).astype(BF)


TABLE_SCRATCH = (
    pltpu.VMEM((NZ * NX * LANES, E), F32),
    pltpu.VMEM((LANES, E), F32),
    pltpu.VMEM((NZ, HALF, E), F32),
    pltpu.SMEM((CHUNKS * NX * NZ * LANES,), I32),
    pltpu.SMEM((NX * NZ + 1,), I32),
    pltpu.SemaphoreType.DMA((CHUNKS, NX)),
)


class Table:
    def __init__(
        self, half, index_hbm_ref, weight_ref, row_ref, pooled_ref, out_ref, scratch
    ):
        self.half = half
        self.pooled_ref = pooled_ref
        self.index_hbm_ref, self.weight_ref, self.row_ref = index_hbm_ref, weight_ref, row_ref
        self.out_ref = out_ref
        self.group_ref, self.spill_ref, self.total_ref = scratch[:3]
        self.index_ref, self.spilled_ref, self.index_sems = scratch[3:]

    def index_copy(self, c, x):
        part = NZ * LANES
        start = ((x * CHUNKS + c) * BUCKETS + self.half * NZ) * LANES
        return pltpu.make_async_copy(
            self.index_hbm_ref.at[pl.ds(start, part)],
            self.index_ref.at[pl.ds((c * NX + x) * part, part)],
            self.index_sems.at[c, x],
        )

    def begin(self):
        for c in range(CHUNKS):
            for x in range(NX):
                self.index_copy(c, x).start()
        self.group_ref[...] = jnp.zeros_like(self.group_ref)
        self.spill_ref[...] = jnp.zeros_like(self.spill_ref)

    def vector_row(self, c, x, o):
        return pl.ds((x * CHUNKS + c) * BUCKETS + self.half * NZ + o, 1)

    def index_row(self, c, x, o):
        return ((c * NX + x) * NZ + o) * LANES

    def fetch(self, source_row, count, shift, target_ref, start):
        def some(j, unused):
            source = source_row + j * UNROLL
            target = pl.multiple_of(start + j * UNROLL, UNROLL)
            for u in range(UNROLL):
                target_ref[pl.ds(target + u, 1), :] = self.pooled_ref[
                    pl.ds(self.index_ref[source + u] + shift, 1), :
                ]
            return unused

        lax.fori_loop(0, (count + (UNROLL - 1)) // UNROLL, some, 0)

    def gather(self, x, spilled):
        self.index_copy(0, x).wait()

        def bucket_step(o, spilled):
            row = self.index_row(0, x, o)
            count = self.index_ref[row + USED]
            start = (o * NX + x) * LANES
            self.fetch(row, jnp.minimum(count, USED), x * (FEAT * SAMP), self.group_ref, start)
            self.spilled_ref[spilled] = o * NX + x
            return spilled + (count > USED).astype(I32)

        return lax.fori_loop(0, NZ, bucket_step, spilled)

    def finish(self, spilled):
        blank = jnp.zeros((8 - NX, LANES), F32)
        for o in range(NZ):
            rows = jnp.concatenate(
                [self.row_ref[self.vector_row(0, x, o), :] for x in range(NX)], axis=1
            )
            weights = [self.weight_ref[self.vector_row(0, x, o), :] for x in range(NX)]
            columns = jnp.concatenate([*weights, blank], axis=0).T
            values = []
            for x in range(NX):
                start = (o * NX + x) * LANES
                values.append(self.group_ref[start : start + LANES, :] * columns[:, x : x + 1])
            values = jnp.concatenate(values, axis=0).astype(BF)
            self.total_ref[o] = jnp.dot(chosen(rows), values, preferred_element_type=F32)
        for c in range(1, CHUNKS):
            for x in range(NX):
                self.index_copy(c, x).wait()

        def spill_step(k, unused):
            i = self.spilled_ref[k]
            x, o = i & (NX - 1), i >> 2
            count = self.index_ref[self.index_row(0, x, o) + USED]

            def chunk_step(c, unused):
                rest = jnp.minimum(count - c * USED, USED)
                self.fetch(self.index_row(c, x, o), rest, x * (FEAT * SAMP), self.spill_ref, 0)
                weight = self.weight_ref[self.vector_row(c, x, o), :]
                column = jnp.broadcast_to(weight, (8, LANES)).T[:, :1]
                self.total_ref[o] += jnp.dot(
                    chosen(self.row_ref[self.vector_row(c, x, o), :]),
                    (self.spill_ref[...] * column).astype(BF),
                    preferred_element_type=F32,
                )
                return unused

            return lax.fori_loop(1, (count + (USED - 1)) // USED, chunk_step, unused)

        lax.fori_loop(0, spilled, spill_step, 0)
        self.out_ref[...] = self.total_ref[...].astype(BF)


UP_STEP = 1024
UP_STEPS = TIN // UP_STEP
UP_PART = 512


def pooled_kernel(
    me_ref,
    grad_ref,
    hidden0_ref,
    hidden1_ref,
    hidden2_ref,
    hidden3_ref,
    down_ref,
    up_hbm_ref,
    pooled_hbm_ref,
    pooled_ref,
    hid_ref,
    up_ref,
    up_sems,
    pooled_sems,
):
    def up_copy(k):
        rows = pl.ds(pl.multiple_of(k * UP_STEP, UP_STEP), UP_STEP)
        return pltpu.make_async_copy(up_hbm_ref.at[rows], up_ref.at[rows], up_sems.at[k])

    def pooled_copy(k, x):
        start = x * FEAT * SAMP + k * UP_STEP // E * SAMP
        rows = pl.ds(pl.multiple_of(start, UP_STEP), UP_STEP)
        return pltpu.make_async_copy(
            pooled_ref.at[rows], pooled_hbm_ref.at[rows], pooled_sems.at[k, x]
        )

    for k in range(UP_STEPS):
        up_copy(k).start()
    for r, hidden_ref in enumerate((hidden0_ref, hidden1_ref, hidden2_ref, hidden3_ref)):
        x = me_ref[0] ^ r
        backward = lax.dot_general(grad_ref[x], down_ref[...], NT, preferred_element_type=F32)
        keep = hidden_ref[...].astype(F32) > 0
        there = pl.ds(pl.multiple_of(x * SAMP, SAMP), SAMP)
        hid_ref[there, :] = jnp.where(keep, backward, 0.0).astype(BF)

    def up_step(k, unused):
        up_copy(k).wait()
        for j in range(UP_STEP // UP_PART):
            rows = pl.ds(pl.multiple_of(k * UP_STEP + j * UP_PART, UP_PART), UP_PART)
            result = lax.dot_general(
                hid_ref[...], up_ref[rows, :], NT, preferred_element_type=F32
            )
            result = result.astype(BF).astype(F32)
            for x in range(NX):
                for i in range(UP_PART // E):
                    block = (k * UP_STEP + j * UP_PART) // E + i
                    start = pl.multiple_of((x * FEAT + block) * SAMP, SAMP)
                    pooled_ref[pl.ds(start, SAMP), :] = result[
                        x * SAMP : (x + 1) * SAMP, i * E : (i + 1) * E
                    ]
        for x in range(NX):
            pooled_copy(k, x).start()
        return unused

    lax.fori_loop(0, UP_STEPS, up_step, 0)
    for k in range(UP_STEPS):
        for x in range(NX):
            pooled_copy(k, x).wait()


def pooled_gradients(me, grads, hiddens, down, up):
    hbm = pl.BlockSpec(memory_space=pltpu.HBM)
    vmem = pl.BlockSpec(memory_space=pltpu.VMEM)
    return pl.pallas_call(
        pooled_kernel,
        out_shape=pltpu.HBM((NX * FEAT * SAMP, E), F32),
        in_specs=[pl.BlockSpec(memory_space=pltpu.SMEM), *[vmem] * (NX + 2), hbm],
        out_specs=hbm,
        scratch_shapes=[
            pltpu.VMEM((NX * FEAT * SAMP, E), F32),
            pltpu.VMEM((NX * SAMP, HID), BF),
            pltpu.VMEM((TIN, HID), BF),
            pltpu.SemaphoreType.DMA((UP_STEPS,)),
            pltpu.SemaphoreType.DMA((UP_STEPS, NX)),
        ],
        compiler_params=pltpu.CompilerParams(vmem_limit_bytes=32 << 20),
        cost_estimate=pl.CostEstimate(flops=5 << 30, bytes_accessed=20 << 20, transcendentals=0),
    )(me, grads, *hiddens, down, in_hbm(up))


def table_kernel(
    half,
    index_hbm_ref,
    weight_ref,
    row_ref,
    pooled_hbm_ref,
    out_ref,
    pooled_ref,
    pooled_sems,
    *scratch,
):
    table = Table(half, index_hbm_ref, weight_ref, row_ref, pooled_ref, out_ref, scratch)

    def pooled_copy(x):
        rows = pl.ds(x * FEAT * SAMP, FEAT * SAMP)
        return pltpu.make_async_copy(
            pooled_hbm_ref.at[rows], pooled_ref.at[rows], pooled_sems.at[x]
        )

    for x in range(NX):
        pooled_copy(x).start()
    table.begin()
    spilled = 0
    for x in range(NX):
        pooled_copy(x).wait()
        spilled = table.gather(x, spilled)
    table.finish(spilled)


def half_tables(half, index, weight, rows, pooled):
    hbm = pl.BlockSpec(memory_space=pltpu.HBM)
    vmem = pl.BlockSpec(memory_space=pltpu.VMEM)
    return pl.pallas_call(
        functools.partial(table_kernel, half),
        out_shape=jax.ShapeDtypeStruct((NZ, HALF, E), BF),
        in_specs=[hbm, vmem, vmem, hbm],
        out_specs=vmem,
        scratch_shapes=[
            pltpu.VMEM((NX * FEAT * SAMP, E), F32),
            pltpu.SemaphoreType.DMA((NX,)),
            *TABLE_SCRATCH,
        ],
        compiler_params=pltpu.CompilerParams(vmem_limit_bytes=32 << 20),
        cost_estimate=pl.CostEstimate(flops=5 << 30, bytes_accessed=10 << 20, transcendentals=0),
    )(in_hbm(index), weight, rows, in_hbm(pooled))


def local(
    out_grad,
    hidden_pre,
    down_proj,
    up_proj,
    feature_slot,
    element_segment,
    element_weight,
    row_owner,
    row_local,
):
    own = hidden_pre[0]
    hiddens = [own] + [
        lax.ppermute(own, "x", [(i, i ^ r) for i in range(NX)]) for r in range(1, NX)
    ]
    by_tower = jnp.transpose(out_grad, (1, 0, 2))
    grads = lax.all_to_all(
        jnp.broadcast_to(by_tower, (NX, *by_tower.shape)).reshape(-1, *by_tower.shape[1:]),
        ("x", "tower"),
        split_axis=0,
        concat_axis=0,
        tiled=True,
    ).reshape(NX, SAMP, TOUT)
    swap_x = functools.partial(
        lax.all_to_all, axis_name="x", split_axis=0, concat_axis=0, tiled=True
    )
    flat = (1, ELEMS)
    buckets = bucket_elements(
        element_segment.reshape(flat),
        element_weight.reshape(flat),
        row_owner.reshape(flat),
        row_local.reshape(flat),
        feature_slot,
        grads,
    )
    parts = swap_x(buckets).reshape(NX, PIECES, CHUNKS * BUCKETS, LANES).astype(F32)
    index = (parts[:, 0] * SAMP + parts[:, 1]).astype(I32).reshape(-1)
    rows = parts[:, 2].astype(I32).reshape(NX * CHUNKS * BUCKETS, LANES)
    weight = (parts[:, 3] + parts[:, 4]).reshape(NX * CHUNKS * BUCKETS, LANES)
    me = lax.axis_index("x").astype(I32).reshape(1)
    pooled = pooled_gradients(me, grads, hiddens, down_proj[0], up_proj[0])
    swap = functools.partial(
        lax.all_to_all, axis_name="z", split_axis=0, concat_axis=0, tiled=True
    )
    first = swap(half_tables(0, index, weight, rows, pooled))
    second = swap(half_tables(1, index, weight, rows, pooled))
    table_grad = jnp.concatenate(
        [jnp.sum(first.astype(F32), axis=0), jnp.sum(second.astype(F32), axis=0)], axis=0
    )
    return table_grad.reshape(1, ROW_DEV, E)


def solution(mesh):
    towers = mesh.shape["tower"]
    grid = Mesh(mesh.devices.reshape(towers, NZ, NX), ("tower", "z", "x"))
    shard = ("z", "x")
    in_specs = (
        P(("tower", "z", "x"), None, None),
        P("tower", shard, None),
        P("tower", None, None),
        P("tower", None, None),
        P("tower", None),
        P("tower", shard, None),
        P("tower", shard, None),
        P("tower", shard, None, None),
        P("tower", shard, None),
    )
    out_specs = P("tower", shard, None)
    return jax.shard_map(local, mesh=grid, in_specs=in_specs, out_specs=out_specs, check_vma=False)
```

time: 124 us -> 107 us (0.86)
  the two profiles are of different devices: /device:TPU:8 before, /device:TPU:7 now
where the time goes in v4:
time: 107 us
  Pallas kernels  39.6 us (37%)
  starting transfers between devices  38.1 us (36%)
  waiting for transfers between devices  25.6 us (24%)
  local copies, waits for them, and re-layouts  1.66 us (2%)
  other arithmetic  1.59 us (1%)
    pallas_call x2, Pallas kernels, half_tables(): pl.pallas_call(functools.partial(table_kernel, half), out_shape=jax.Shape...  25.3 us
    all_to_all x1, waiting for transfers between devices, local(): second = swap(half_tables(1, index, weight, rows, pooled))  17.8 us
    all_to_all x1, starting transfers between devices, local(): lax.all_to_all(jnp.broadcast_to(by_tower, (NX, *by_tower.shape)).reshape(...  11.1 us
    all_to_all x1, starting transfers between devices, local(): first = swap(half_tables(0, index, weight, rows, pooled))  10.4 us
    ppermute x3, starting transfers between devices, local(): lax.ppermute(own, 'x', [(i, i ^ r) for i in range(NX)])  8.98 us
    pallas_call x1, Pallas kernels, pooled_gradients(): pl.pallas_call(pooled_kernel, out_shape=pltpu.HBM((NX * FEAT * SAMP, E),...  8.62 us
    pallas_call x1, Pallas kernels, bucket_elements(): pl.pallas_call(bucket_kernel, out_shape=jax.ShapeDtypeStruct((NX, PIECES,...  5.65 us
    all_to_all x1, waiting for transfers between devices, local(): first = swap(half_tables(0, index, weight, rows, pooled))  5.25 us
  transfers between devices with their start and end apart: 7, of which 3 were waited for; matrix products, arithmetic and copies ran while one was open for 0% of the time, Pallas kernels for 25%

profile of v4, /device:TPU:7, one launch (start us, length us, event | category | flops | bytes accessed | tf_op | source)
XLA Modules:
  0.0 106.6 jit_solution(9965580850493442265)
XLA Ops:
  0.0 0.0 copy-start.1
  0.0 0.0 copy-start
  0.0 0.9 copy.10
  0.9 0.7 broadcast_in_dim.3
  1.7 11.1 %all-to-all-start = ((bf16[64,8,256]{2,1,0:T(8,128)(2,1)}), bf16[64,8,256]{2,1,0:T(8,128)(2,1)S(1)}, u32[]{:S(2)}, u32[]{:S(2)}) async-start(bf16[64,8,256]{2,1,0:T(8,128)(2,1)} %bitcast.5), calls=%async_computation | async-start | bytes 524288 | tf_op jit(solution)/shard_map/all_to_all | solution.py:386
  12.8 1.9 %collective-permute-start.2 = (bf16[128,1024]{1,0:T(8,128)(2,1)}, bf16[128,1024]{1,0:T(8,128)(2,1)S(1)}, u32[]{:S(2)}, u32[]{:S(2)}) collective-permute-start(bf16[128,1024]{1,0:T(8,128)(2,1)} %bitcast.38), channel_id=1, source_target_pairs={{0,3},{1,2},{2,1},{3,0},{4,7},{5,6},{6,5},{7,4},{8,11},{9,10},{10,... | collective-permute-start | bytes 786440 | tf_op jit(solution)/shard_map/ppermute | solution.py:383
  14.7 4.2 %collective-permute-start.1 = (bf16[128,1024]{1,0:T(8,128)(2,1)}, bf16[128,1024]{1,0:T(8,128)(2,1)S(1)}, u32[]{:S(2)}, u32[]{:S(2)}) collective-permute-start(bf16[128,1024]{1,0:T(8,128)(2,1)} %bitcast.39), channel_id=1, source_target_pairs={{0,2},{1,3},{2,0},{3,1},{4,6},{5,7},{6,4},{7,5},{8,10},{9,11},{10,... | collective-permute-start | bytes 786440 | tf_op jit(solution)/shard_map/ppermute | solution.py:383
  18.9 2.9 %collective-permute-start = (bf16[128,1024]{1,0:T(8,128)(2,1)}, bf16[128,1024]{1,0:T(8,128)(2,1)S(1)}, u32[]{:S(2)}, u32[]{:S(2)}) collective-permute-start(bf16[128,1024]{1,0:T(8,128)(2,1)} %bitcast.40), channel_id=1, source_target_pairs={{0,1},{1,0},{2,3},{3,2},{4,5},{5,4},{6,7},{7,6},{8,9},{9,8},{10,11... | collective-permute-start | bytes 786440 | tf_op jit(solution)/shard_map/ppermute | solution.py:383
  21.8 2.5 %all-to-all-done = bf16[64,8,256]{2,1,0:T(8,128)(2,1)S(1)} async-done(((bf16[64,8,256]{2,1,0:T(8,128)(2,1)}), bf16[64,8,256]{2,1,0:T(8,128)(2,1)S(1)}, u32[]{:S(2)}, u32[]{:S(2)}) %all-to-all-start) | async-done | bytes 262176 | tf_op jit(solution)/shard_map/all_to_all | solution.py:386
  24.3 5.6 %shard_map.91 = bf16[4,5,3,16,128]{4,3,2,1,0:T(8,128)(2,1)} custom-call(s32[1,5120]{1,0:T(1,128)} %bitcast.46, f32[1,5120]{1,0:T(1,128)} %bitcast.47, s32[1,5120]{1,0:T(1,128)} %bitcast.48, s32[1,5120]{1,0:T(1,128)} %bitcast.49, s32[1,32]{1,0:T(1,128)} %slot_ref.1, bf16[4,128,256]{2,1,0:T(8,128)(2,1)S(1)} %bitcast.31), custom_call_target="tpu_custom_call" | custom-call | flops 3221225472 | bytes 1048576 | tf_op jit(solution)/shard_map/pallas_call | solution.py:112
  30.0 4.1 %all-to-all-start.1 = ((bf16[4,5,3,16,128]{4,3,2,1,0:T(8,128)(2,1)}), bf16[4,5,3,16,128]{4,3,2,1,0:T(8,128)(2,1)S(1)}, u32[]{:S(2)}, u32[]{:S(2)}) async-start(bf16[4,5,3,16,128]{4,3,2,1,0:T(8,128)(2,1)} %shard_map.91), calls=%async_computation.1 | async-start | bytes 491520 | tf_op jit(solution)/shard_map/all_to_all | solution.py:405
  34.1 0.0 collective-permute-done.2.hidden3_ref
  34.1 0.0 collective-permute-done.1.hidden2_ref
  34.1 0.0 collective-permute-done.hidden1_ref
  34.1 0.0 copy-done.1
  34.1 0.0 copy-done
  34.1 8.6 %shard_map.92.pooled_hbm_ref = f32[16384,128]{1,0:T(8,128)} custom-call(s32[1]{0:T(128)} %bitcast.12.me_ref, bf16[4,128,256]{2,1,0:T(8,128)(2,1)S(1)} %bitcast.32, bf16[128,1024]{1,0:T(8,128)(2,1)S(1)} %bitcast.41, bf16[128,1024]{1,0:T(8,128)(2,1)S(1)} %collective-permute-done.hidden1_ref, bf16[128,1024]{1,0:T(8,128)(2,1)S(1)} %collective-permute-done.1.hidden2_ref, ...), custom_call_target="tpu_custom_call" | custom-call | flops 5368709120 | bytes 20971520 | tf_op jit(solution)/shard_map/pallas_call | solution.py:306
  42.8 0.0 all-to-all-done.1
  42.8 0.1 bitcast_convert_fusion
  42.9 0.7 fusion
  43.5 12.6 %shard_map.93 = bf16[8,256,128]{2,1,0:T(8,128)(2,1)} custom-call(s32[24576]{0:T(1024)} %bitcast.42, f32[192,128]{1,0:T(8,128)S(1)} %bitcast.33, s32[192,128]{1,0:T(8,128)S(1)} %bitcast.35, f32[16384,128]{1,0:T(8,128)} %shard_map.92.pooled_hbm_ref), custom_call_target="tpu_custom_call" | custom-call | flops 5368709120 | bytes 10485760 | tf_op jit(solution)/shard_map/pallas_call | solution.py:355
  56.1 10.4 %all-to-all-start.2 = ((bf16[8,256,128]{2,1,0:T(8,128)(2,1)}), bf16[8,256,128]{2,1,0:T(8,128)(2,1)S(1)}, u32[]{:S(2)}, u32[]{:S(2)}) async-start(bf16[8,256,128]{2,1,0:T(8,128)(2,1)} %shard_map.93), calls=%async_computation.2 | async-start | bytes 1048576 | tf_op jit(solution)/shard_map/all_to_all | solution.py:414
  66.5 12.7 %shard_map.94 = bf16[8,256,128]{2,1,0:T(8,128)(2,1)} custom-call(s32[24576]{0:T(1024)} %bitcast.43, f32[192,128]{1,0:T(8,128)S(1)} %bitcast.34, s32[192,128]{1,0:T(8,128)S(1)} %bitcast.36, f32[16384,128]{1,0:T(8,128)} %shard_map.92.pooled_hbm_ref), custom_call_target="tpu_custom_call" | custom-call | flops 5368709120 | bytes 10485760 | tf_op jit(solution)/shard_map/pallas_call | solution.py:355
  79.2 5.3 %all-to-all-done.2 = bf16[8,256,128]{2,1,0:T(8,128)(2,1)S(1)} async-done(((bf16[8,256,128]{2,1,0:T(8,128)(2,1)}), bf16[8,256,128]{2,1,0:T(8,128)(2,1)S(1)}, u32[]{:S(2)}, u32[]{:S(2)}) %all-to-all-start.2) | async-done | bytes 524320 | tf_op jit(solution)/shard_map/all_to_all | solution.py:414
  84.5 3.5 %all-to-all-start.3 = ((bf16[8,256,128]{2,1,0:T(8,128)(2,1)}), bf16[8,256,128]{2,1,0:T(8,128)(2,1)S(1)}, u32[]{:S(2)}, u32[]{:S(2)}) async-start(bf16[8,256,128]{2,1,0:T(8,128)(2,1)} %shard_map.94), calls=%async_computation.3 | async-start | bytes 1048576 | tf_op jit(solution)/shard_map/all_to_all | solution.py:415
  88.0 0.1 convert_reduce_fusion.1
  88.0 17.8 %all-to-all-done.3 = bf16[8,256,128]{2,1,0:T(8,128)(2,1)S(1)} async-done(((bf16[8,256,128]{2,1,0:T(8,128)(2,1)}), bf16[8,256,128]{2,1,0:T(8,128)(2,1)S(1)}, u32[]{:S(2)}, u32[]{:S(2)}) %all-to-all-start.3) | async-done | bytes 524320 | tf_op jit(solution)/shard_map/all_to_all | solution.py:415
  105.8 0.1 convert_reduce_fusion
  105.9 0.7 maximum_bitcast_fusion
  (1 shorter events, 0.0 us)
Async XLA Ops:
  0.0 34.1 %copy-start.1 = (bf16[1,128,1024]{2,1,0:T(8,128)(2,1)S(1)}, bf16[1,128,1024]{2,1,0:T(8,128)(2,1)}, u32[]{:S(2)}) copy-start(bf16[1,128,1024]{2,1,0:T(8,128)(2,1)} %param.10) | copy-start | bytes 786436
  0.0 34.1 %copy-start = (bf16[1,1024,256]{2,1,0:T(8,128)(2,1)S(1)}, bf16[1,1024,256]{2,1,0:T(8,128)(2,1)}, u32[]{:S(2)}) copy-start(bf16[1,1024,256]{2,1,0:T(8,128)(2,1)} %param.11) | copy-start | bytes 1572868
  1.7 22.7 %all-to-all-start = ((bf16[64,8,256]{2,1,0:T(8,128)(2,1)}), bf16[64,8,256]{2,1,0:T(8,128)(2,1)S(1)}, u32[]{:S(2)}, u32[]{:S(2)}) async-start(bf16[64,8,256]{2,1,0:T(8,128)(2,1)} %bitcast.5), calls=%async_computation | async-start | bytes 524288 | tf_op jit(solution)/shard_map/all_to_all | solution.py:386
  12.8 21.3 %collective-permute-start.2 = (bf16[128,1024]{1,0:T(8,128)(2,1)}, bf16[128,1024]{1,0:T(8,128)(2,1)S(1)}, u32[]{:S(2)}, u32[]{:S(2)}) collective-permute-start(bf16[128,1024]{1,0:T(8,128)(2,1)} %bitcast.38), channel_id=1, source_target_pairs={{0,3},{1,2},{2,1},{3,0},{4,7},{5,6},{6,5},{7,4},{8,11},{9,10},{10,... | collective-permute-start | bytes 786440 | tf_op jit(solution)/shard_map/ppermute | solution.py:383
  14.7 19.4 %collective-permute-start.1 = (bf16[128,1024]{1,0:T(8,128)(2,1)}, bf16[128,1024]{1,0:T(8,128)(2,1)S(1)}, u32[]{:S(2)}, u32[]{:S(2)}) collective-permute-start(bf16[128,1024]{1,0:T(8,128)(2,1)} %bitcast.39), channel_id=1, source_target_pairs={{0,2},{1,3},{2,0},{3,1},{4,6},{5,7},{6,4},{7,5},{8,10},{9,11},{10,... | collective-permute-start | bytes 786440 | tf_op jit(solution)/shard_map/ppermute | solution.py:383
  18.9 15.2 %collective-permute-start = (bf16[128,1024]{1,0:T(8,128)(2,1)}, bf16[128,1024]{1,0:T(8,128)(2,1)S(1)}, u32[]{:S(2)}, u32[]{:S(2)}) collective-permute-start(bf16[128,1024]{1,0:T(8,128)(2,1)} %bitcast.40), channel_id=1, source_target_pairs={{0,1},{1,0},{2,3},{3,2},{4,5},{5,4},{6,7},{7,6},{8,9},{9,8},{10,11... | collective-permute-start | bytes 786440 | tf_op jit(solution)/shard_map/ppermute | solution.py:383
  30.0 12.8 %all-to-all-start.1 = ((bf16[4,5,3,16,128]{4,3,2,1,0:T(8,128)(2,1)}), bf16[4,5,3,16,128]{4,3,2,1,0:T(8,128)(2,1)S(1)}, u32[]{:S(2)}, u32[]{:S(2)}) async-start(bf16[4,5,3,16,128]{4,3,2,1,0:T(8,128)(2,1)} %shard_map.91), calls=%async_computation.1 | async-start | bytes 491520 | tf_op jit(solution)/shard_map/all_to_all | solution.py:405
  56.1 28.3 %all-to-all-start.2 = ((bf16[8,256,128]{2,1,0:T(8,128)(2,1)}), bf16[8,256,128]{2,1,0:T(8,128)(2,1)S(1)}, u32[]{:S(2)}, u32[]{:S(2)}) async-start(bf16[8,256,128]{2,1,0:T(8,128)(2,1)} %shard_map.93), calls=%async_computation.2 | async-start | bytes 1048576 | tf_op jit(solution)/shard_map/all_to_all | solution.py:414
  84.5 21.4 %all-to-all-start.3 = ((bf16[8,256,128]{2,1,0:T(8,128)(2,1)}), bf16[8,256,128]{2,1,0:T(8,128)(2,1)S(1)}, u32[]{:S(2)}, u32[]{:S(2)}) async-start(bf16[8,256,128]{2,1,0:T(8,128)(2,1)} %shard_map.94), calls=%async_computation.3 | async-start | bytes 1048576 | tf_op jit(solution)/shard_map/all_to_all | solution.py:415

commit v5 on v4

--- a/solution.py
+++ b/solution.py
@@ -30,6 +30,7 @@
 USED = 120
 STEP = 512
 UNROLL = 16
+BATCH = 4
 BF = jnp.bfloat16
 F32 = jnp.float32
 I32 = jnp.int32
@@ -61,10 +62,11 @@
     ).astype(F32).astype(BF)
     sub_ids = lax.broadcasted_iota(I32, (SUBS, STEP), 0)
     feat_ids = lax.broadcasted_iota(I32, (FEAT, STEP), 0)
-    slot_ids = lax.broadcasted_iota(I32, (SLOTS, STEP), 0).astype(F32)
+    most = (CHUNKS - 1) * LANES
+    slot_ids = lax.broadcasted_iota(I32, (most, STEP), 0).astype(F32)
     acc_ref[...] = jnp.zeros_like(acc_ref)
 
-    def step(k, carry):
+    def step(k, carry, first=0, width=most):
         cols = pl.ds(pl.multiple_of(k * STEP, STEP), STEP)
         seg = seg_ref[:, cols]
         weight = weight_ref[:, cols]
@@ -88,11 +90,20 @@
         place = rank
         for c in range(1, CHUNKS):
             place = place + jnp.where(rank >= c * USED, float(LANES - USED), 0.0)
-        right = jnp.where(slot_ids == place, 1.0, 0.0).astype(BF)
-        acc_ref[...] += lax.dot_general(left, right, NT, preferred_element_type=F32)
+        right = jnp.where(slot_ids[:width] == place - first, 1.0, 0.0).astype(BF)
+        acc_ref[:, first : first + width] += lax.dot_general(
+            left, right, NT, preferred_element_type=F32
+        )
         return inclusive[:, STEP - 1 : STEP]
 
-    count = lax.fori_loop(0, ELEMS // STEP, step, jnp.zeros((SUBS, 1), F32), unroll=10)
+    nothing = jnp.zeros((SUBS, 1), F32)
+    count = lax.fori_loop(0, ELEMS // STEP, step, nothing, unroll=10)
+
+    @pl.when(jnp.max(count) > (CHUNKS - 1) * USED)
+    def _():
+        last = functools.partial(step, first=most, width=LANES)
+        lax.fori_loop(0, ELEMS // STEP, last, nothing)
+
     count = jnp.broadcast_to(count.astype(I32), (SUBS, LANES))
     count_parts = ((count >> 7).astype(F32), (count & 127).astype(F32))
     spare = lax.broadcasted_iota(I32, (SUBS, LANES), 1) >= USED
@@ -127,10 +138,11 @@
 
 TABLE_SCRATCH = (
     pltpu.VMEM((NZ * NX * LANES, E), F32),
-    pltpu.VMEM((LANES, E), F32),
+    pltpu.VMEM((BATCH * LANES, E), F32),
     pltpu.VMEM((NZ, HALF, E), F32),
+    pltpu.VMEM((NZ * NX * LANES, E), F32),
     pltpu.SMEM((CHUNKS * NX * NZ * LANES,), I32),
-    pltpu.SMEM((NX * NZ + 1,), I32),
+    pltpu.SMEM((CHUNKS * NX * NZ,), I32),
     pltpu.SemaphoreType.DMA((CHUNKS, NX)),
 )
 
@@ -143,8 +155,8 @@
         self.pooled_ref = pooled_ref
         self.index_hbm_ref, self.weight_ref, self.row_ref = index_hbm_ref, weight_ref, row_ref
         self.out_ref = out_ref
-        self.group_ref, self.spill_ref, self.total_ref = scratch[:3]
-        self.index_ref, self.spilled_ref, self.index_sems = scratch[3:]
+        self.group_ref, self.spill_ref, self.total_ref, self.scale_ref = scratch[:4]
+        self.index_ref, self.spilled_ref, self.index_sems = scratch[4:]
 
     def index_copy(self, c, x):
         part = NZ * LANES
@@ -161,6 +173,15 @@
                 self.index_copy(c, x).start()
         self.group_ref[...] = jnp.zeros_like(self.group_ref)
         self.spill_ref[...] = jnp.zeros_like(self.spill_ref)
+        blank = jnp.zeros((8 - NX, LANES), F32)
+        for o in range(NZ):
+            weights = [self.weight_ref[self.vector_row(0, x, o), :] for x in range(NX)]
+            columns = jnp.concatenate([*weights, blank], axis=0).T
+            for x in range(NX):
+                start = (o * NX + x) * LANES
+                self.scale_ref[start : start + LANES, :] = jnp.broadcast_to(
+                    columns[:, x : x + 1], (LANES, E)
+                )
 
     def vector_row(self, c, x, o):
         return pl.ds((x * CHUNKS + c) * BUCKETS + self.half * NZ + o, 1)
@@ -188,49 +209,50 @@
             count = self.index_ref[row + USED]
             start = (o * NX + x) * LANES
             self.fetch(row, jnp.minimum(count, USED), x * (FEAT * SAMP), self.group_ref, start)
-            self.spilled_ref[spilled] = o * NX + x
-            return spilled + (count > USED).astype(I32)
+            for c in range(1, CHUNKS):
+                self.spilled_ref[spilled] = (c * NZ + o) * NX + x
+                spilled = spilled + (count > c * USED).astype(I32)
+            return spilled
 
         return lax.fori_loop(0, NZ, bucket_step, spilled)
 
     def finish(self, spilled):
-        blank = jnp.zeros((8 - NX, LANES), F32)
         for o in range(NZ):
             rows = jnp.concatenate(
                 [self.row_ref[self.vector_row(0, x, o), :] for x in range(NX)], axis=1
             )
-            weights = [self.weight_ref[self.vector_row(0, x, o), :] for x in range(NX)]
-            columns = jnp.concatenate([*weights, blank], axis=0).T
-            values = []
-            for x in range(NX):
-                start = (o * NX + x) * LANES
-                values.append(self.group_ref[start : start + LANES, :] * columns[:, x : x + 1])
-            values = jnp.concatenate(values, axis=0).astype(BF)
+            these = slice(o * NX * LANES, (o + 1) * NX * LANES)
+            values = (self.group_ref[these, :] * self.scale_ref[these, :]).astype(BF)
             self.total_ref[o] = jnp.dot(chosen(rows), values, preferred_element_type=F32)
         for c in range(1, CHUNKS):
             for x in range(NX):
                 self.index_copy(c, x).wait()
 
         def spill_step(k, unused):
-            i = self.spilled_ref[k]
-            x, o = i & (NX - 1), i >> 2
-            count = self.index_ref[self.index_row(0, x, o) + USED]
-
-            def chunk_step(c, unused):
-                rest = jnp.minimum(count - c * USED, USED)
-                self.fetch(self.index_row(c, x, o), rest, x * (FEAT * SAMP), self.spill_ref, 0)
-                weight = self.weight_ref[self.vector_row(c, x, o), :]
+            entries = []
+            for q in range(BATCH):
+                number = k * BATCH + q
+                entry = self.spilled_ref[jnp.minimum(number, spilled - 1)]
+                x, o = entry & (NX - 1), (entry >> 2) & (NZ - 1)
+                c = entry >> 5
+                count = self.index_ref[self.index_row(0, x, o) + USED] - c * USED
+                count = jnp.where(number < spilled, jnp.minimum(count, USED), 0)
+                shift = x * (FEAT * SAMP)
+                self.fetch(self.index_row(c, x, o), count, shift, self.spill_ref, q * LANES)
+                entries.append((x, o, c, count))
+            for q, (x, o, c, count) in enumerate(entries):
+                row = self.vector_row(c, x, o)
+                weight = jnp.where(count > 0, self.weight_ref[row, :], 0.0)
                 column = jnp.broadcast_to(weight, (8, LANES)).T[:, :1]
+                values = self.spill_ref[q * LANES : (q + 1) * LANES, :] * column
                 self.total_ref[o] += jnp.dot(
-                    chosen(self.row_ref[self.vector_row(c, x, o), :]),
-                    (self.spill_ref[...] * column).astype(BF),
+                    chosen(self.row_ref[row, :]),
+                    values.astype(BF),
                     preferred_element_type=F32,
                 )
-                return unused
-
-            return lax.fori_loop(1, (count + (USED - 1)) // USED, chunk_step, unused)
-
-        lax.fori_loop(0, spilled, spill_step, 0)
+            return unused
+
+        lax.fori_loop(0, (spilled + (BATCH - 1)) // BATCH, spill_step, 0)
         self.out_ref[...] = self.total_ref[...].astype(BF)
 
 

time: 107 us -> 101 us (0.944)
  the two profiles are of different devices: /device:TPU:7 before, /device:TPU:1 now
where the time goes in v5:
time: 101 us; the launch traced here: 100 us
  starting transfers between devices  38.4 us (38%)
  Pallas kernels  31.8 us (31%)
  waiting for transfers between devices  26.9 us (27%)
  local copies, waits for them, and re-layouts  1.66 us (2%)
  other arithmetic  1.59 us (2%)
    pallas_call x2, Pallas kernels, half_tables(): pl.pallas_call(functools.partial(table_kernel, half), out_shape=jax.Shape...  19.1 us
    all_to_all x1, waiting for transfers between devices, local(): second = swap(half_tables(1, index, weight, rows, pooled))  16.4 us
    all_to_all x1, starting transfers between devices, local(): lax.all_to_all(jnp.broadcast_to(by_tower, (NX, *by_tower.shape)).reshape(...  11.6 us
    all_to_all x1, starting transfers between devices, local(): first = swap(half_tables(0, index, weight, rows, pooled))  10.3 us
    ppermute x3, starting transfers between devices, local(): lax.ppermute(own, 'x', [(i, i ^ r) for i in range(NX)])  9.13 us
    pallas_call x1, Pallas kernels, pooled_gradients(): pl.pallas_call(pooled_kernel, out_shape=pltpu.HBM((NX * FEAT * SAMP, E),...  8.61 us
    all_to_all x1, waiting for transfers between devices, local(): first = swap(half_tables(0, index, weight, rows, pooled))  7.6 us
    pallas_call x1, Pallas kernels, bucket_elements(): pl.pallas_call(bucket_kernel, out_shape=jax.ShapeDtypeStruct((NX, PIECES,...  4.14 us
  transfers between devices with their start and end apart: 7, of which 3 were waited for; matrix products, arithmetic and copies ran while one was open for 0% of the time, Pallas kernels for 22%

profile of v5, /device:TPU:1, one launch (start us, length us, event | category | flops | bytes accessed | tf_op | source)
XLA Modules:
  0.0 100.4 jit_solution(8133069546868515741)
XLA Ops:
  0.0 0.0 copy-start.1
  0.0 0.0 copy-start
  0.0 0.9 copy.10
  0.9 0.7 broadcast_in_dim.3
  1.7 11.6 %all-to-all-start = ((bf16[64,8,256]{2,1,0:T(8,128)(2,1)}), bf16[64,8,256]{2,1,0:T(8,128)(2,1)S(1)}, u32[]{:S(2)}, u32[]{:S(2)}) async-start(bf16[64,8,256]{2,1,0:T(8,128)(2,1)} %bitcast.5), calls=%async_computation | async-start | bytes 524288 | tf_op jit(solution)/shard_map/all_to_all | solution.py:408
  13.3 4.7 %collective-permute-start.2 = (bf16[128,1024]{1,0:T(8,128)(2,1)}, bf16[128,1024]{1,0:T(8,128)(2,1)S(1)}, u32[]{:S(2)}, u32[]{:S(2)}) collective-permute-start(bf16[128,1024]{1,0:T(8,128)(2,1)} %bitcast.38), channel_id=1, source_target_pairs={{0,3},{1,2},{2,1},{3,0},{4,7},{5,6},{6,5},{7,4},{8,11},{9,10},{10,... | collective-permute-start | bytes 786440 | tf_op jit(solution)/shard_map/ppermute | solution.py:405
  18.0 2.3 %collective-permute-start.1 = (bf16[128,1024]{1,0:T(8,128)(2,1)}, bf16[128,1024]{1,0:T(8,128)(2,1)S(1)}, u32[]{:S(2)}, u32[]{:S(2)}) collective-permute-start(bf16[128,1024]{1,0:T(8,128)(2,1)} %bitcast.39), channel_id=1, source_target_pairs={{0,2},{1,3},{2,0},{3,1},{4,6},{5,7},{6,4},{7,5},{8,10},{9,11},{10,... | collective-permute-start | bytes 786440 | tf_op jit(solution)/shard_map/ppermute | solution.py:405
  20.3 2.1 %collective-permute-start = (bf16[128,1024]{1,0:T(8,128)(2,1)}, bf16[128,1024]{1,0:T(8,128)(2,1)S(1)}, u32[]{:S(2)}, u32[]{:S(2)}) collective-permute-start(bf16[128,1024]{1,0:T(8,128)(2,1)} %bitcast.40), channel_id=1, source_target_pairs={{0,1},{1,0},{2,3},{3,2},{4,5},{5,4},{6,7},{7,6},{8,9},{9,8},{10,11... | collective-permute-start | bytes 786440 | tf_op jit(solution)/shard_map/ppermute | solution.py:405
  22.4 2.8 %all-to-all-done = bf16[64,8,256]{2,1,0:T(8,128)(2,1)S(1)} async-done(((bf16[64,8,256]{2,1,0:T(8,128)(2,1)}), bf16[64,8,256]{2,1,0:T(8,128)(2,1)S(1)}, u32[]{:S(2)}, u32[]{:S(2)}) %all-to-all-start) | async-done | bytes 262176 | tf_op jit(solution)/shard_map/all_to_all | solution.py:408
  25.3 4.1 %shard_map.91 = bf16[4,5,3,16,128]{4,3,2,1,0:T(8,128)(2,1)} custom-call(s32[1,5120]{1,0:T(1,128)} %bitcast.46, f32[1,5120]{1,0:T(1,128)} %bitcast.47, s32[1,5120]{1,0:T(1,128)} %bitcast.48, s32[1,5120]{1,0:T(1,128)} %bitcast.49, s32[1,32]{1,0:T(1,128)} %slot_ref.1, bf16[4,128,256]{2,1,0:T(8,128)(2,1)S(1)} %bitcast.31), custom_call_target="tpu_custom_call" | custom-call | flops 3221225472 | bytes 1048576 | tf_op jit(solution)/shard_map/pallas_call | solution.py:123
  29.4 3.8 %all-to-all-start.1 = ((bf16[4,5,3,16,128]{4,3,2,1,0:T(8,128)(2,1)}), bf16[4,5,3,16,128]{4,3,2,1,0:T(8,128)(2,1)S(1)}, u32[]{:S(2)}, u32[]{:S(2)}) async-start(bf16[4,5,3,16,128]{4,3,2,1,0:T(8,128)(2,1)} %shard_map.91), calls=%async_computation.1 | async-start | bytes 491520 | tf_op jit(solution)/shard_map/all_to_all | solution.py:427
  33.2 0.0 collective-permute-done.2.hidden3_ref
  33.2 0.0 collective-permute-done.1.hidden2_ref
  33.2 0.0 collective-permute-done.hidden1_ref
  33.3 0.0 copy-done.1
  33.3 0.0 copy-done
  33.3 8.6 %shard_map.92.pooled_hbm_ref = f32[16384,128]{1,0:T(8,128)} custom-call(s32[1]{0:T(128)} %bitcast.12.me_ref, bf16[4,128,256]{2,1,0:T(8,128)(2,1)S(1)} %bitcast.32, bf16[128,1024]{1,0:T(8,128)(2,1)S(1)} %bitcast.41, bf16[128,1024]{1,0:T(8,128)(2,1)S(1)} %collective-permute-done.hidden1_ref, bf16[128,1024]{1,0:T(8,128)(2,1)S(1)} %collective-permute-done.1.hidden2_ref, ...), custom_call_target="tpu_custom_call" | custom-call | flops 5368709120 | bytes 20971520 | tf_op jit(solution)/shard_map/pallas_call | solution.py:328
  41.9 0.0 all-to-all-done.1
  41.9 0.1 bitcast_convert_fusion
  42.0 0.7 fusion
  42.6 9.6 %shard_map.93 = bf16[8,256,128]{2,1,0:T(8,128)(2,1)} custom-call(s32[24576]{0:T(1024)} %bitcast.42, f32[192,128]{1,0:T(8,128)S(1)} %bitcast.33, s32[192,128]{1,0:T(8,128)S(1)} %bitcast.35, f32[16384,128]{1,0:T(8,128)} %shard_map.92.pooled_hbm_ref), custom_call_target="tpu_custom_call" | custom-call | flops 5368709120 | bytes 10485760 | tf_op jit(solution)/shard_map/pallas_call | solution.py:377
  52.3 10.3 %all-to-all-start.2 = ((bf16[8,256,128]{2,1,0:T(8,128)(2,1)}), bf16[8,256,128]{2,1,0:T(8,128)(2,1)S(1)}, u32[]{:S(2)}, u32[]{:S(2)}) async-start(bf16[8,256,128]{2,1,0:T(8,128)(2,1)} %shard_map.93), calls=%async_computation.2 | async-start | bytes 1048576 | tf_op jit(solution)/shard_map/all_to_all | solution.py:436
  62.6 9.4 %shard_map.94 = bf16[8,256,128]{2,1,0:T(8,128)(2,1)} custom-call(s32[24576]{0:T(1024)} %bitcast.43, f32[192,128]{1,0:T(8,128)S(1)} %bitcast.34, s32[192,128]{1,0:T(8,128)S(1)} %bitcast.36, f32[16384,128]{1,0:T(8,128)} %shard_map.92.pooled_hbm_ref), custom_call_target="tpu_custom_call" | custom-call | flops 5368709120 | bytes 10485760 | tf_op jit(solution)/shard_map/pallas_call | solution.py:377
  72.0 7.6 %all-to-all-done.2 = bf16[8,256,128]{2,1,0:T(8,128)(2,1)S(1)} async-done(((bf16[8,256,128]{2,1,0:T(8,128)(2,1)}), bf16[8,256,128]{2,1,0:T(8,128)(2,1)S(1)}, u32[]{:S(2)}, u32[]{:S(2)}) %all-to-all-start.2) | async-done | bytes 524320 | tf_op jit(solution)/shard_map/all_to_all | solution.py:436
  79.6 3.5 %all-to-all-start.3 = ((bf16[8,256,128]{2,1,0:T(8,128)(2,1)}), bf16[8,256,128]{2,1,0:T(8,128)(2,1)S(1)}, u32[]{:S(2)}, u32[]{:S(2)}) async-start(bf16[8,256,128]{2,1,0:T(8,128)(2,1)} %shard_map.94), calls=%async_computation.3 | async-start | bytes 1048576 | tf_op jit(solution)/shard_map/all_to_all | solution.py:437
  83.1 0.1 convert_reduce_fusion.1
  83.2 16.4 %all-to-all-done.3 = bf16[8,256,128]{2,1,0:T(8,128)(2,1)S(1)} async-done(((bf16[8,256,128]{2,1,0:T(8,128)(2,1)}), bf16[8,256,128]{2,1,0:T(8,128)(2,1)S(1)}, u32[]{:S(2)}, u32[]{:S(2)}) %all-to-all-start.3) | async-done | bytes 524320 | tf_op jit(solution)/shard_map/all_to_all | solution.py:437
  99.6 0.1 convert_reduce_fusion
  99.7 0.7 maximum_bitcast_fusion
  (1 shorter events, 0.0 us)
Async XLA Ops:
  0.0 33.3 %copy-start.1 = (bf16[1,128,1024]{2,1,0:T(8,128)(2,1)S(1)}, bf16[1,128,1024]{2,1,0:T(8,128)(2,1)}, u32[]{:S(2)}) copy-start(bf16[1,128,1024]{2,1,0:T(8,128)(2,1)} %param.10) | copy-start | bytes 786436
  0.0 33.3 %copy-start = (bf16[1,1024,256]{2,1,0:T(8,128)(2,1)S(1)}, bf16[1,1024,256]{2,1,0:T(8,128)(2,1)}, u32[]{:S(2)}) copy-start(bf16[1,1024,256]{2,1,0:T(8,128)(2,1)} %param.11) | copy-start | bytes 1572868
  1.7 23.6 %all-to-all-start = ((bf16[64,8,256]{2,1,0:T(8,128)(2,1)}), bf16[64,8,256]{2,1,0:T(8,128)(2,1)S(1)}, u32[]{:S(2)}, u32[]{:S(2)}) async-start(bf16[64,8,256]{2,1,0:T(8,128)(2,1)} %bitcast.5), calls=%async_computation | async-start | bytes 524288 | tf_op jit(solution)/shard_map/all_to_all | solution.py:408
  13.3 19.9 %collective-permute-start.2 = (bf16[128,1024]{1,0:T(8,128)(2,1)}, bf16[128,1024]{1,0:T(8,128)(2,1)S(1)}, u32[]{:S(2)}, u32[]{:S(2)}) collective-permute-start(bf16[128,1024]{1,0:T(8,128)(2,1)} %bitcast.38), channel_id=1, source_target_pairs={{0,3},{1,2},{2,1},{3,0},{4,7},{5,6},{6,5},{7,4},{8,11},{9,10},{10,... | collective-permute-start | bytes 786440 | tf_op jit(solution)/shard_map/ppermute | solution.py:405
  18.0 15.2 %collective-permute-start.1 = (bf16[128,1024]{1,0:T(8,128)(2,1)}, bf16[128,1024]{1,0:T(8,128)(2,1)S(1)}, u32[]{:S(2)}, u32[]{:S(2)}) collective-permute-start(bf16[128,1024]{1,0:T(8,128)(2,1)} %bitcast.39), channel_id=1, source_target_pairs={{0,2},{1,3},{2,0},{3,1},{4,6},{5,7},{6,4},{7,5},{8,10},{9,11},{10,... | collective-permute-start | bytes 786440 | tf_op jit(solution)/shard_map/ppermute | solution.py:405
  20.3 12.9 %collective-permute-start = (bf16[128,1024]{1,0:T(8,128)(2,1)}, bf16[128,1024]{1,0:T(8,128)(2,1)S(1)}, u32[]{:S(2)}, u32[]{:S(2)}) collective-permute-start(bf16[128,1024]{1,0:T(8,128)(2,1)} %bitcast.40), channel_id=1, source_target_pairs={{0,1},{1,0},{2,3},{3,2},{4,5},{5,4},{6,7},{7,6},{8,9},{9,8},{10,11... | collective-permute-start | bytes 786440 | tf_op jit(solution)/shard_map/ppermute | solution.py:405
  29.4 12.5 %all-to-all-start.1 = ((bf16[4,5,3,16,128]{4,3,2,1,0:T(8,128)(2,1)}), bf16[4,5,3,16,128]{4,3,2,1,0:T(8,128)(2,1)S(1)}, u32[]{:S(2)}, u32[]{:S(2)}) async-start(bf16[4,5,3,16,128]{4,3,2,1,0:T(8,128)(2,1)} %shard_map.91), calls=%async_computation.1 | async-start | bytes 491520 | tf_op jit(solution)/shard_map/all_to_all | solution.py:427
  52.3 27.4 %all-to-all-start.2 = ((bf16[8,256,128]{2,1,0:T(8,128)(2,1)}), bf16[8,256,128]{2,1,0:T(8,128)(2,1)S(1)}, u32[]{:S(2)}, u32[]{:S(2)}) async-start(bf16[8,256,128]{2,1,0:T(8,128)(2,1)} %shard_map.93), calls=%async_computation.2 | async-start | bytes 1048576 | tf_op jit(solution)/shard_map/all_to_all | solution.py:436
  79.6 20.0 %all-to-all-start.3 = ((bf16[8,256,128]{2,1,0:T(8,128)(2,1)}), bf16[8,256,128]{2,1,0:T(8,128)(2,1)S(1)}, u32[]{:S(2)}, u32[]{:S(2)}) async-start(bf16[8,256,128]{2,1,0:T(8,128)(2,1)} %shard_map.94), calls=%async_computation.3 | async-start | bytes 1048576 | tf_op jit(solution)/shard_map/all_to_all | solution.py:437

commit v6 on v5

--- a/solution.py
+++ b/solution.py
@@ -141,33 +141,40 @@
     pltpu.VMEM((BATCH * LANES, E), F32),
     pltpu.VMEM((NZ, HALF, E), F32),
     pltpu.VMEM((NZ * NX * LANES, E), F32),
-    pltpu.SMEM((CHUNKS * NX * NZ * LANES,), I32),
+    pltpu.VMEM((NX * CHUNKS * BUCKETS, LANES), I32),
+    pltpu.VMEM((NX * CHUNKS * BUCKETS, LANES), I32),
+    pltpu.VMEM((NX * CHUNKS * BUCKETS, LANES), F32),
+    pltpu.SMEM((CHUNKS * NX * NZ, LANES), I32),
     pltpu.SMEM((CHUNKS * NX * NZ,), I32),
     pltpu.SemaphoreType.DMA((CHUNKS, NX)),
 )
 
 
 class Table:
-    def __init__(
-        self, half, index_hbm_ref, weight_ref, row_ref, pooled_ref, out_ref, scratch
-    ):
+    def __init__(self, half, parts_ref, pooled_ref, out_ref, scratch):
         self.half = half
-        self.pooled_ref = pooled_ref
-        self.index_hbm_ref, self.weight_ref, self.row_ref = index_hbm_ref, weight_ref, row_ref
-        self.out_ref = out_ref
+        self.parts_ref, self.pooled_ref, self.out_ref = parts_ref, pooled_ref, out_ref
         self.group_ref, self.spill_ref, self.total_ref, self.scale_ref = scratch[:4]
-        self.index_ref, self.spilled_ref, self.index_sems = scratch[4:]
+        self.place_ref, self.row_ref, self.weight_ref = scratch[4:7]
+        self.index_ref, self.spilled_ref, self.index_sems = scratch[7:]
 
     def index_copy(self, c, x):
-        part = NZ * LANES
-        start = ((x * CHUNKS + c) * BUCKETS + self.half * NZ) * LANES
+        start = (x * CHUNKS + c) * BUCKETS + self.half * NZ
         return pltpu.make_async_copy(
-            self.index_hbm_ref.at[pl.ds(start, part)],
-            self.index_ref.at[pl.ds((c * NX + x) * part, part)],
+            self.place_ref.at[pl.ds(start, NZ)],
+            self.index_ref.at[pl.ds((c * NX + x) * NZ, NZ)],
             self.index_sems.at[c, x],
         )
 
     def begin(self):
+        for x in range(NX):
+            block, sample, row, high, middle = [
+                self.parts_ref[x, p].astype(F32) for p in range(PIECES)
+            ]
+            these = slice(x * CHUNKS * BUCKETS, (x + 1) * CHUNKS * BUCKETS)
+            self.place_ref[these, :] = (block * SAMP + sample).astype(I32)
+            self.row_ref[these, :] = row.astype(I32)
+            self.weight_ref[these, :] = high + middle
         for c in range(CHUNKS):
             for x in range(NX):
                 self.index_copy(c, x).start()
@@ -187,15 +194,17 @@
         return pl.ds((x * CHUNKS + c) * BUCKETS + self.half * NZ + o, 1)
 
     def index_row(self, c, x, o):
-        return ((c * NX + x) * NZ + o) * LANES
+        return (c * NX + x) * NZ + o
 
     def fetch(self, source_row, count, shift, target_ref, start):
+        places = self.index_ref.at[source_row]
+
         def some(j, unused):
-            source = source_row + j * UNROLL
+            source = j * UNROLL
             target = pl.multiple_of(start + j * UNROLL, UNROLL)
             for u in range(UNROLL):
                 target_ref[pl.ds(target + u, 1), :] = self.pooled_ref[
-                    pl.ds(self.index_ref[source + u] + shift, 1), :
+                    pl.ds(places[source + u] + shift, 1), :
                 ]
             return unused
 
@@ -206,7 +215,7 @@
 
         def bucket_step(o, spilled):
             row = self.index_row(0, x, o)
-            count = self.index_ref[row + USED]
+            count = self.index_ref[row, USED]
             start = (o * NX + x) * LANES
             self.fetch(row, jnp.minimum(count, USED), x * (FEAT * SAMP), self.group_ref, start)
             for c in range(1, CHUNKS):
@@ -235,7 +244,7 @@
                 entry = self.spilled_ref[jnp.minimum(number, spilled - 1)]
                 x, o = entry & (NX - 1), (entry >> 2) & (NZ - 1)
                 c = entry >> 5
-                count = self.index_ref[self.index_row(0, x, o) + USED] - c * USED
+                count = self.index_ref[self.index_row(0, x, o), USED] - c * USED
                 count = jnp.where(number < spilled, jnp.minimum(count, USED), 0)
                 shift = x * (FEAT * SAMP)
                 self.fetch(self.index_row(c, x, o), count, shift, self.spill_ref, q * LANES)
@@ -344,16 +353,14 @@
 
 def table_kernel(
     half,
-    index_hbm_ref,
-    weight_ref,
-    row_ref,
+    parts_ref,
     pooled_hbm_ref,
     out_ref,
     pooled_ref,
     pooled_sems,
     *scratch,
 ):
-    table = Table(half, index_hbm_ref, weight_ref, row_ref, pooled_ref, out_ref, scratch)
+    table = Table(half, parts_ref, pooled_ref, out_ref, scratch)
 
     def pooled_copy(x):
         rows = pl.ds(x * FEAT * SAMP, FEAT * SAMP)
@@ -371,13 +378,13 @@
     table.finish(spilled)
 
 
-def half_tables(half, index, weight, rows, pooled):
+def half_tables(half, parts, pooled):
     hbm = pl.BlockSpec(memory_space=pltpu.HBM)
     vmem = pl.BlockSpec(memory_space=pltpu.VMEM)
     return pl.pallas_call(
         functools.partial(table_kernel, half),
         out_shape=jax.ShapeDtypeStruct((NZ, HALF, E), BF),
-        in_specs=[hbm, vmem, vmem, hbm],
+        in_specs=[vmem, hbm],
         out_specs=vmem,
         scratch_shapes=[
             pltpu.VMEM((NX * FEAT * SAMP, E), F32),
@@ -386,7 +393,7 @@
         ],
         compiler_params=pltpu.CompilerParams(vmem_limit_bytes=32 << 20),
         cost_estimate=pl.CostEstimate(flops=5 << 30, bytes_accessed=10 << 20, transcendentals=0),
-    )(in_hbm(index), weight, rows, in_hbm(pooled))
+    )(parts, in_hbm(pooled))
 
 
 def local(
@@ -401,9 +408,10 @@
     row_local,
 ):
     own = hidden_pre[0]
-    hiddens = [own] + [
-        lax.ppermute(own, "x", [(i, i ^ r) for i in range(NX)]) for r in range(1, NX)
+    near, side, far = [
+        lax.ppermute(own, "x", [(i, i ^ r) for i in range(NX)]) for r in (1, 3, 2)
     ]
+    hiddens = (own, near, far, side)
     by_tower = jnp.transpose(out_grad, (1, 0, 2))
     grads = lax.all_to_all(
         jnp.broadcast_to(by_tower, (NX, *by_tower.shape)).reshape(-1, *by_tower.shape[1:]),
@@ -424,17 +432,14 @@
         feature_slot,
         grads,
     )
-    parts = swap_x(buckets).reshape(NX, PIECES, CHUNKS * BUCKETS, LANES).astype(F32)
-    index = (parts[:, 0] * SAMP + parts[:, 1]).astype(I32).reshape(-1)
-    rows = parts[:, 2].astype(I32).reshape(NX * CHUNKS * BUCKETS, LANES)
-    weight = (parts[:, 3] + parts[:, 4]).reshape(NX * CHUNKS * BUCKETS, LANES)
+    parts = swap_x(buckets).reshape(NX, PIECES, CHUNKS * BUCKETS, LANES)
     me = lax.axis_index("x").astype(I32).reshape(1)
     pooled = pooled_gradients(me, grads, hiddens, down_proj[0], up_proj[0])
     swap = functools.partial(
         lax.all_to_all, axis_name="z", split_axis=0, concat_axis=0, tiled=True
     )
-    first = swap(half_tables(0, index, weight, rows, pooled))
-    second = swap(half_tables(1, index, weight, rows, pooled))
+    first = swap(half_tables(0, parts, pooled))
+    second = swap(half_tables(1, parts, pooled))
     table_grad = jnp.concatenate(
         [jnp.sum(first.astype(F32), axis=0), jnp.sum(second.astype(F32), axis=0)], axis=0
     )

time: 101 us -> 101 us (level)
  the two profiles are of different devices: /device:TPU:1 before, /device:TPU:23 now
where the time goes in v6:
time: 101 us; the launch traced here: 100 us
  starting transfers between devices  38.7 us (38%)
  Pallas kernels  32.6 us (32%)
  waiting for transfers between devices  26.5 us (26%)
  local copies, waits for them, and re-layouts  1.66 us (2%)
    pallas_call x2, Pallas kernels, half_tables(): pl.pallas_call(functools.partial(table_kernel, half), out_shape=jax.Shape...  19.9 us
    all_to_all x1, waiting for transfers between devices, local(): second = swap(half_tables(1, parts, pooled))  17.8 us
    all_to_all x1, starting transfers between devices, local(): lax.all_to_all(jnp.broadcast_to(by_tower, (NX, *by_tower.shape)).reshape(...  10.9 us
    all_to_all x1, starting transfers between devices, local(): first = swap(half_tables(0, parts, pooled))  9.98 us
    ppermute x3, starting transfers between devices, local(): lax.ppermute(own, 'x', [(i, i ^ r) for i in range(NX)])  8.98 us
    pallas_call x1, Pallas kernels, pooled_gradients(): pl.pallas_call(pooled_kernel, out_shape=pltpu.HBM((NX * FEAT * SAMP, E),...  8.61 us
    all_to_all x1, waiting for transfers between devices, local(): first = swap(half_tables(0, parts, pooled))  7.86 us
    all_to_all x1, starting transfers between devices, local(): parts = swap_x(buckets).reshape(NX, PIECES, CHUNKS * BUCKETS, LANES)  5.28 us
  transfers between devices with their start and end apart: 7, of which 3 were waited for; matrix products, arithmetic and copies ran while one was open for 0% of the time, Pallas kernels for 23%

profile of v6, /device:TPU:23, one launch (start us, length us, event | category | flops | bytes accessed | tf_op | source)
XLA Modules:
  0.0 100.4 jit_solution(11546589453092877163)
XLA Ops:
  0.0 0.0 copy-start.1
  0.0 0.0 copy-start
  0.0 0.9 copy.10
  0.9 0.7 broadcast_in_dim.3
  1.7 10.9 %all-to-all-start = ((bf16[64,8,256]{2,1,0:T(8,128)(2,1)}), bf16[64,8,256]{2,1,0:T(8,128)(2,1)S(1)}, u32[]{:S(2)}, u32[]{:S(2)}) async-start(bf16[64,8,256]{2,1,0:T(8,128)(2,1)} %bitcast.5), calls=%async_computation | async-start | bytes 524288 | tf_op jit(solution)/shard_map/all_to_all | solution.py:416
  12.6 2.0 %collective-permute-start.2 = (bf16[128,1024]{1,0:T(8,128)(2,1)}, bf16[128,1024]{1,0:T(8,128)(2,1)S(1)}, u32[]{:S(2)}, u32[]{:S(2)}) collective-permute-start(bf16[128,1024]{1,0:T(8,128)(2,1)} %bitcast.19), channel_id=1, source_target_pairs={{0,3},{1,2},{2,1},{3,0},{4,7},{5,6},{6,5},{7,4},{8,11},{9,10},{10,... | collective-permute-start | bytes 786440 | tf_op jit(solution)/shard_map/ppermute | solution.py:412
  14.6 4.1 %collective-permute-start.1 = (bf16[128,1024]{1,0:T(8,128)(2,1)}, bf16[128,1024]{1,0:T(8,128)(2,1)S(1)}, u32[]{:S(2)}, u32[]{:S(2)}) collective-permute-start(bf16[128,1024]{1,0:T(8,128)(2,1)} %bitcast.20), channel_id=1, source_target_pairs={{0,2},{1,3},{2,0},{3,1},{4,6},{5,7},{6,4},{7,5},{8,10},{9,11},{10,... | collective-permute-start | bytes 786440 | tf_op jit(solution)/shard_map/ppermute | solution.py:412
  18.7 2.9 %collective-permute-start = (bf16[128,1024]{1,0:T(8,128)(2,1)}, bf16[128,1024]{1,0:T(8,128)(2,1)S(1)}, u32[]{:S(2)}, u32[]{:S(2)}) collective-permute-start(bf16[128,1024]{1,0:T(8,128)(2,1)} %bitcast.21), channel_id=1, source_target_pairs={{0,1},{1,0},{2,3},{3,2},{4,5},{5,4},{6,7},{7,6},{8,9},{9,8},{10,11... | collective-permute-start | bytes 786440 | tf_op jit(solution)/shard_map/ppermute | solution.py:412
  21.6 0.8 all-to-all-done
  22.4 4.1 %shard_map.91 = bf16[4,5,3,16,128]{4,3,2,1,0:T(8,128)(2,1)} custom-call(s32[1,5120]{1,0:T(1,128)} %bitcast.25, f32[1,5120]{1,0:T(1,128)} %bitcast.26, s32[1,5120]{1,0:T(1,128)} %bitcast.27, s32[1,5120]{1,0:T(1,128)} %bitcast.28, s32[1,32]{1,0:T(1,128)} %slot_ref.1, bf16[4,128,256]{2,1,0:T(8,128)(2,1)S(1)} %bitcast.14), custom_call_target="tpu_custom_call" | custom-call | flops 3221225472 | bytes 1048576 | tf_op jit(solution)/shard_map/pallas_call | solution.py:123
  26.5 5.3 %all-to-all-start.1 = ((bf16[4,5,3,16,128]{4,3,2,1,0:T(8,128)(2,1)}), bf16[4,5,3,16,128]{4,3,2,1,0:T(8,128)(2,1)S(1)}, u32[]{:S(2)}, u32[]{:S(2)}) async-start(bf16[4,5,3,16,128]{4,3,2,1,0:T(8,128)(2,1)} %shard_map.91), calls=%async_computation.1 | async-start | bytes 491520 | tf_op jit(solution)/shard_map/all_to_all | solution.py:435
  31.8 0.0 collective-permute-done.2.hidden3_ref
  31.8 0.0 collective-permute-done.1.hidden2_ref
  31.8 0.0 collective-permute-done.hidden1_ref
  31.8 0.0 copy-done.1
  31.9 0.0 copy-done
  31.9 8.6 %shard_map.92.pooled_hbm_ref = f32[16384,128]{1,0:T(8,128)} custom-call(s32[1]{0:T(128)} %bitcast.8.me_ref, bf16[4,128,256]{2,1,0:T(8,128)(2,1)S(1)} %bitcast.15, bf16[128,1024]{1,0:T(8,128)(2,1)S(1)} %bitcast.22, bf16[128,1024]{1,0:T(8,128)(2,1)S(1)} %collective-permute-done.hidden1_ref, bf16[128,1024]{1,0:T(8,128)(2,1)S(1)} %collective-permute-done.1.hidden2_ref, ...), custom_call_target="tpu_custom_call" | custom-call | flops 5368709120 | bytes 20971520 | tf_op jit(solution)/shard_map/pallas_call | solution.py:337
  40.5 0.0 all-to-all-done.1
  40.5 9.8 %shard_map.93 = bf16[8,256,128]{2,1,0:T(8,128)(2,1)} custom-call(bf16[4,5,48,128]{3,2,1,0:T(8,128)(2,1)S(1)} %bitcast.16, f32[16384,128]{1,0:T(8,128)} %shard_map.92.pooled_hbm_ref), custom_call_target="tpu_custom_call" | custom-call | flops 5368709120 | bytes 10485760 | tf_op jit(solution)/shard_map/pallas_call | solution.py:384
  50.3 10.0 %all-to-all-start.2 = ((bf16[8,256,128]{2,1,0:T(8,128)(2,1)}), bf16[8,256,128]{2,1,0:T(8,128)(2,1)S(1)}, u32[]{:S(2)}, u32[]{:S(2)}) async-start(bf16[8,256,128]{2,1,0:T(8,128)(2,1)} %shard_map.93), calls=%async_computation.2 | async-start | bytes 1048576 | tf_op jit(solution)/shard_map/all_to_all | solution.py:441
  60.3 10.1 %shard_map.94 = bf16[8,256,128]{2,1,0:T(8,128)(2,1)} custom-call(bf16[4,5,48,128]{3,2,1,0:T(8,128)(2,1)S(1)} %bitcast.17, f32[16384,128]{1,0:T(8,128)} %shard_map.92.pooled_hbm_ref), custom_call_target="tpu_custom_call" | custom-call | flops 5368709120 | bytes 10485760 | tf_op jit(solution)/shard_map/pallas_call | solution.py:384
  70.3 7.9 %all-to-all-done.2 = bf16[8,256,128]{2,1,0:T(8,128)(2,1)S(1)} async-done(((bf16[8,256,128]{2,1,0:T(8,128)(2,1)}), bf16[8,256,128]{2,1,0:T(8,128)(2,1)S(1)}, u32[]{:S(2)}, u32[]{:S(2)}) %all-to-all-start.2) | async-done | bytes 524320 | tf_op jit(solution)/shard_map/all_to_all | solution.py:441
  78.2 3.5 %all-to-all-start.3 = ((bf16[8,256,128]{2,1,0:T(8,128)(2,1)}), bf16[8,256,128]{2,1,0:T(8,128)(2,1)S(1)}, u32[]{:S(2)}, u32[]{:S(2)}) async-start(bf16[8,256,128]{2,1,0:T(8,128)(2,1)} %shard_map.94), calls=%async_computation.3 | async-start | bytes 1048576 | tf_op jit(solution)/shard_map/all_to_all | solution.py:442
  81.7 0.1 convert_reduce_fusion.1
  81.8 17.8 %all-to-all-done.3 = bf16[8,256,128]{2,1,0:T(8,128)(2,1)S(1)} async-done(((bf16[8,256,128]{2,1,0:T(8,128)(2,1)}), bf16[8,256,128]{2,1,0:T(8,128)(2,1)S(1)}, u32[]{:S(2)}, u32[]{:S(2)}) %all-to-all-start.3) | async-done | bytes 524320 | tf_op jit(solution)/shard_map/all_to_all | solution.py:442
  99.6 0.1 convert_reduce_fusion
  99.7 0.7 maximum_bitcast_fusion
Async XLA Ops:
  0.0 31.8 %copy-start.1 = (bf16[1,128,1024]{2,1,0:T(8,128)(2,1)S(1)}, bf16[1,128,1024]{2,1,0:T(8,128)(2,1)}, u32[]{:S(2)}) copy-start(bf16[1,128,1024]{2,1,0:T(8,128)(2,1)} %param.10) | copy-start | bytes 786436
  0.0 31.9 %copy-start = (bf16[1,1024,256]{2,1,0:T(8,128)(2,1)S(1)}, bf16[1,1024,256]{2,1,0:T(8,128)(2,1)}, u32[]{:S(2)}) copy-start(bf16[1,1024,256]{2,1,0:T(8,128)(2,1)} %param.11) | copy-start | bytes 1572868
  1.7 20.7 %all-to-all-start = ((bf16[64,8,256]{2,1,0:T(8,128)(2,1)}), bf16[64,8,256]{2,1,0:T(8,128)(2,1)S(1)}, u32[]{:S(2)}, u32[]{:S(2)}) async-start(bf16[64,8,256]{2,1,0:T(8,128)(2,1)} %bitcast.5), calls=%async_computation | async-start | bytes 524288 | tf_op jit(solution)/shard_map/all_to_all | solution.py:416
  12.6 19.2 %collective-permute-start.2 = (bf16[128,1024]{1,0:T(8,128)(2,1)}, bf16[128,1024]{1,0:T(8,128)(2,1)S(1)}, u32[]{:S(2)}, u32[]{:S(2)}) collective-permute-start(bf16[128,1024]{1,0:T(8,128)(2,1)} %bitcast.19), channel_id=1, source_target_pairs={{0,3},{1,2},{2,1},{3,0},{4,7},{5,6},{6,5},{7,4},{8,11},{9,10},{10,... | collective-permute-start | bytes 786440 | tf_op jit(solution)/shard_map/ppermute | solution.py:412
  14.6 17.3 %collective-permute-start.1 = (bf16[128,1024]{1,0:T(8,128)(2,1)}, bf16[128,1024]{1,0:T(8,128)(2,1)S(1)}, u32[]{:S(2)}, u32[]{:S(2)}) collective-permute-start(bf16[128,1024]{1,0:T(8,128)(2,1)} %bitcast.20), channel_id=1, source_target_pairs={{0,2},{1,3},{2,0},{3,1},{4,6},{5,7},{6,4},{7,5},{8,10},{9,11},{10,... | collective-permute-start | bytes 786440 | tf_op jit(solution)/shard_map/ppermute | solution.py:412
  18.7 13.2 %collective-permute-start = (bf16[128,1024]{1,0:T(8,128)(2,1)}, bf16[128,1024]{1,0:T(8,128)(2,1)S(1)}, u32[]{:S(2)}, u32[]{:S(2)}) collective-permute-start(bf16[128,1024]{1,0:T(8,128)(2,1)} %bitcast.21), channel_id=1, source_target_pairs={{0,1},{1,0},{2,3},{3,2},{4,5},{5,4},{6,7},{7,6},{8,9},{9,8},{10,11... | collective-permute-start | bytes 786440 | tf_op jit(solution)/shard_map/ppermute | solution.py:412
  26.5 13.9 %all-to-all-start.1 = ((bf16[4,5,3,16,128]{4,3,2,1,0:T(8,128)(2,1)}), bf16[4,5,3,16,128]{4,3,2,1,0:T(8,128)(2,1)S(1)}, u32[]{:S(2)}, u32[]{:S(2)}) async-start(bf16[4,5,3,16,128]{4,3,2,1,0:T(8,128)(2,1)} %shard_map.91), calls=%async_computation.1 | async-start | bytes 491520 | tf_op jit(solution)/shard_map/all_to_all | solution.py:435
  50.3 27.9 %all-to-all-start.2 = ((bf16[8,256,128]{2,1,0:T(8,128)(2,1)}), bf16[8,256,128]{2,1,0:T(8,128)(2,1)S(1)}, u32[]{:S(2)}, u32[]{:S(2)}) async-start(bf16[8,256,128]{2,1,0:T(8,128)(2,1)} %shard_map.93), calls=%async_computation.2 | async-start | bytes 1048576 | tf_op jit(solution)/shard_map/all_to_all | solution.py:441
  78.2 21.4 %all-to-all-start.3 = ((bf16[8,256,128]{2,1,0:T(8,128)(2,1)}), bf16[8,256,128]{2,1,0:T(8,128)(2,1)S(1)}, u32[]{:S(2)}, u32[]{:S(2)}) async-start(bf16[8,256,128]{2,1,0:T(8,128)(2,1)} %shard_map.94), calls=%async_computation.3 | async-start | bytes 1048576 | tf_op jit(solution)/shard_map/all_to_all | solution.py:442

commit v7 on v6

--- a/solution.py
+++ b/solution.py
@@ -270,14 +270,31 @@
 UP_PART = 512
 
 
+def backward_kernel(grad_ref, down_ref, backward_ref):
+    backward_ref[...] = lax.dot_general(
+        grad_ref[...], down_ref[...], NT, preferred_element_type=F32
+    ).astype(BF)
+
+
+def hidden_gradients(grads, down):
+    vmem = pl.BlockSpec(memory_space=pltpu.VMEM)
+    return pl.pallas_call(
+        backward_kernel,
+        out_shape=jax.ShapeDtypeStruct((NX * SAMP, HID), BF),
+        in_specs=[vmem, vmem],
+        out_specs=vmem,
+        compiler_params=pltpu.CompilerParams(vmem_limit_bytes=16 << 20),
+        cost_estimate=pl.CostEstimate(flops=1 << 28, bytes_accessed=2 << 20, transcendentals=0),
+    )(grads.reshape(NX * SAMP, TOUT), down)
+
+
 def pooled_kernel(
     me_ref,
-    grad_ref,
+    backward_ref,
     hidden0_ref,
     hidden1_ref,
     hidden2_ref,
     hidden3_ref,
-    down_ref,
     up_hbm_ref,
     pooled_hbm_ref,
     pooled_ref,
@@ -300,10 +317,9 @@
     for k in range(UP_STEPS):
         up_copy(k).start()
     for r, hidden_ref in enumerate((hidden0_ref, hidden1_ref, hidden2_ref, hidden3_ref)):
-        x = me_ref[0] ^ r
-        backward = lax.dot_general(grad_ref[x], down_ref[...], NT, preferred_element_type=F32)
+        there = pl.ds(pl.multiple_of((me_ref[0] ^ r) * SAMP, SAMP), SAMP)
         keep = hidden_ref[...].astype(F32) > 0
-        there = pl.ds(pl.multiple_of(x * SAMP, SAMP), SAMP)
+        backward = backward_ref[there, :].astype(F32)
         hid_ref[there, :] = jnp.where(keep, backward, 0.0).astype(BF)
 
     def up_step(k, unused):
@@ -331,13 +347,13 @@
             pooled_copy(k, x).wait()
 
 
-def pooled_gradients(me, grads, hiddens, down, up):
+def pooled_gradients(me, backward, hiddens, up):
     hbm = pl.BlockSpec(memory_space=pltpu.HBM)
     vmem = pl.BlockSpec(memory_space=pltpu.VMEM)
     return pl.pallas_call(
         pooled_kernel,
         out_shape=pltpu.HBM((NX * FEAT * SAMP, E), F32),
-        in_specs=[pl.BlockSpec(memory_space=pltpu.SMEM), *[vmem] * (NX + 2), hbm],
+        in_specs=[pl.BlockSpec(memory_space=pltpu.SMEM), *[vmem] * (NX + 1), hbm],
         out_specs=hbm,
         scratch_shapes=[
             pltpu.VMEM((NX * FEAT * SAMP, E), F32),
@@ -348,7 +364,7 @@
         ],
         compiler_params=pltpu.CompilerParams(vmem_limit_bytes=32 << 20),
         cost_estimate=pl.CostEstimate(flops=5 << 30, bytes_accessed=20 << 20, transcendentals=0),
-    )(me, grads, *hiddens, down, in_hbm(up))
+    )(me, backward, *hiddens, in_hbm(up))
 
 
 def table_kernel(
@@ -434,7 +450,8 @@
     )
     parts = swap_x(buckets).reshape(NX, PIECES, CHUNKS * BUCKETS, LANES)
     me = lax.axis_index("x").astype(I32).reshape(1)
-    pooled = pooled_gradients(me, grads, hiddens, down_proj[0], up_proj[0])
+    backward = hidden_gradients(grads, down_proj[0])
+    pooled = pooled_gradients(me, backward, hiddens, up_proj[0])
     swap = functools.partial(
         lax.all_to_all, axis_name="z", split_axis=0, concat_axis=0, tiled=True
     )

time: 101 us -> 102 us (level)
  the two profiles are of different devices: /device:TPU:23 before, /device:TPU:1 now
where the time goes in v7:
time: 102 us; the launch traced here: 101 us
  starting transfers between devices  38.2 us (37%)
  waiting for transfers between devices  30.4 us (30%)
  Pallas kernels  29.7 us (29%)
  local copies, waits for them, and re-layouts  1.66 us (2%)
    all_to_all x1, waiting for transfers between devices, local(): second = swap(half_tables(1, parts, pooled))  17.8 us
    pallas_call x2, Pallas kernels, half_tables(): pl.pallas_call(functools.partial(table_kernel, half), out_shape=jax.Shape...  16.8 us
    all_to_all x1, starting transfers between devices, local(): lax.all_to_all(jnp.broadcast_to(by_tower, (NX, *by_tower.shape)).reshape(...  11.6 us
    all_to_all x1, starting transfers between devices, local(): first = swap(half_tables(0, parts, pooled))  10.1 us
    all_to_all x1, waiting for transfers between devices, local(): first = swap(half_tables(0, parts, pooled))  9.76 us
    ppermute x3, starting transfers between devices, local(): lax.ppermute(own, 'x', [(i, i ^ r) for i in range(NX)])  9.13 us
    pallas_call x1, Pallas kernels, pooled_gradients(): pl.pallas_call(pooled_kernel, out_shape=pltpu.HBM((NX * FEAT * SAMP, E),...  8.29 us
    pallas_call x1, Pallas kernels, bucket_elements(): pl.pallas_call(bucket_kernel, out_shape=jax.ShapeDtypeStruct((NX, PIECES,...  4.14 us
  transfers between devices with their start and end apart: 7, of which 3 were waited for; matrix products, arithmetic and copies ran while one was open for 0% of the time, Pallas kernels for 21%

profile of v7, /device:TPU:1, one launch (start us, length us, event | category | flops | bytes accessed | tf_op | source)
XLA Modules:
  0.0 101.0 jit_solution(16914896583059839835)
XLA Ops:
  0.0 0.0 copy-start.1
  0.0 0.0 copy-start
  0.0 0.9 copy.10
  0.9 0.7 broadcast_in_dim.3
  1.7 11.6 %all-to-all-start = ((bf16[64,8,256]{2,1,0:T(8,128)(2,1)}), bf16[64,8,256]{2,1,0:T(8,128)(2,1)S(1)}, u32[]{:S(2)}, u32[]{:S(2)}) async-start(bf16[64,8,256]{2,1,0:T(8,128)(2,1)} %bitcast.5), calls=%async_computation | async-start | bytes 524288 | tf_op jit(solution)/shard_map/all_to_all | solution.py:432
  13.3 4.7 %collective-permute-start.2 = (bf16[128,1024]{1,0:T(8,128)(2,1)}, bf16[128,1024]{1,0:T(8,128)(2,1)S(1)}, u32[]{:S(2)}, u32[]{:S(2)}) collective-permute-start(bf16[128,1024]{1,0:T(8,128)(2,1)} %bitcast.20), channel_id=1, source_target_pairs={{0,3},{1,2},{2,1},{3,0},{4,7},{5,6},{6,5},{7,4},{8,11},{9,10},{10,... | collective-permute-start | bytes 786440 | tf_op jit(solution)/shard_map/ppermute | solution.py:428
  18.0 2.3 %collective-permute-start.1 = (bf16[128,1024]{1,0:T(8,128)(2,1)}, bf16[128,1024]{1,0:T(8,128)(2,1)S(1)}, u32[]{:S(2)}, u32[]{:S(2)}) collective-permute-start(bf16[128,1024]{1,0:T(8,128)(2,1)} %bitcast.21), channel_id=1, source_target_pairs={{0,2},{1,3},{2,0},{3,1},{4,6},{5,7},{6,4},{7,5},{8,10},{9,11},{10,... | collective-permute-start | bytes 786440 | tf_op jit(solution)/shard_map/ppermute | solution.py:428
  20.3 2.1 %collective-permute-start = (bf16[128,1024]{1,0:T(8,128)(2,1)}, bf16[128,1024]{1,0:T(8,128)(2,1)S(1)}, u32[]{:S(2)}, u32[]{:S(2)}) collective-permute-start(bf16[128,1024]{1,0:T(8,128)(2,1)} %bitcast.22), channel_id=1, source_target_pairs={{0,1},{1,0},{2,3},{3,2},{4,5},{5,4},{6,7},{7,6},{8,9},{9,8},{10,11... | collective-permute-start | bytes 786440 | tf_op jit(solution)/shard_map/ppermute | solution.py:428
  22.4 2.8 %all-to-all-done = bf16[64,8,256]{2,1,0:T(8,128)(2,1)S(1)} async-done(((bf16[64,8,256]{2,1,0:T(8,128)(2,1)}), bf16[64,8,256]{2,1,0:T(8,128)(2,1)S(1)}, u32[]{:S(2)}, u32[]{:S(2)}) %all-to-all-start) | async-done | bytes 262176 | tf_op jit(solution)/shard_map/all_to_all | solution.py:432
  25.3 4.1 %shard_map.91 = bf16[4,5,3,16,128]{4,3,2,1,0:T(8,128)(2,1)} custom-call(s32[1,5120]{1,0:T(1,128)} %bitcast.26, f32[1,5120]{1,0:T(1,128)} %bitcast.27, s32[1,5120]{1,0:T(1,128)} %bitcast.28, s32[1,5120]{1,0:T(1,128)} %bitcast.29, s32[1,32]{1,0:T(1,128)} %slot_ref.1, bf16[4,128,256]{2,1,0:T(8,128)(2,1)S(1)} %bitcast.15), custom_call_target="tpu_custom_call" | custom-call | flops 3221225472 | bytes 1048576 | tf_op jit(solution)/shard_map/pallas_call | solution.py:123
  29.4 3.8 %all-to-all-start.1 = ((bf16[4,5,3,16,128]{4,3,2,1,0:T(8,128)(2,1)}), bf16[4,5,3,16,128]{4,3,2,1,0:T(8,128)(2,1)S(1)}, u32[]{:S(2)}, u32[]{:S(2)}) async-start(bf16[4,5,3,16,128]{4,3,2,1,0:T(8,128)(2,1)} %shard_map.91), calls=%async_computation.1 | async-start | bytes 491520 | tf_op jit(solution)/shard_map/all_to_all | solution.py:451
  33.2 0.0 copy-done
  33.2 0.5 shard_map.92.backward_ref
  33.7 0.0 collective-permute-done.2.hidden3_ref
  33.7 0.0 collective-permute-done.1.hidden2_ref
  33.7 0.0 collective-permute-done.hidden1_ref
  33.7 0.0 copy-done.1
  33.8 8.3 %shard_map.93.pooled_hbm_ref = f32[16384,128]{1,0:T(8,128)} custom-call(s32[1]{0:T(128)} %bitcast.8.me_ref, bf16[512,1024]{1,0:T(8,128)(2,1)S(1)} %shard_map.92.backward_ref, bf16[128,1024]{1,0:T(8,128)(2,1)S(1)} %bitcast.23, bf16[128,1024]{1,0:T(8,128)(2,1)S(1)} %collective-permute-done.hidden1_ref, ...), custom_call_target="tpu_custom_call" | custom-call | flops 5368709120 | bytes 20971520 | tf_op jit(solution)/shard_map/pallas_call | solution.py:353
  42.0 0.0 all-to-all-done.1
  42.1 8.6 %shard_map.94 = bf16[8,256,128]{2,1,0:T(8,128)(2,1)} custom-call(bf16[4,5,48,128]{3,2,1,0:T(8,128)(2,1)S(1)} %bitcast.18, f32[16384,128]{1,0:T(8,128)} %shard_map.93.pooled_hbm_ref), custom_call_target="tpu_custom_call" | custom-call | flops 5368709120 | bytes 10485760 | tf_op jit(solution)/shard_map/pallas_call | solution.py:400
  50.7 10.1 %all-to-all-start.2 = ((bf16[8,256,128]{2,1,0:T(8,128)(2,1)}), bf16[8,256,128]{2,1,0:T(8,128)(2,1)S(1)}, u32[]{:S(2)}, u32[]{:S(2)}) async-start(bf16[8,256,128]{2,1,0:T(8,128)(2,1)} %shard_map.94), calls=%async_computation.2 | async-start | bytes 1048576 | tf_op jit(solution)/shard_map/all_to_all | solution.py:458
  60.8 8.2 %shard_map.95 = bf16[8,256,128]{2,1,0:T(8,128)(2,1)} custom-call(bf16[4,5,48,128]{3,2,1,0:T(8,128)(2,1)S(1)} %bitcast.19, f32[16384,128]{1,0:T(8,128)} %shard_map.93.pooled_hbm_ref), custom_call_target="tpu_custom_call" | custom-call | flops 5368709120 | bytes 10485760 | tf_op jit(solution)/shard_map/pallas_call | solution.py:400
  69.0 9.8 %all-to-all-done.2 = bf16[8,256,128]{2,1,0:T(8,128)(2,1)S(1)} async-done(((bf16[8,256,128]{2,1,0:T(8,128)(2,1)}), bf16[8,256,128]{2,1,0:T(8,128)(2,1)S(1)}, u32[]{:S(2)}, u32[]{:S(2)}) %all-to-all-start.2) | async-done | bytes 524320 | tf_op jit(solution)/shard_map/all_to_all | solution.py:458
  78.8 3.5 %all-to-all-start.3 = ((bf16[8,256,128]{2,1,0:T(8,128)(2,1)}), bf16[8,256,128]{2,1,0:T(8,128)(2,1)S(1)}, u32[]{:S(2)}, u32[]{:S(2)}) async-start(bf16[8,256,128]{2,1,0:T(8,128)(2,1)} %shard_map.95), calls=%async_computation.3 | async-start | bytes 1048576 | tf_op jit(solution)/shard_map/all_to_all | solution.py:459
  82.3 0.1 convert_reduce_fusion.1
  82.4 17.8 %all-to-all-done.3 = bf16[8,256,128]{2,1,0:T(8,128)(2,1)S(1)} async-done(((bf16[8,256,128]{2,1,0:T(8,128)(2,1)}), bf16[8,256,128]{2,1,0:T(8,128)(2,1)S(1)}, u32[]{:S(2)}, u32[]{:S(2)}) %all-to-all-start.3) | async-done | bytes 524320 | tf_op jit(solution)/shard_map/all_to_all | solution.py:459
  100.2 0.1 convert_reduce_fusion
  100.2 0.7 maximum_bitcast_fusion
Async XLA Ops:
  0.0 33.7 %copy-start.1 = (bf16[1,128,1024]{2,1,0:T(8,128)(2,1)S(1)}, bf16[1,128,1024]{2,1,0:T(8,128)(2,1)}, u32[]{:S(2)}) copy-start(bf16[1,128,1024]{2,1,0:T(8,128)(2,1)} %param.10) | copy-start | bytes 786436
  0.0 33.2 %copy-start = (bf16[1,1024,256]{2,1,0:T(8,128)(2,1)S(1)}, bf16[1,1024,256]{2,1,0:T(8,128)(2,1)}, u32[]{:S(2)}) copy-start(bf16[1,1024,256]{2,1,0:T(8,128)(2,1)} %param.11) | copy-start | bytes 1572868
  1.7 23.6 %all-to-all-start = ((bf16[64,8,256]{2,1,0:T(8,128)(2,1)}), bf16[64,8,256]{2,1,0:T(8,128)(2,1)S(1)}, u32[]{:S(2)}, u32[]{:S(2)}) async-start(bf16[64,8,256]{2,1,0:T(8,128)(2,1)} %bitcast.5), calls=%async_computation | async-start | bytes 524288 | tf_op jit(solution)/shard_map/all_to_all | solution.py:432
  13.3 20.4 %collective-permute-start.2 = (bf16[128,1024]{1,0:T(8,128)(2,1)}, bf16[128,1024]{1,0:T(8,128)(2,1)S(1)}, u32[]{:S(2)}, u32[]{:S(2)}) collective-permute-start(bf16[128,1024]{1,0:T(8,128)(2,1)} %bitcast.20), channel_id=1, source_target_pairs={{0,3},{1,2},{2,1},{3,0},{4,7},{5,6},{6,5},{7,4},{8,11},{9,10},{10,... | collective-permute-start | bytes 786440 | tf_op jit(solution)/shard_map/ppermute | solution.py:428
  18.0 15.7 %collective-permute-start.1 = (bf16[128,1024]{1,0:T(8,128)(2,1)}, bf16[128,1024]{1,0:T(8,128)(2,1)S(1)}, u32[]{:S(2)}, u32[]{:S(2)}) collective-permute-start(bf16[128,1024]{1,0:T(8,128)(2,1)} %bitcast.21), channel_id=1, source_target_pairs={{0,2},{1,3},{2,0},{3,1},{4,6},{5,7},{6,4},{7,5},{8,10},{9,11},{10,... | collective-permute-start | bytes 786440 | tf_op jit(solution)/shard_map/ppermute | solution.py:428
  20.3 13.4 %collective-permute-start = (bf16[128,1024]{1,0:T(8,128)(2,1)}, bf16[128,1024]{1,0:T(8,128)(2,1)S(1)}, u32[]{:S(2)}, u32[]{:S(2)}) collective-permute-start(bf16[128,1024]{1,0:T(8,128)(2,1)} %bitcast.22), channel_id=1, source_target_pairs={{0,1},{1,0},{2,3},{3,2},{4,5},{5,4},{6,7},{7,6},{8,9},{9,8},{10,11... | collective-permute-start | bytes 786440 | tf_op jit(solution)/shard_map/ppermute | solution.py:428
  29.4 12.6 %all-to-all-start.1 = ((bf16[4,5,3,16,128]{4,3,2,1,0:T(8,128)(2,1)}), bf16[4,5,3,16,128]{4,3,2,1,0:T(8,128)(2,1)S(1)}, u32[]{:S(2)}, u32[]{:S(2)}) async-start(bf16[4,5,3,16,128]{4,3,2,1,0:T(8,128)(2,1)} %shard_map.91), calls=%async_computation.1 | async-start | bytes 491520 | tf_op jit(solution)/shard_map/all_to_all | solution.py:451
  50.7 28.1 %all-to-all-start.2 = ((bf16[8,256,128]{2,1,0:T(8,128)(2,1)}), bf16[8,256,128]{2,1,0:T(8,128)(2,1)S(1)}, u32[]{:S(2)}, u32[]{:S(2)}) async-start(bf16[8,256,128]{2,1,0:T(8,128)(2,1)} %shard_map.94), calls=%async_computation.2 | async-start | bytes 1048576 | tf_op jit(solution)/shard_map/all_to_all | solution.py:458
  78.8 21.4 %all-to-all-start.3 = ((bf16[8,256,128]{2,1,0:T(8,128)(2,1)}), bf16[8,256,128]{2,1,0:T(8,128)(2,1)S(1)}, u32[]{:S(2)}, u32[]{:S(2)}) async-start(bf16[8,256,128]{2,1,0:T(8,128)(2,1)} %shard_map.95), calls=%async_computation.3 | async-start | bytes 1048576 | tf_op jit(solution)/shard_map/all_to_all | solution.py:459

commit v8 on v7

--- a/solution.py
+++ b/solution.py
@@ -457,9 +457,7 @@
     )
     first = swap(half_tables(0, parts, pooled))
     second = swap(half_tables(1, parts, pooled))
-    table_grad = jnp.concatenate(
-        [jnp.sum(first.astype(F32), axis=0), jnp.sum(second.astype(F32), axis=0)], axis=0
-    )
+    table_grad = jnp.sum(jnp.concatenate([first, second], axis=1).astype(F32), axis=0)
     return table_grad.reshape(1, ROW_DEV, E)
 
 

time: 102 us -> 101 us (level)
  blocking collectives: 0 us -> 20.1 us
  waiting for transfers between devices: 30.4 us -> 14 us
  starting transfers between devices: 38.2 us -> 34.7 us
  Pallas kernels: 29.7 us -> 28.2 us
    all_to_all x0 -> x1, blocking collectives: none -> 20.1 us  [local(): second = swap(half_tables(1, parts, pooled))]
    all_to_all x1 -> x0, waiting for transfers between devices: 17.8 us -> none  [local(): second = swap(half_tables(1, parts, pooled))]
    all_to_all x1 -> x0, starting transfers between devices: 3.49 us -> none  [local(): second = swap(half_tables(1, parts, pooled))]
    pallas_call x2, Pallas kernels: 16.8 us -> 15.2 us  [half_tables(): pl.pallas_call(functools.partial(table_kernel, half), out_shape=jax.Shape...]
    all_to_all x1, waiting for transfers between devices: 9.76 us -> 11.1 us  [local(): first = swap(half_tables(0, parts, pooled))]
  transfers between devices with their start and end apart: 7 -> 6, of which waited for: 3 -> 2; matrix products, arithmetic and copies ran while one was open for 0% -> 0% of each run, Pallas kernels for 21% -> 20%
where the time goes in v8:
time: 101 us; the launch traced here: 99.5 us
  starting transfers between devices  34.7 us (34%)
  Pallas kernels  28.2 us (28%)
  blocking collectives  20.1 us (20%)
  waiting for transfers between devices  14 us (14%)
  local copies, waits for them, and re-layouts  1.59 us (2%)
    all_to_all x1, blocking collectives, local(): second = swap(half_tables(1, parts, pooled))  20.1 us
    pallas_call x2, Pallas kernels, half_tables(): pl.pallas_call(functools.partial(table_kernel, half), out_shape=jax.Shape...  15.2 us
    all_to_all x1, starting transfers between devices, local(): lax.all_to_all(jnp.broadcast_to(by_tower, (NX, *by_tower.shape)).reshape(...  11.6 us
    all_to_all x1, waiting for transfers between devices, local(): first = swap(half_tables(0, parts, pooled))  11.1 us
    all_to_all x1, starting transfers between devices, local(): first = swap(half_tables(0, parts, pooled))  10 us
    ppermute x3, starting transfers between devices, local(): lax.ppermute(own, 'x', [(i, i ^ r) for i in range(NX)])  9.13 us
    pallas_call x1, Pallas kernels, pooled_gradients(): pl.pallas_call(pooled_kernel, out_shape=pltpu.HBM((NX * FEAT * SAMP, E),...  8.27 us
    pallas_call x1, Pallas kernels, bucket_elements(): pl.pallas_call(bucket_kernel, out_shape=jax.ShapeDtypeStruct((NX, PIECES,...  4.19 us
  transfers between devices with their start and end apart: 6, of which 2 were waited for; matrix products, arithmetic and copies ran while one was open for 0% of the time, Pallas kernels for 20%

profile of v8, /device:TPU:1, one launch (start us, length us, event | category | flops | bytes accessed | tf_op | source)
XLA Modules:
  0.0 99.5 jit_solution(10191743501876783113)
XLA Ops:
  0.0 0.9 copy.10
  0.9 0.7 broadcast_in_dim.3
  1.6 11.6 %all-to-all-start = ((bf16[64,8,256]{2,1,0:T(8,128)(2,1)}), bf16[64,8,256]{2,1,0:T(8,128)(2,1)S(1)}, u32[]{:S(2)}, u32[]{:S(2)}) async-start(bf16[64,8,256]{2,1,0:T(8,128)(2,1)} %bitcast.5), calls=%async_computation | async-start | bytes 524288 | tf_op jit(solution)/shard_map/all_to_all | solution.py:432
  13.2 4.7 %collective-permute-start.2 = (bf16[128,1024]{1,0:T(8,128)(2,1)}, bf16[128,1024]{1,0:T(8,128)(2,1)S(1)}, u32[]{:S(2)}, u32[]{:S(2)}) collective-permute-start(bf16[128,1024]{1,0:T(8,128)(2,1)} %bitcast.19), channel_id=1, source_target_pairs={{0,3},{1,2},{2,1},{3,0},{4,7},{5,6},{6,5},{7,4},{8,11},{9,10},{10,... | collective-permute-start | bytes 786440 | tf_op jit(solution)/shard_map/ppermute | solution.py:428
  17.9 2.3 %collective-permute-start.1 = (bf16[128,1024]{1,0:T(8,128)(2,1)}, bf16[128,1024]{1,0:T(8,128)(2,1)S(1)}, u32[]{:S(2)}, u32[]{:S(2)}) collective-permute-start(bf16[128,1024]{1,0:T(8,128)(2,1)} %bitcast.20), channel_id=1, source_target_pairs={{0,2},{1,3},{2,0},{3,1},{4,6},{5,7},{6,4},{7,5},{8,10},{9,11},{10,... | collective-permute-start | bytes 786440 | tf_op jit(solution)/shard_map/ppermute | solution.py:428
  20.2 2.1 %collective-permute-start = (bf16[128,1024]{1,0:T(8,128)(2,1)}, bf16[128,1024]{1,0:T(8,128)(2,1)S(1)}, u32[]{:S(2)}, u32[]{:S(2)}) collective-permute-start(bf16[128,1024]{1,0:T(8,128)(2,1)} %bitcast.21), channel_id=1, source_target_pairs={{0,1},{1,0},{2,3},{3,2},{4,5},{5,4},{6,7},{7,6},{8,9},{9,8},{10,11... | collective-permute-start | bytes 786440 | tf_op jit(solution)/shard_map/ppermute | solution.py:428
  22.4 2.8 %all-to-all-done = bf16[64,8,256]{2,1,0:T(8,128)(2,1)S(1)} async-done(((bf16[64,8,256]{2,1,0:T(8,128)(2,1)}), bf16[64,8,256]{2,1,0:T(8,128)(2,1)S(1)}, u32[]{:S(2)}, u32[]{:S(2)}) %all-to-all-start) | async-done | bytes 262176 | tf_op jit(solution)/shard_map/all_to_all | solution.py:432
  25.2 0.0 copy-start
  25.2 4.2 %shard_map.91 = bf16[4,5,3,16,128]{4,3,2,1,0:T(8,128)(2,1)} custom-call(s32[1,5120]{1,0:T(1,128)} %bitcast.25, f32[1,5120]{1,0:T(1,128)} %bitcast.26, s32[1,5120]{1,0:T(1,128)} %bitcast.27, s32[1,5120]{1,0:T(1,128)} %bitcast.28, s32[1,32]{1,0:T(1,128)} %slot_ref.1, bf16[4,128,256]{2,1,0:T(8,128)(2,1)S(1)} %bitcast.14), custom_call_target="tpu_custom_call" | custom-call | flops 3221225472 | bytes 1048576 | tf_op jit(solution)/shard_map/pallas_call | solution.py:123
  29.4 0.0 copy-start.1
  29.4 3.9 %all-to-all-start.1 = ((bf16[4,5,3,16,128]{4,3,2,1,0:T(8,128)(2,1)}), bf16[4,5,3,16,128]{4,3,2,1,0:T(8,128)(2,1)S(1)}, u32[]{:S(2)}, u32[]{:S(2)}) async-start(bf16[4,5,3,16,128]{4,3,2,1,0:T(8,128)(2,1)} %shard_map.91), calls=%async_computation.1 | async-start | bytes 491520 | tf_op jit(solution)/shard_map/all_to_all | solution.py:451
  33.3 0.0 copy-done
  33.4 0.5 shard_map.92.backward_ref
  33.8 0.0 collective-permute-done.2.hidden3_ref
  33.8 0.0 collective-permute-done.1.hidden2_ref
  33.8 0.0 collective-permute-done.hidden1_ref
  33.9 0.0 copy-done.1
  33.9 8.3 %shard_map.93.pooled_hbm_ref = f32[16384,128]{1,0:T(8,128)} custom-call(s32[1]{0:T(128)} %bitcast.8.me_ref, bf16[512,1024]{1,0:T(8,128)(2,1)S(1)} %shard_map.92.backward_ref, bf16[128,1024]{1,0:T(8,128)(2,1)S(1)} %bitcast.22, bf16[128,1024]{1,0:T(8,128)(2,1)S(1)} %collective-permute-done.hidden1_ref, ...), custom_call_target="tpu_custom_call" | custom-call | flops 5368709120 | bytes 20971520 | tf_op jit(solution)/shard_map/pallas_call | solution.py:353
  42.1 0.0 all-to-all-done.1
  42.2 8.4 %shard_map.94 = bf16[8,256,128]{2,1,0:T(8,128)(2,1)} custom-call(bf16[4,5,48,128]{3,2,1,0:T(8,128)(2,1)S(1)} %bitcast.17, f32[16384,128]{1,0:T(8,128)} %shard_map.93.pooled_hbm_ref), custom_call_target="tpu_custom_call" | custom-call | flops 5368709120 | bytes 10485760 | tf_op jit(solution)/shard_map/pallas_call | solution.py:400
  50.5 10.0 %all-to-all-start.2 = ((bf16[8,256,128]{2,1,0:T(8,128)(2,1)}), bf16[8,256,128]{2,1,0:T(8,128)(2,1)S(1)}, u32[]{:S(2)}, u32[]{:S(2)}) async-start(bf16[8,256,128]{2,1,0:T(8,128)(2,1)} %shard_map.94), calls=%async_computation.2 | async-start | bytes 1048576 | tf_op jit(solution)/shard_map/all_to_all | solution.py:458
  60.6 6.9 %shard_map.95 = bf16[8,256,128]{2,1,0:T(8,128)(2,1)S(1)} custom-call(bf16[4,5,48,128]{3,2,1,0:T(8,128)(2,1)S(1)} %bitcast.18, f32[16384,128]{1,0:T(8,128)} %shard_map.93.pooled_hbm_ref), custom_call_target="tpu_custom_call" | custom-call | flops 5368709120 | bytes 10485760 | tf_op jit(solution)/shard_map/pallas_call | solution.py:400
  67.4 11.1 %all-to-all-done.2 = bf16[8,256,128]{2,1,0:T(8,128)(2,1)S(1)} async-done(((bf16[8,256,128]{2,1,0:T(8,128)(2,1)}), bf16[8,256,128]{2,1,0:T(8,128)(2,1)S(1)}, u32[]{:S(2)}, u32[]{:S(2)}) %all-to-all-start.2) | async-done | bytes 524320 | tf_op jit(solution)/shard_map/all_to_all | solution.py:458
  78.5 20.1 %all_to_all.20 = bf16[8,256,128]{2,1,0:T(8,128)(2,1)S(1)} all-to-all(bf16[8,256,128]{2,1,0:T(8,128)(2,1)S(1)} %shard_map.95), channel_id=1, replica_groups=mesh['tower'=16,'z'=8,'x'=4] {'z'}, dimensions={0} | all-to-all | bytes 1048576 | tf_op jit(solution)/shard_map/all_to_all | solution.py:459
  98.6 0.8 convert_reduce_fusion
Async XLA Ops:
  1.6 23.6 %all-to-all-start = ((bf16[64,8,256]{2,1,0:T(8,128)(2,1)}), bf16[64,8,256]{2,1,0:T(8,128)(2,1)S(1)}, u32[]{:S(2)}, u32[]{:S(2)}) async-start(bf16[64,8,256]{2,1,0:T(8,128)(2,1)} %bitcast.5), calls=%async_computation | async-start | bytes 524288 | tf_op jit(solution)/shard_map/all_to_all | solution.py:432
  13.2 20.6 %collective-permute-start.2 = (bf16[128,1024]{1,0:T(8,128)(2,1)}, bf16[128,1024]{1,0:T(8,128)(2,1)S(1)}, u32[]{:S(2)}, u32[]{:S(2)}) collective-permute-start(bf16[128,1024]{1,0:T(8,128)(2,1)} %bitcast.19), channel_id=1, source_target_pairs={{0,3},{1,2},{2,1},{3,0},{4,7},{5,6},{6,5},{7,4},{8,11},{9,10},{10,... | collective-permute-start | bytes 786440 | tf_op jit(solution)/shard_map/ppermute | solution.py:428
  17.9 15.9 %collective-permute-start.1 = (bf16[128,1024]{1,0:T(8,128)(2,1)}, bf16[128,1024]{1,0:T(8,128)(2,1)S(1)}, u32[]{:S(2)}, u32[]{:S(2)}) collective-permute-start(bf16[128,1024]{1,0:T(8,128)(2,1)} %bitcast.20), channel_id=1, source_target_pairs={{0,2},{1,3},{2,0},{3,1},{4,6},{5,7},{6,4},{7,5},{8,10},{9,11},{10,... | collective-permute-start | bytes 786440 | tf_op jit(solution)/shard_map/ppermute | solution.py:428
  20.2 13.6 %collective-permute-start = (bf16[128,1024]{1,0:T(8,128)(2,1)}, bf16[128,1024]{1,0:T(8,128)(2,1)S(1)}, u32[]{:S(2)}, u32[]{:S(2)}) collective-permute-start(bf16[128,1024]{1,0:T(8,128)(2,1)} %bitcast.21), channel_id=1, source_target_pairs={{0,1},{1,0},{2,3},{3,2},{4,5},{5,4},{6,7},{7,6},{8,9},{9,8},{10,11... | collective-permute-start | bytes 786440 | tf_op jit(solution)/shard_map/ppermute | solution.py:428
  25.2 8.1 %copy-start = (bf16[1,1024,256]{2,1,0:T(8,128)(2,1)S(1)}, bf16[1,1024,256]{2,1,0:T(8,128)(2,1)}, u32[]{:S(2)}) copy-start(bf16[1,1024,256]{2,1,0:T(8,128)(2,1)} %param.11) | copy-start | bytes 1572868
  29.4 4.4 %copy-start.1 = (bf16[1,128,1024]{2,1,0:T(8,128)(2,1)S(1)}, bf16[1,128,1024]{2,1,0:T(8,128)(2,1)}, u32[]{:S(2)}) copy-start(bf16[1,128,1024]{2,1,0:T(8,128)(2,1)} %param.10) | copy-start | bytes 786436
  29.4 12.7 %all-to-all-start.1 = ((bf16[4,5,3,16,128]{4,3,2,1,0:T(8,128)(2,1)}), bf16[4,5,3,16,128]{4,3,2,1,0:T(8,128)(2,1)S(1)}, u32[]{:S(2)}, u32[]{:S(2)}) async-start(bf16[4,5,3,16,128]{4,3,2,1,0:T(8,128)(2,1)} %shard_map.91), calls=%async_computation.1 | async-start | bytes 491520 | tf_op jit(solution)/shard_map/all_to_all | solution.py:451
  50.5 28.0 %all-to-all-start.2 = ((bf16[8,256,128]{2,1,0:T(8,128)(2,1)}), bf16[8,256,128]{2,1,0:T(8,128)(2,1)S(1)}, u32[]{:S(2)}, u32[]{:S(2)}) async-start(bf16[8,256,128]{2,1,0:T(8,128)(2,1)} %shard_map.94), calls=%async_computation.2 | async-start | bytes 1048576 | tf_op jit(solution)/shard_map/all_to_all | solution.py:458
